TPU v7x, 128 devices: a whole 4x4x4 slice. The times are simulated.
128 devices in a mesh: tile: 64 (over x, z, y), win: 2 (over core).
Axes of the slice: x: 4, y: 4, z: 4, core: 2. Of those that a mesh axis runs over, the one named last changes fastest.
Arguments:
- grid: bfloat16 [2, 2048, 32, 256], P('win', 'tile'), may hold values from -6 to 6
- tokens: bfloat16 [2, 524288, 256], P('win', 'tile'), may hold values from -50 to 50
- targets: int32 [2, 4096, 1], P('win', 'tile'), may hold values from 0 to 63; in each aligned block of 64 rows (0 to 63, 64 to 127, ..., all dimensions but the last counted through in order) at most 2 rows name the same one
- sub_masks: int32 [2, 4096, 8], P('win', 'tile'), may hold values from 0 to 1, as said below
- live_counts: int32 [2, 4096], P('win', 'tile'), may hold values from 1 to 128
- edge_turns: int32 [64, 2], P('tile'), may hold values 0 or 1
- w_query: bfloat16 [256, 256], replicated, may hold values from -0.375 to 0.375
- w_key: bfloat16 [256, 256], replicated, may hold values from -0.375 to 0.375
- w_value: bfloat16 [256, 256], replicated, may hold values from -0.375 to 0.375
- w_out: bfloat16 [256, 256], replicated, may hold values from -0.375 to 0.375
- w_conv: bfloat16 [3, 3, 256, 256], replicated, may hold values from -0.21875 to 0.21875
- token_cotan: bfloat16 [2, 524288, 256], P('win', 'tile'), may hold values from -6 to 6
Outputs:
- token_out: bfloat16 [2, 524288, 256], P('win', 'tile')
- token_grad: bfloat16 [2, 524288, 256], P('win', 'tile')
- grid_grad: bfloat16 [2, 2048, 32, 256], P('win', 'tile')
- upd_query: float32 [256, 256], replicated
- upd_key: float32 [256, 256], replicated
- upd_value: float32 [256, 256], replicated
- upd_out: float32 [256, 256], replicated
- upd_conv: float32 [3, 3, 256, 256], replicated
Inputs may be any that keep to these rules, and one draw needn't show every extreme that they name: `targets`: among the 64 token blocks of one device, no tile block is named more than 2 times, and some tile block is named exactly 2 times. `sub_masks`: each row holds exactly one 1.
All inputs are finite; a program needn't handle non-finite values. No bound on the sum of `edge_turns` on one device may be relied on, other than what follows from the above.
Results may differ from a plain program's by a relative error of at most 0.04.
The roundings to bfloat16 on the way count: a program that leaves them out, or rounds other values in their place, can miss the bound.
Values may be sent and summed in bfloat16 or wider, within the bound.
No kernel may reach another device: no remote copies, remote signals or barrier semaphores. Data moves between devices by JAX's collectives and lax.ppermute only.
A program may use at most 256 MiB of HBM per device.

v0:
```python
import math

import jax
import jax.numpy as jnp
from jax import lax
from jax.sharding import PartitionSpec as P

D = 256
HEADS = 8
BT = 128
RY = 32
RX = 32
SUB = 8
KEYS = 128
CAP = 2
GROUP = 16


EPSILON = 1e-06


def padded_2(block, sides, width):
    for axis, dim in sides:
        count = lax.axis_size(axis)
        forward = [(i, i + 1) for i in range(count - 1)]
        forward.append((count - 1, 0))
        backward = [(target, source) for source, target in forward]
        low = lax.ppermute(
            lax.slice_in_dim(block, block.shape[dim] - width, None, axis=dim), axis, forward
        )
        high = lax.ppermute(lax.slice_in_dim(block, 0, width, axis=dim), axis, backward)
        block = jnp.concatenate([low, block, high], axis=dim)
    return block


def from_behind(value, axis, by):
    length = lax.axis_size(axis)
    return lax.ppermute(value, axis, [(i, (i + by) % length) for i in range(length)])


def turned(row, flag):
    return jnp.where(flag == 1, row[::-1], row)


def rms_scaled(grad, total):
    return grad / jnp.sqrt(total / grad.size + EPSILON)


def local(
    grid,
    tokens,
    targets,
    sub_masks,
    live_counts,
    edge_turns,
    w_query,
    w_key,
    w_value,
    w_out,
    w_conv,
    token_cotan,
):
    f32 = jnp.float32
    bf16 = jnp.bfloat16
    ntile = lax.axis_size("tile")
    slots = ntile * CAP
    groups = slots // GROUP
    head_dim = D // HEADS
    scale = 1.0 / math.sqrt(head_dim)
    turns = edge_turns[0]
    tok_rows = tokens.shape[1]
    nblocks = tok_rows // BT
    field = grid[0]
    rimmed = padded_2(field, (("tile", 0),), 1)
    top = turned(rimmed[0], turns[0])
    bottom = turned(rimmed[-1], turns[1])
    rimmed = jnp.concatenate([top[None], field, bottom[None]], axis=0)
    padded = jnp.pad(rimmed, ((0, 0), (1, 1), (0, 0)))
    total = field.astype(f32)
    for a in range(3):
        for b in range(3):
            cells = padded[a : a + RY, b : b + RX].reshape(-1, D)
            total = total + jnp.dot(cells, w_conv[a, b], preferred_element_type=f32).reshape(
                RY, RX, D
            )
    hidden = total.astype(bf16).reshape(-1, D)
    key_table = (
        jnp.dot(hidden, w_key, preferred_element_type=f32).astype(bf16).reshape(SUB, KEYS, D)
    )
    value_table = (
        jnp.dot(hidden, w_value, preferred_element_type=f32).astype(bf16).reshape(SUB, KEYS, D)
    )
    x = tokens[0]
    dest = targets[0, :, 0]
    dest_hot = (dest[:, None] == jnp.arange(ntile, dtype=jnp.int32)[None, :]).astype(jnp.int32)
    before = jnp.cumsum(dest_hot, axis=0) - dest_hot
    rank = jnp.sum(before * dest_hot, axis=1)
    slot_of = dest * CAP + rank
    placing = (jnp.arange(slots, dtype=jnp.int32)[:, None] == slot_of[None, :]).astype(bf16)

    def to_slots(block_rows):
        return jnp.dot(placing, block_rows, preferred_element_type=f32).astype(bf16)

    def from_slots(slot_rows):
        return lax.dot_general(
            placing, slot_rows, (((0,), (0,)), ((), ())), preferred_element_type=f32
        ).astype(bf16)

    queries = jnp.dot(x, w_query, preferred_element_type=f32).astype(bf16)
    send_q = to_slots(queries.reshape(nblocks, BT * D)).reshape(ntile, CAP, BT, D)
    send_sub = to_slots(sub_masks[0].astype(bf16)).reshape(ntile, CAP, SUB)
    recv_q, recv_sub = (
        lax.all_to_all(send_q, "tile", split_axis=0, concat_axis=0, tiled=True),
        lax.all_to_all(send_sub, "tile", split_axis=0, concat_axis=0, tiled=True),
    )
    q_groups = recv_q.reshape(groups, GROUP, BT, D)
    sub_groups = recv_sub.reshape(groups, GROUP, SUB)
    sub_index = jnp.sum(
        recv_sub.reshape(groups, GROUP, SUB).astype(f32)
        * jnp.arange(SUB, dtype=f32)[None, None, :],
        axis=2,
    ).astype(jnp.int32)

    def pick(sub_g, table):
        chosen = jnp.einsum("gs,skd->gkd", sub_g, table, preferred_element_type=f32).astype(bf16)
        return chosen.reshape(GROUP, KEYS, HEADS, head_dim)

    def forward_group(item):
        q_g, sub_g = item
        k_h = pick(sub_g, key_table)
        v_h = pick(sub_g, value_table)
        q_h = q_g.reshape(GROUP, BT, HEADS, head_dim)
        scores = jnp.einsum("gqhe,gkhe->ghqk", q_h, k_h, preferred_element_type=f32) * scale
        shifted = jnp.exp(scores - jnp.max(scores, axis=-1, keepdims=True))
        weights = (shifted / jnp.sum(shifted, axis=-1, keepdims=True)).astype(bf16)
        attended = jnp.einsum("ghqk,gkhe->gqhe", weights, v_h, preferred_element_type=f32).astype(
            bf16
        )
        return (attended.reshape(GROUP, BT, D), weights)

    attended_slots, kept_weights = lax.map(forward_group, (q_groups, sub_groups))
    back_out = lax.all_to_all(
        attended_slots.reshape(ntile, CAP, BT, D), "tile", split_axis=0, concat_axis=0, tiled=True
    )
    attended = from_slots(back_out.reshape(slots, BT * D)).reshape(tok_rows, D)
    live = (jnp.arange(BT, dtype=jnp.int32)[None, :] < live_counts[0][:, None]).reshape(tok_rows, 1)
    mixed = jnp.dot(attended, w_out, preferred_element_type=f32)
    token_out = jnp.where(live, mixed, 0.0).astype(bf16)
    out_cot = jnp.where(live, token_cotan[0], jnp.zeros((), bf16))
    grad_out = lax.dot_general(
        attended, out_cot, (((0,), (0,)), ((), ())), preferred_element_type=f32
    )
    attended_grad = lax.dot_general(
        out_cot, w_out, (((1,), (1,)), ((), ())), preferred_element_type=f32
    ).astype(bf16)
    send_grad = to_slots(attended_grad.reshape(nblocks, BT * D)).reshape(ntile, CAP, BT, D)
    recv_grad = lax.all_to_all(send_grad, "tile", split_axis=0, concat_axis=0, tiled=True)
    grad_groups = recv_grad.reshape(groups, GROUP, BT, D)

    def backward_group(carry, item):
        key_acc, value_acc = carry
        q_g, sub_g, idx_g, d_g, weights = item
        k_h = pick(sub_g, key_table)
        v_h = pick(sub_g, value_table)
        q_h = q_g.reshape(GROUP, BT, HEADS, head_dim)
        d_h = d_g.reshape(GROUP, BT, HEADS, head_dim)
        weight_grad = jnp.einsum("gqhe,gkhe->ghqk", d_h, v_h, preferred_element_type=f32)
        wf = weights.astype(f32)
        score_grad = (
            wf * (weight_grad - jnp.sum(wf * weight_grad, axis=-1, keepdims=True)) * scale
        ).astype(bf16)
        query_grad = jnp.einsum(
            "ghqk,gkhe->gqhe", score_grad, k_h, preferred_element_type=f32
        ).astype(bf16)
        key_part = jnp.einsum(
            "ghqk,gqhe->gkhe", score_grad, q_h, preferred_element_type=f32
        ).reshape(GROUP, KEYS, D)
        value_part = jnp.einsum(
            "ghqk,gqhe->gkhe", weights, d_h, preferred_element_type=f32
        ).reshape(GROUP, KEYS, D)
        key_acc = key_acc.at[idx_g].add(key_part)
        value_acc = value_acc.at[idx_g].add(value_part)
        return ((key_acc, value_acc), query_grad.reshape(GROUP, BT, D))

    zero = jnp.zeros((SUB, KEYS, D), f32)
    (key_grad, value_grad), query_slots = lax.scan(
        backward_group, (zero, zero), (q_groups, sub_groups, sub_index, grad_groups, kept_weights)
    )
    back_query = lax.all_to_all(
        query_slots.reshape(ntile, CAP, BT, D), "tile", split_axis=0, concat_axis=0, tiled=True
    )
    query_grad = from_slots(back_query.reshape(slots, BT * D)).reshape(tok_rows, D)
    token_grad = lax.dot_general(
        query_grad, w_query, (((1,), (1,)), ((), ())), preferred_element_type=f32
    ).astype(bf16)
    grad_query = lax.dot_general(
        x, query_grad, (((0,), (0,)), ((), ())), preferred_element_type=f32
    )
    keys_back = key_grad.reshape(-1, D).astype(bf16)
    values_back = value_grad.reshape(-1, D).astype(bf16)
    grad_key = lax.dot_general(
        hidden, keys_back, (((0,), (0,)), ((), ())), preferred_element_type=f32
    )
    grad_value = lax.dot_general(
        hidden, values_back, (((0,), (0,)), ((), ())), preferred_element_type=f32
    )
    hidden_grad = lax.dot_general(
        keys_back, w_key, (((1,), (1,)), ((), ())), preferred_element_type=f32
    )
    hidden_grad = hidden_grad + lax.dot_general(
        values_back, w_value, (((1,), (1,)), ((), ())), preferred_element_type=f32
    )
    hidden_back = hidden_grad.astype(bf16)
    rim_grad = jnp.zeros((RY + 2, RX + 2, D), f32)
    tap_rows = []
    for a in range(3):
        for b in range(3):
            cells = padded[a : a + RY, b : b + RX].reshape(-1, D)
            tap_rows.append(
                lax.dot_general(
                    cells, hidden_back, (((0,), (0,)), ((), ())), preferred_element_type=f32
                )
            )
            back = lax.dot_general(
                hidden_back, w_conv[a, b], (((1,), (1,)), ((), ())), preferred_element_type=f32
            )
            rim_grad = rim_grad + jnp.pad(back.reshape(RY, RX, D), ((a, 2 - a), (b, 2 - b), (0, 0)))
    grad_conv = jnp.stack(tap_rows).reshape(3, 3, D, D)
    field_grad = hidden_grad.reshape(RY, RX, D) + rim_grad[1:-1, 1:-1]
    up_send = turned(rim_grad[0, 1:-1], turns[0])
    from_below = from_behind(up_send, "tile", -1)
    down_send = turned(rim_grad[-1, 1:-1], turns[1])
    from_above = from_behind(down_send, "tile", 1)
    field_grad = field_grad.at[-1].add(from_below)
    field_grad = field_grad.at[0].add(from_above)
    grid_grad = field_grad.astype(bf16)[None]
    sums = lax.psum((grad_query, grad_key, grad_value, grad_out, grad_conv), ("tile", "win"))
    upd_query, upd_key, upd_value, upd_out, upd_conv = [
        rms_scaled(item, jnp.sum(item * item)) for item in sums
    ]
    return (
        token_out[None],
        token_grad[None],
        grid_grad,
        upd_query,
        upd_key,
        upd_value,
        upd_out,
        upd_conv,
    )


def solution(mesh):
    return jax.shard_map(
        local,
        mesh=mesh,
        in_specs=(
            P("win", "tile", None, None),
            P("win", "tile", None),
            P("win", "tile", None),
            P("win", "tile", None),
            P("win", "tile"),
            P("tile", None),
            P(),
            P(),
            P(),
            P(),
            P(),
            P("win", "tile", None),
        ),
        out_specs=(
            P("win", "tile", None),
            P("win", "tile", None),
            P("win", "tile", None, None),
            P(),
            P(),
            P(),
            P(),
            P(),
        ),
        check_vma=False,
    )
```

profile of v0, /device:TPU:1, one launch (start us, length us, event | category | flops | bytes accessed | tf_op | source)
XLA Modules:
  0.0 1366.0 jit_solution(2177226460324795545)
XLA Ops:
  11.1 12.0 all-to-all-start
  28.6 7.4 reshape.339
  35.9 7.8 convolution_convert_fusion.6
  43.7 9.1 copy.66
  52.8 10.2 all-to-all-start.1
  63.0 6.7 collective-permute-start.1
  76.8 7.4 reshape.346
  84.2 7.8 convolution_convert_fusion.5
  91.9 9.2 copy.68
  101.7 53.8 %collective-permute-done.1 = bf16[1,32,256]{2,1,0:T(8,128)(2,1)S(1)} collective-permute-done((bf16[1,32,256]{2,1,0:T(8,128)(2,1)S(1)}, bf16[1,32,256]{2,1,0:T(8,128)(2,1)S(1)}, u32[]{:S(2)}, u32[]{:S(2)}) %collective-permute-start.1) | collective-permute-done | bytes 16416 | tf_op jit(solution)/shard_map/ppermute | solution.py:31
  155.6 8.3 collective-permute-done
  171.3 31.1 %all-to-all-start.3 = ((bf16[64,2,128,256]{3,2,1,0:T(8,128)(2,1)}), bf16[64,2,128,256]{3,2,1,0:T(8,128)(2,1)}, u32[]{:S(2)}, u32[]{:S(2)}) async-start(bf16[64,2,128,256]{3,2,1,0:T(8,128)(2,1)} %bitcast.402), calls=%async_computation.3 | async-start | bytes 16777216 | tf_op jit(solution)/shard_map/all_to_all | solution.py:157
  202.5 11.9 copy.49
  219.7 201.7 %while.28 = (s32[]{:T(128)}, bf16[8,16,128,256]{2,3,1,0:T(8,128)(2,1)}, bf16[8,16,8,128,128]{3,4,2,1,0:T(8,128)(2,1)}, bf16[8,16,8]{1,2,0:T(8,128)(2,1)S(1)}, bf...) while((s32[]{:T(128)}, ...), condition=%wide.region_5.6_spmd, body=%wide.region_2.5_spmd.sunk | while | flops 297271424 | bytes 45225056 | solution.py:141
  228.9 9.0 bitcast_dynamic-update-slice_fusion.2
  254.1 9.1 bitcast_dynamic-update-slice_fusion.2
  279.4 9.1 bitcast_dynamic-update-slice_fusion.2
  304.6 9.0 bitcast_dynamic-update-slice_fusion.2
  329.8 9.0 bitcast_dynamic-update-slice_fusion.2
  355.0 9.1 bitcast_dynamic-update-slice_fusion.2
  380.2 9.1 bitcast_dynamic-update-slice_fusion.2
  405.5 9.0 bitcast_dynamic-update-slice_fusion.2
  421.5 11.9 copy.54
  440.9 433.7 %while.29 = (s32[]{:T(128)}, f32[8,128,256]{2,1,0:T(8,128)}, f32[8,128,256]{2,1,0:T(8,128)}, bf16[8,16,128,256]{2,3,1,0:T(8,128)(2,1)}, s32[8,16]{1,0:T(8,128)S(...) while((s32[]{:T(128)}, f32[8,128,256]{2,1,0:T(8,128)}, ...), condition=%wide.region_11.12_spmd, body=%wide.region_7.11_spmd.sunk | while | flops 585662784 | bytes 116399552 | solution.py:186
  452.7 11.1 fusion.282
  466.1 12.0 fusion.283
  484.6 5.9 fusion.284
  507.2 10.9 fusion.282
  520.5 11.9 fusion.283
  538.6 5.9 fusion.284
  561.3 10.9 fusion.282
  574.5 11.9 fusion.283
  592.6 5.9 fusion.284
  615.3 11.0 fusion.282
  628.6 11.9 fusion.283
  646.6 5.9 fusion.284
  669.3 11.1 fusion.282
  682.7 12.0 fusion.283
  700.8 5.9 fusion.284
  723.5 10.9 fusion.282
  736.8 11.9 fusion.283
  754.8 5.9 fusion.284
  777.5 10.9 fusion.282
  790.8 11.9 fusion.283
  808.9 5.9 fusion.284
  831.5 10.9 fusion.282
  844.9 11.9 fusion.283
  863.2 5.9 fusion.284
  874.6 11.8 copy.58
  886.4 14.5 %all-to-all-start.4 = ((bf16[64,2,128,256]{3,2,1,0:T(8,128)(2,1)}), bf16[64,2,128,256]{3,2,1,0:T(8,128)(2,1)}, u32[]{:S(2)}, u32[]{:S(2)}) async-start(bf16[64,2,128,256]{3,2,1,0:T(8,128)(2,1)} %copy.58), calls=%async_computation.4 | async-start | bytes 16777216 | tf_op jit(solution)/shard_map/all_to_all | solution.py:189
  901.0 12.0 copy.53
  913.0 95.6 %all-to-all-done.4 = bf16[64,2,128,256]{3,2,1,0:T(8,128)(2,1)} async-done(((bf16[64,2,128,256]{3,2,1,0:T(8,128)(2,1)}), bf16[64,2,128,256]{3,2,1,0:T(8,128)(2,1)}, u32[]{:S(2)}, u32[]{:S(2)}) %all-to-all-start.4) | async-done | bytes 8388640 | tf_op jit(solution)/shard_map/all_to_all | solution.py:189
  1008.6 21.8 %all-to-all-start.2 = ((bf16[64,2,128,256]{3,2,1,0:T(8,128)(2,1)}), bf16[64,2,128,256]{3,2,1,0:T(8,128)(2,1)}, u32[]{:S(2)}, u32[]{:S(2)}) async-start(bf16[64,2,128,256]{3,2,1,0:T(8,128)(2,1)} %copy.53), calls=%async_computation.2 | async-start | bytes 16777216 | tf_op jit(solution)/shard_map/all_to_all | solution.py:142
  1041.6 6.9 collective-permute-start.2
  1056.4 12.4 copy.69
  1068.7 6.7 convolution_convert_fusion.7
  1075.4 7.6 reshape.351
  1088.5 51.1 %all-to-all-done.2 = bf16[64,2,128,256]{3,2,1,0:T(8,128)(2,1)} async-done(((bf16[64,2,128,256]{3,2,1,0:T(8,128)(2,1)}), bf16[64,2,128,256]{3,2,1,0:T(8,128)(2,1)}, u32[]{:S(2)}, u32[]{:S(2)}) %all-to-all-start.2) | async-done | bytes 8388640 | tf_op jit(solution)/shard_map/all_to_all | solution.py:142
  1139.6 12.4 copy.67
  1151.9 6.7 convolution_convert_fusion.8
  1158.6 7.4 reshape.345
  1166.0 7.8 fusion.49
  1177.9 7.8 collective-permute-done.3
  1195.1 148.9 %all-reduce.13.cloned.1.call-done = (f32[256,256]{0,1:T(8,128)}, f32[256,256]{1,0:T(8,128)}, f32[256,256]{1,0:T(8,128)}, f32[256,256]{1,0:T(8,128)}, f32[3,3,256,256]{3,2,1,0:T(8,128)}) async-done(((f32[256,256]{0,1:T(8,128)}, f32[256,256]{1,0:T(8,128)}, f32[256,256]{1,0:T(8,128)}, f32[256,256]{1,0:T(8,128)}, f32[3,3,256,256]{3,2,1,0:T(8,128)}), (f32[256,256]{0,1:T(8,128)}, f32[256,256]{1,0:T(8,128)}, ...) | async-done | bytes 3407888 | tf_op jit(solution)/shard_map/psum | solution.py:237
  (372 shorter events, 416.2 us)
Async XLA Ops:
  7.2 15.9 %copy-start = (bf16[256,256]{1,0:T(8,128)(2,1)S(1)}, bf16[256,256]{1,0:T(8,128)(2,1)}, u32[]{:S(2)}) copy-start(bf16[256,256]{1,0:T(8,128)(2,1)} %param.26) | copy-start | bytes 393220
  9.6 74.6 %copy-start.37 = (s32[64]{0:T(128)}, s32[64]{0:T(128)S(1)}, u32[]{:S(2)}) copy-start(s32[64]{0:T(128)S(1)} %multiply_add_fusion) | copy-start | bytes 772
  11.1 41.7 %all-to-all-start = ((bf16[64,2,8]{2,1,0:T(2,128)(2,1)}), bf16[64,2,8]{2,1,0:T(2,128)(2,1)S(1)}, u32[]{:S(2)}, u32[]{:S(2)}) async-start(bf16[64,2,8]{2,1,0:T(2,128)(2,1)} %bitcast.27), calls=%async_computation | async-start | bytes 65536 | tf_op jit(solution)/shard_map/all_to_all | solution.py:114
  52.8 10.2 copy-start.8
  52.8 17.5 %copy-start.41 = (s32[1,2]{1,0:T(1,128)S(1)}, s32[1,2]{1,0:T(1,128)}, u32[]{:S(2)}) copy-start(s32[1,2]{1,0:T(1,128)} %param.25) | copy-start | bytes 28
  52.8 19.4 %copy-start.42 = (s32[1,64]{1,0:T(1,128)S(1)}, s32[1,64]{1,0:T(1,128)}, u32[]{:S(2)}) copy-start(s32[1,64]{1,0:T(1,128)} %param.24) | copy-start | bytes 772
  52.8 19.5 %copy-start.43 = (bf16[256,256]{1,0:T(8,128)(2,1)S(1)}, bf16[256,256]{1,0:T(8,128)(2,1)}, u32[]{:S(2)}) copy-start(bf16[256,256]{1,0:T(8,128)(2,1)} %param.29) | copy-start | bytes 393220
  52.8 118.5 %all-to-all-start.1 = ((bf16[64,2,128,256]{3,2,1,0:T(8,128)(2,1)}), bf16[64,2,128,256]{3,2,1,0:T(8,128)(2,1)}, u32[]{:S(2)}, u32[]{:S(2)}) async-start(bf16[64,2,128,256]{3,2,1,0:T(8,128)(2,1)} %bitcast.403), calls=%async_computation.1 | async-start | bytes 16777216 | tf_op jit(solution)/shard_map/all_to_all | solution.py:113
  63.0 92.5 %collective-permute-start.1 = (bf16[1,32,256]{2,1,0:T(8,128)(2,1)S(1)}, bf16[1,32,256]{2,1,0:T(8,128)(2,1)S(1)}, u32[]{:S(2)}, u32[]{:S(2)}) collective-permute-start(bf16[1,32,256]{2,1,0:T(8,128)(2,1)S(1)} %get-tuple-element.246), channel_id=1, source_target_pairs={{2,0},{4,2},{6,4},{8,6},{10,8},{12,10},{14,12},{16,14},{18,16},{20... | collective-permute-start | bytes 49160 | tf_op jit(solution)/shard_map/ppermute | solution.py:31
  69.8 94.2 %collective-permute-start = (bf16[1,32,256]{2,1,0:T(8,128)(2,1)S(1)}, bf16[1,32,256]{2,1,0:T(8,128)(2,1)S(1)}, u32[]{:S(2)}, u32[]{:S(2)}) collective-permute-start(bf16[1,32,256]{2,1,0:T(8,128)(2,1)S(1)} %get-tuple-element.245), channel_id=1, source_target_pairs={{0,2},{2,4},{4,6},{6,8},{8,10},{10,12},{12,14},{14,16},{16,18},{18... | collective-permute-start | bytes 49160 | tf_op jit(solution)/shard_map/ppermute | solution.py:28
  72.3 4.5 copy-start.39
  91.9 9.2 copy-start.14
  164.0 2.8 copy-start.33
  164.1 2.2 copy-start.35
  164.4 1.6 copy-start.6
  166.9 1.7 copy-start.31
  167.2 1.4 copy-start.10
  171.3 250.1 %all-to-all-start.3 = ((bf16[64,2,128,256]{3,2,1,0:T(8,128)(2,1)}), bf16[64,2,128,256]{3,2,1,0:T(8,128)(2,1)}, u32[]{:S(2)}, u32[]{:S(2)}) async-start(bf16[64,2,128,256]{3,2,1,0:T(8,128)(2,1)} %bitcast.402), calls=%async_computation.3 | async-start | bytes 16777216 | tf_op jit(solution)/shard_map/all_to_all | solution.py:157
  484.6 7.8 copy-start.2
  538.6 7.8 copy-start.2
  548.7 1.0 copy-start.3
  592.6 7.8 copy-start.2
  602.7 1.0 copy-start.3
  646.6 7.8 copy-start.2
  656.7 1.0 copy-start.3
  700.8 7.8 copy-start.2
  754.8 7.8 copy-start.2
  808.9 7.8 copy-start.2
  818.9 1.0 copy-start.3
  863.2 7.8 copy-start.2
  886.4 122.1 %all-to-all-start.4 = ((bf16[64,2,128,256]{3,2,1,0:T(8,128)(2,1)}), bf16[64,2,128,256]{3,2,1,0:T(8,128)(2,1)}, u32[]{:S(2)}, u32[]{:S(2)}) async-start(bf16[64,2,128,256]{3,2,1,0:T(8,128)(2,1)} %copy.58), calls=%async_computation.4 | async-start | bytes 16777216 | tf_op jit(solution)/shard_map/all_to_all | solution.py:189
  913.0 117.4 %copy-start.9 = (bf16[1,32,32,256]{3,2,1,0:T(8,128)(2,1)S(1)}, bf16[1,32,32,256]{3,2,1,0:T(8,128)(2,1)}, u32[]{:S(2)}) copy-start(bf16[1,32,32,256]{3,2,1,0:T(8,128)(2,1)} %param.20) | copy-start | bytes 1572868
  913.0 117.4 %copy-start.34 = (bf16[1,32,256]{2,1,0:T(8,128)(2,1)S(1)}, bf16[1,32,256]{2,1,0:T(8,128)(2,1)}, u32[]{:S(2)}) copy-start(bf16[1,32,256]{2,1,0:T(8,128)(2,1)} %copy-done.33) | copy-start | bytes 49156
  913.0 117.5 %copy-start.36 = (bf16[1,32,256]{2,1,0:T(8,128)(2,1)S(1)}, bf16[1,32,256]{2,1,0:T(8,128)(2,1)}, u32[]{:S(2)}) copy-start(bf16[1,32,256]{2,1,0:T(8,128)(2,1)} %copy-done.35) | copy-start | bytes 49156
  913.0 118.4 %copy-start.7 = (bf16[34,34,256]{2,1,0:T(8,128)(2,1)S(1)}, bf16[34,34,256]{2,1,0:T(8,128)(2,1)}, u32[]{:S(2)}) copy-start(bf16[34,34,256]{2,1,0:T(8,128)(2,1)} %copy-done.6) | copy-start | bytes 1775620
  1008.6 131.0 %all-to-all-start.2 = ((bf16[64,2,128,256]{3,2,1,0:T(8,128)(2,1)}), bf16[64,2,128,256]{3,2,1,0:T(8,128)(2,1)}, u32[]{:S(2)}, u32[]{:S(2)}) async-start(bf16[64,2,128,256]{3,2,1,0:T(8,128)(2,1)} %copy.53), calls=%async_computation.2 | async-start | bytes 16777216 | tf_op jit(solution)/shard_map/all_to_all | solution.py:142
  1030.3 2.9 copy-start.1
  1030.4 313.6 %all-reduce.13.cloned.1.call-start = ((), (), s32[]{:S(2)}) async-start(), calls=%async_computation.5 | async-start | bytes 6815744 | tf_op jit(solution)/shard_map/psum | solution.py:237
  1031.4 1.9 copy-start.4
  1031.4 2.0 copy-start.32
  1031.4 2.3 copy-start.30
  1033.2 1.8 copy-start.15
  1038.0 10.5 copy-start.11
  1039.4 1.1 copy-start.12
  1040.7 11.4 copy-start.26
  1040.7 11.7 copy-start.28
  1040.7 12.1 copy-start.27
  1041.6 136.3 %collective-permute-start.2 = (f32[32,256]{1,0:T(8,128)S(1)}, f32[32,256]{1,0:T(8,128)S(1)}, u32[]{:S(2)}, u32[]{:S(2)}) collective-permute-start(f32[32,256]{1,0:T(8,128)S(1)} %get-tuple-element.234), channel_id=1, source_target_pairs={{0,126},{2,0},{4,2},{6,4},{8,6},{10,8},{12,10},{14,12},{16,14},{18... | collective-permute-start | bytes 98312 | tf_op jit(solution)/shard_map/ppermute | solution.py:38
  1049.6 4.0 copy-start.25
  1050.6 3.3 copy-start.24
  1052.4 2.2 copy-start.23
  1055.0 1.4 copy-start.18
  1056.4 12.4 copy-start.38
  1158.6 7.4 copy-start.40
  1166.0 7.9 copy-start.13
  1166.0 7.9 copy-start.16
  1173.9 12.7 copy-start.5
  1174.1 11.6 collective-permute-start.3
  1186.6 3.3 copy-start.17
  1186.6 3.3 copy-start.44
  1344.0 7.0 copy-start.21
  1344.0 7.0 copy-start.22
  1344.0 10.5 copy-start.20
  1344.0 12.6 copy-start.19
  (5 other events, 4.8 us)
Sparse Core Ops, SparseCore 0:
  1174.0 169.9 all-reduce.12
where the time goes:
time: 1380 us; the launch traced here: 1370 us
  matrix products  461 us (33%)
  waiting for transfers between devices  367 us (27%)
  local copies, waits for them, and re-layouts  267 us (19%)
  other arithmetic  143 us (10%)
  starting transfers between devices  108 us (8%)
  between operations  19.8 us (1%)
    psum x1, waiting for transfers between devices, local(): lax.psum((grad_query, grad_key, grad_value, grad_out, grad_conv), ('tile'...  149 us
    all_to_all x1, waiting for transfers between devices, local(): lax.all_to_all(query_slots.reshape(ntile, CAP, BT, D), 'tile', split_axis...  95.6 us
    dot_general x8, matrix products, backward_group(): jnp.einsum('ghqk,gqhe->gkhe', score_grad, q_h, preferred_element_type=f32)  95.3 us
    dot_general x8, matrix products, backward_group(): jnp.einsum('ghqk,gkhe->gqhe', score_grad, k_h, preferred_element_type=f32)  87.7 us
    dynamic_update_slice x8, other arithmetic, local(): lax.map(forward_group, (q_groups, sub_groups))  72.5 us
    ppermute x1, waiting for transfers between devices, padded_2(): lax.ppermute(lax.slice_in_dim(block, 0, width, axis=dim), axis, backward)  53.8 us
    all_to_all x1, waiting for transfers between devices, local(): lax.all_to_all(attended_slots.reshape(ntile, CAP, BT, D), 'tile', split_a...  51.1 us
    dot_general x32, matrix products, pick(): jnp.einsum('gs,skd->gkd', sub_g, table, preferred_element_type=f32)  48.6 us
  transfers between devices with their start and end apart: 10, of which 7 were waited for; matrix products, arithmetic and copies ran while one was open for 28% of the time, Pallas kernels for 0%

commit v1 on v0

v1 whole, which is shorter than its diff:
```python
import math

import jax
import jax.numpy as jnp
from jax import lax
from jax.experimental import pallas as pl
from jax.experimental.pallas import tpu as pltpu
from jax.sharding import PartitionSpec as P

D = 256
HEADS = 8
HD = 32
BT = 128
RY = 32
RX = 32
SUB = 8
KEYS = 128
CELLS = RY * RX
EPSILON = 1e-06
SCALE = 1.0 / math.sqrt(HD)
EXP2_SCALE = SCALE * math.log2(math.e)
STEP = 8

f32 = jnp.float32
bf16 = jnp.bfloat16


def mm(a, b):
    return lax.dot_general(a, b, (((1,), (0,)), ((), ())), preferred_element_type=f32)


def mm_nt(a, b):
    return lax.dot_general(a, b, (((1,), (1,)), ((), ())), preferred_element_type=f32)


def whole(shape):
    return pl.BlockSpec(shape, lambda *_: (0,) * len(shape))


def hidden_kernel(req_ref, rim_ref, w_ref, send_a, send_b, shifts_ref, hid, sems):
    rim = rim_ref[...].astype(f32)
    rows = rim.shape[0]
    col = lax.broadcasted_iota(jnp.int32, (rows, D), 0) % RX
    shifts_ref[0] = jnp.where(col == 0, 0.0, pltpu.roll(rim, 1, 0)).astype(bf16)
    shifts_ref[1] = rim_ref[...]
    shifts_ref[2] = jnp.where(col == RX - 1, 0.0, pltpu.roll(rim, rows - 1, 0)).astype(bf16)
    piece = CELLS // 4

    @pl.loop(0, 4)
    def _(i):
        base = i * piece
        total = rim_ref[pl.ds(pl.multiple_of(base + RX, RX), piece), :].astype(f32)
        for a in range(3):
            for b in range(3):
                cells = shifts_ref[b, pl.ds(pl.multiple_of(base + a * RX, RX), piece), :]
                total = total + mm(cells, w_ref[3 * a + b])
        hid[pl.ds(pl.multiple_of(base, piece), piece), :] = total.astype(bf16)

    count = send_a.shape[0]

    def copy(c, out, s):
        sub = jnp.minimum(req_ref[s, c], SUB - 1)
        source = hid.at[pl.ds(pl.multiple_of(sub * KEYS, KEYS), KEYS), :]
        return pltpu.make_async_copy(source, out.at[s], sems.at[c])

    @pl.loop(0, count)
    def _(s):
        copy(0, send_a, s).start()
        copy(1, send_b, s).start()

    @pl.loop(0, count)
    def _(s):
        copy(0, send_a, s).wait()
        copy(1, send_b, s).wait()


def hidden_sends(req, rimmed, w_conv):
    count = req.shape[0]
    slots = jax.ShapeDtypeStruct((count, KEYS, D), bf16)
    rows = (RY + 2) * RX
    return pl.pallas_call(
        hidden_kernel,
        out_shape=(slots, slots, jax.ShapeDtypeStruct((3, rows, D), bf16)),
        in_specs=[
            pl.BlockSpec(memory_space=pltpu.SMEM),
            pl.BlockSpec(memory_space=pltpu.VMEM),
            pl.BlockSpec(memory_space=pltpu.VMEM),
        ],
        out_specs=(
            pl.BlockSpec(memory_space=pl.ANY),
            pl.BlockSpec(memory_space=pl.ANY),
            pl.BlockSpec(memory_space=pltpu.VMEM),
        ),
        scratch_shapes=[
            pltpu.VMEM((CELLS, D), bf16),
            pltpu.SemaphoreType.DMA((2,)),
        ],
        compiler_params=pltpu.CompilerParams(vmem_limit_bytes=40 * 1024 * 1024),
        cost_estimate=pl.CostEstimate(
            flops=2 * 9 * CELLS * D * D, bytes_accessed=20_000_000, transcendentals=0
        ),
        name="conv_sends",
    )(req, rimmed, w_conv)


def attend_kernel(
    meta, h_ref, x_ref, c_ref, wq, wq_t, wkv, wkv_t, wo, wo_t, grads_in, *rest
):
    out_ref, tgrad_ref, hgrad_ref, grads_ref = rest[-4:]
    i = pl.program_id(0)

    @pl.when(i == 0)
    def _():
        grads_ref[...] = grads_in[...]

    @pl.when(i < meta[3, 0])
    def _():
        live = meta[2, i]
        h = h_ref[0]
        x = x_ref[0]
        row = lax.broadcasted_iota(jnp.int32, (BT, D), 0)
        cot = jnp.where(row < live, c_ref[0].astype(f32), 0.0).astype(bf16)
        kv = mm(h, wkv[...]).astype(bf16)
        kv_t = mm_nt(wkv_t[...], h).astype(bf16)
        q_t = mm_nt(wq_t[...], x).astype(bf16)
        d_t = mm_nt(wo[...], cot).astype(bf16)
        zero = jnp.zeros((HD, BT), bf16)
        none = jnp.zeros((2 * HD, 2 * BT), bf16)

        def paired(t, p):
            first = t[2 * HD * p : 2 * HD * p + HD]
            second = t[2 * HD * p + HD : 2 * HD * p + 2 * HD]
            return jnp.concatenate(
                [
                    jnp.concatenate([first, zero], axis=1),
                    jnp.concatenate([zero, second], axis=1),
                ],
                axis=0,
            )

        def deep(pair, p):
            return jnp.concatenate([pair, none] if p % 2 == 0 else [none, pair], axis=0)

        att_rows, qg_rows, kg_rows, vg_rows = [], [], [], []
        for p in range(HEADS // 2):
            lanes = slice(128 * (p // 2), 128 * (p // 2) + 128)
            feats = slice(2 * HD * p, 2 * HD * p + 2 * HD)
            q2 = paired(q_t, p)
            d2 = paired(d_t, p)
            scores = mm(kv[:, lanes], deep(q2, p))
            top = jnp.max(scores, axis=0, keepdims=True)
            e = jnp.exp2((scores - top) * EXP2_SCALE)
            w = (e * (1.0 / jnp.sum(e, axis=0, keepdims=True))).astype(bf16)
            wf = w.astype(f32)
            wg = mm(kv[:, D + lanes.start : D + lanes.stop], deep(d2, p))
            mean = jnp.sum(wf * wg, axis=0, keepdims=True)
            sg = (wf * (wg - mean)).astype(bf16)
            att = mm(kv_t[D + feats.start : D + feats.stop], w)
            att_rows += [att[:HD, :BT], att[HD:, BT:]]
            qg = mm(kv_t[feats], sg)
            qg_rows += [qg[:HD, :BT], qg[HD:, BT:]]
            kg_rows.append(mm_nt(q2, sg) * SCALE)
            vg_rows.append(mm_nt(d2, w))
        att_t = jnp.concatenate(att_rows, axis=0).astype(bf16)
        qg_t = (jnp.concatenate(qg_rows, axis=0) * SCALE).astype(bf16)
        kvg_t = jnp.concatenate(kg_rows + vg_rows, axis=0).astype(bf16)
        lane = lax.broadcasted_iota(jnp.int32, (D, BT), 1)
        mixed = jnp.where(lane < live, mm(wo_t[...], att_t), 0.0)
        out_ref[0] = mixed.T.astype(bf16)
        tgrad_ref[0] = mm(wq[...], qg_t).T.astype(bf16)
        hgrad_ref[0] = mm(wkv[...], kvg_t).astype(bf16)
        grads_ref[0:256] += mm(qg_t, x)
        grads_ref[256:768] += mm(kvg_t, h)
        grads_ref[768:1024] += mm(att_t, cot)


def attend(meta, slots, x, cot, weights, grads, kept):
    nblocks = x.shape[0]
    count = slots.shape[0]
    by_tile = lambda i, m: (m[1, i], 0, 0)
    by_block = lambda i, m: (m[0, i], 0, 0)
    rows = pl.BlockSpec((1, BT, D), by_block)
    in_specs = [pl.BlockSpec((1, KEYS, D), by_tile), rows, rows]
    in_specs += [whole(w.shape) for w in weights] + [whole((4 * D, D))]
    in_specs += [pl.BlockSpec(memory_space=pl.ANY)] * len(kept)
    args = [meta, slots, x, cot, *weights, grads, *kept]
    first_kept = len(args) - len(kept)
    token_shape = jax.ShapeDtypeStruct((nblocks, BT, D), bf16)
    return pl.pallas_call(
        attend_kernel,
        out_shape=(
            token_shape,
            token_shape,
            jax.ShapeDtypeStruct((count, D, KEYS), bf16),
            jax.ShapeDtypeStruct((4 * D, D), f32),
        ),
        grid_spec=pltpu.PrefetchScalarGridSpec(
            num_scalar_prefetch=1,
            grid=(nblocks,),
            in_specs=in_specs,
            out_specs=(
                rows,
                rows,
                pl.BlockSpec((1, D, KEYS), by_tile),
                whole((4 * D, D)),
            ),
        ),
        input_output_aliases={first_kept + j: j for j in range(len(kept))},
        compiler_params=pltpu.CompilerParams(
            dimension_semantics=("arbitrary",), vmem_limit_bytes=40 * 1024 * 1024
        ),
        cost_estimate=pl.CostEstimate(
            flops=nblocks * 400_000_000, bytes_accessed=nblocks * 400_000, transcendentals=0
        ),
        name="attend",
    )(*args)


def add_slots(req_ref, slots_ref, acc_ref, column):
    i = pl.program_id(0)
    for j in range(STEP):
        sub = req_ref[i * STEP + j, column]

        @pl.when(sub < SUB)
        def _():
            at = pl.ds(pl.multiple_of(sub * D, D), D)
            acc_ref[at, :] += slots_ref[j].astype(f32)


def gather_kernel(req_ref, slots_ref, acc_ref):
    @pl.when(pl.program_id(0) == 0)
    def _():
        acc_ref[...] = jnp.zeros_like(acc_ref)

    add_slots(req_ref, slots_ref, acc_ref, 0)


def finish_kernel(req_ref, slots_ref, acc_in, shifts_ref, grads_ref, hgrad_ref, sums_ref, acc_ref, back_t):
    i = pl.program_id(0)

    @pl.when(i == 0)
    def _():
        acc_ref[...] = acc_in[...]

    add_slots(req_ref, slots_ref, acc_ref, 1)

    @pl.when(i == pl.num_programs(0) - 1)
    def _():
        sums_ref[0 : 4 * D] = grads_ref[...].astype(bf16)
        for s in range(SUB):
            part = acc_ref[s * D : (s + 1) * D, :]
            hgrad_ref[s * KEYS : (s + 1) * KEYS, :] = part.T
            back_t[:, s * KEYS : (s + 1) * KEYS] = part.astype(bf16)
        for a in range(3):
            for b in range(3):
                at = (4 + 3 * a + b) * D
                cells = shifts_ref[b, a * RX : a * RX + CELLS, :]
                sums_ref[at : at + D] = mm(back_t[...], cells).astype(bf16)


def slot_specs(count):
    return [
        pl.BlockSpec(memory_space=pltpu.SMEM),
        pl.BlockSpec((STEP, D, KEYS), lambda i: (i, 0, 0)),
    ]


def gather_slots(req, slots):
    count = slots.shape[0]
    return pl.pallas_call(
        gather_kernel,
        out_shape=jax.ShapeDtypeStruct((SUB * D, KEYS), f32),
        grid=(count // STEP,),
        in_specs=slot_specs(count),
        out_specs=whole((SUB * D, KEYS)),
        compiler_params=pltpu.CompilerParams(vmem_limit_bytes=40 * 1024 * 1024),
        cost_estimate=pl.CostEstimate(
            flops=count * D * KEYS, bytes_accessed=count * D * KEYS * 2, transcendentals=0
        ),
        name="gather_slots",
    )(req, slots)


def finish(req, slots, acc, shifts, grads):
    count = slots.shape[0]
    return pl.pallas_call(
        finish_kernel,
        out_shape=(
            jax.ShapeDtypeStruct((CELLS, D), f32),
            jax.ShapeDtypeStruct((13 * D, D), bf16),
        ),
        grid=(count // STEP,),
        in_specs=slot_specs(count)
        + [whole(acc.shape), whole(shifts.shape), whole(grads.shape)],
        out_specs=(whole((CELLS, D)), whole((13 * D, D))),
        scratch_shapes=[
            pltpu.VMEM((SUB * D, KEYS), f32),
            pltpu.VMEM((D, CELLS), bf16),
        ],
        compiler_params=pltpu.CompilerParams(vmem_limit_bytes=50 * 1024 * 1024),
        cost_estimate=pl.CostEstimate(
            flops=2 * 9 * CELLS * D * D, bytes_accessed=12_000_000, transcendentals=0
        ),
        name="finish",
    )(req, slots, acc, shifts, grads)


def ring(value, by):
    length = lax.axis_size("tile")
    return lax.ppermute(value, "tile", [(i, (i + by) % length) for i in range(length)])


def turned(row, flag):
    return jnp.where(flag == 1, row[::-1], row)


def exchange(value, axes="tile"):
    return lax.all_to_all(value, axes, split_axis=0, concat_axis=0, tiled=True)


def local(
    grid,
    tokens,
    targets,
    sub_masks,
    live_counts,
    edge_turns,
    w_query,
    w_key,
    w_value,
    w_out,
    w_conv,
    token_cotan,
):
    ntile = lax.axis_size("tile")
    ndev = ntile * lax.axis_size("win")
    me = lax.axis_index("tile")
    turns = edge_turns[0]
    nblocks = tokens.shape[1] // BT
    i32 = jnp.int32

    dest = targets[0, :, 0]
    order = jnp.arange(nblocks, dtype=i32)
    earlier = order[None, :] < order[:, None]
    rank = jnp.sum((earlier & (dest[None, :] == dest[:, None])).astype(i32), axis=1)
    chunk = (rank + dest + me) % 2
    sub = jnp.sum(sub_masks[0] * jnp.arange(SUB, dtype=i32)[None, :], axis=1)
    tiles = jnp.arange(ntile, dtype=i32)
    chunks = jnp.arange(2, dtype=i32)
    at_slot = (dest[:, None, None] == tiles[None, :, None]) & (
        chunk[:, None, None] == chunks[None, None, :]
    )
    want = SUB + jnp.sum(jnp.where(at_slot, sub[:, None, None] - SUB, 0), axis=0)
    req = exchange(want)

    place = jnp.sum((earlier & (chunk[None, :] == chunk[:, None])).astype(i32), axis=1)
    sizes = jnp.sum((chunk[:, None] == chunks[None, :]).astype(i32), axis=0)
    step = jnp.minimum(order[None, :], sizes[:, None] - 1)
    picked = (
        (place[None, None, :] == step[:, :, None]) & (chunk[None, None, :] == chunks[:, None, None])
    ).astype(i32)
    live = live_counts[0]
    columns = jnp.stack([order, dest, live], axis=0)
    lists = jnp.sum(picked[:, None] * columns[None, :, None, :], axis=-1)
    meta = jnp.concatenate(
        [lists, jnp.broadcast_to(sizes[:, None, None], (2, 1, nblocks))], axis=1
    )

    field = grid[0]
    above = turned(ring(field[-1], 1), turns[0])
    below = turned(ring(field[0], -1), turns[1])
    rimmed = jnp.concatenate([above[None], field, below[None]], axis=0).reshape(-1, D)
    send_a, send_b, shifts = hidden_sends(req, rimmed, w_conv.reshape(9, D, D))

    wkv = jnp.concatenate([w_key, w_value], axis=1)
    weights = (w_query, w_query.T, wkv, wkv.T, w_out, w_out.T)
    x = tokens[0].reshape(nblocks, BT, D)
    cot = token_cotan[0].reshape(nblocks, BT, D)
    got_a = exchange(send_a)
    got_b = exchange(send_b)
    zeros = jnp.zeros((4 * D, D), f32)
    out_a, tgrad_a, back_a, grads_a = attend(meta[0], got_a, x, cot, weights, zeros, ())
    ret_a = exchange(back_a)
    token_out, token_grad, back_b, grads = attend(
        meta[1], got_b, x, cot, weights, grads_a, (out_a, tgrad_a)
    )
    ret_b = exchange(back_b)
    acc = gather_slots(req, ret_a)
    hidden_grad, sums = finish(req, ret_b, acc, shifts, grads)

    parts = exchange(sums, ("tile", "win")).reshape(ndev, -1, D)
    share = jnp.sum(parts.astype(f32), axis=0).astype(bf16)
    spread = jnp.broadcast_to(share[None], (ndev,) + share.shape).reshape(-1, D)
    total = exchange(spread, ("tile", "win")).astype(f32).reshape(13, D, D)

    hidden_back = hidden_grad.astype(bf16).reshape(RY, RX, D)
    padded = jnp.pad(hidden_back, ((0, 0), (1, 1), (0, 0)))
    taps = []
    for a in range(3):
        piece = jnp.zeros((RY, RX, D), f32)
        for b in range(3):
            cells = padded[:, 2 - b : 2 - b + RX].reshape(-1, D)
            piece = piece + mm_nt(cells, w_conv[a, b]).reshape(RY, RX, D)
        taps.append(piece)
    from_below = ring(turned(taps[0][0], turns[0]), -1)
    from_above = ring(turned(taps[2][-1], turns[1]), 1)
    field_grad = hidden_grad.reshape(RY, RX, D) + taps[1]
    field_grad = field_grad + jnp.concatenate([taps[0][1:], from_below[None]], axis=0)
    field_grad = field_grad + jnp.concatenate([from_above[None], taps[2][:-1]], axis=0)
    grid_grad = field_grad.astype(bf16)[None]

    def scaled(grad):
        return grad / jnp.sqrt(jnp.mean(grad * grad) + EPSILON)

    upd_query = scaled(total[0]).T
    upd_key = scaled(total[1]).T
    upd_value = scaled(total[2]).T
    upd_out = scaled(total[3])
    upd_conv = scaled(total[4:]).transpose(0, 2, 1).reshape(3, 3, D, D)
    return (
        token_out.reshape(1, -1, D),
        token_grad.reshape(1, -1, D),
        grid_grad,
        upd_query,
        upd_key,
        upd_value,
        upd_out,
        upd_conv,
    )


def solution(mesh):
    return jax.shard_map(
        local,
        mesh=mesh,
        in_specs=(
            P("win", "tile", None, None),
            P("win", "tile", None),
            P("win", "tile", None),
            P("win", "tile", None),
            P("win", "tile"),
            P("tile", None),
            P(),
            P(),
            P(),
            P(),
            P(),
            P("win", "tile", None),
        ),
        out_specs=(
            P("win", "tile", None),
            P("win", "tile", None),
            P("win", "tile", None, None),
            P(),
            P(),
            P(),
            P(),
            P(),
        ),
        check_vma=False,
    )
```

time: 1380 us -> 451 us (0.33); the launches traced: 1370 us -> 452 us
  matrix products: 461 us -> 6.21 us
  waiting for transfers between devices: 367 us -> 86.8 us
  local copies, waits for them, and re-layouts: 267 us -> 31.8 us
  Pallas kernels: 0 us -> 163 us
  other arithmetic: 143 us -> 13 us
  blocking collectives: 0 us -> 55.8 us
  starting transfers between devices: 108 us -> 89.5 us
  between operations: 19.8 us -> 5.89 us
    dot_general x116 -> x9, matrix products: 418 us -> 6.21 us  [mm_nt(): lax.dot_general(a, b, (((1,), (1,)), ((), ())), preferred_element_type=f32)]
    pallas_call x0 -> x5, Pallas kernels: none -> 163 us  [the longest x2 134 us: attend(): pl.pallas_call(attend_kernel, out_shape=(token_shape, token_shape, jax.Sh...]
    psum x1 -> x0, waiting for transfers between devices: 149 us -> none  [local(): lax.psum((grad_query, grad_key, grad_value, grad_out, grad_conv), ('tile'...]
    all_to_all x5 -> x6, waiting for transfers between devices: 148 us -> 61.8 us  [exchange(): return lax.all_to_all(value, axes, split_axis=0, concat_axis=0, tiled=True)]
    reshape x22 -> x0, local copies, waits for them, and re-layouts: 84.2 us -> none  [the longest x8 15.3 us: backward_group(): key_part = jnp.einsum('ghqk,gqhe->gkhe', score_grad, q_h, preferred_eleme...]
    dynamic_update_slice x8 -> x0, other arithmetic: 72.5 us -> none  [local(): lax.map(forward_group, (q_groups, sub_groups))]
    all_to_all x0 -> x1, blocking collectives: none -> 55.8 us  [exchange(): return lax.all_to_all(value, axes, split_axis=0, concat_axis=0, tiled=True)]
    scatter-add x18 -> x0, other arithmetic: 52.2 us -> none  [the longest x8 34.6 us: backward_group(): key_acc = key_acc.at[idx_g].add(key_part)]
  transfers between devices with their start and end apart: 10 -> 10, of which waited for: 7 -> 3; matrix products, arithmetic and copies ran while one was open for 28% -> 3% of each run, Pallas kernels for 0% -> 31%
where the time goes in v1:
time: 451 us; the launch traced here: 452 us
  Pallas kernels  163 us (36%)
  starting transfers between devices  89.5 us (20%)
  waiting for transfers between devices  86.8 us (19%)
  blocking collectives  55.8 us (12%)
  local copies, waits for them, and re-layouts  31.8 us (7%)
  other arithmetic  13 us (3%)
  matrix products  6.21 us (1%)
  between operations  5.89 us (1%)
    pallas_call x2, Pallas kernels, attend(): pl.pallas_call(attend_kernel, out_shape=(token_shape, token_shape, jax.Sh...  134 us
    all_to_all x6, starting transfers between devices, exchange(): return lax.all_to_all(value, axes, split_axis=0, concat_axis=0, tiled=True)  73.4 us
    all_to_all x6, waiting for transfers between devices, exchange(): return lax.all_to_all(value, axes, split_axis=0, concat_axis=0, tiled=True)  61.8 us
    all_to_all x1, blocking collectives, exchange(): return lax.all_to_all(value, axes, split_axis=0, concat_axis=0, tiled=True)  55.8 us
    ppermute x4, waiting for transfers between devices, ring(): lax.ppermute(value, 'tile', [(i, (i + by) % length) for i in range(length)])  25 us
    unnamed x41, local copies, waits for them, and re-layouts  17.4 us
    ppermute x4, starting transfers between devices, ring(): lax.ppermute(value, 'tile', [(i, (i + by) % length) for i in range(length)])  16.1 us
    pallas_call x1, Pallas kernels, hidden_sends(): pl.pallas_call(hidden_kernel, out_shape=(slots, slots, jax.ShapeDtypeStru...  15.6 us
  transfers between devices with their start and end apart: 10, of which 3 were waited for; matrix products, arithmetic and copies ran while one was open for 3% of the time, Pallas kernels for 31%

profile of v1, /device:TPU:1, one launch (start us, length us, event | category | flops | bytes accessed | tf_op | source)
XLA Modules:
  0.0 451.7 jit_solution(16636224047061511963)
XLA Ops:
  0.6 0.9 convert_reduce_fusion.1
  1.5 0.7 iota_compare_fusion
  2.3 0.7 fusion.27
  3.0 0.7 and_select_fusion
  3.7 0.1 select_reduce_fusion
  3.8 0.7 copy.63
  4.5 12.0 %all-to-all-start = ((s32[64,1,2]{2,1,0:T(1,128)}), s32[64,1,2]{2,1,0:T(1,128)S(1)}, u32[]{:S(2)}, u32[]{:S(2)}) async-start(s32[64,1,2]{2,1,0:T(1,128)} %copy.63), calls=%async_computation | async-start | bytes 65536 | tf_op jit(solution)/shard_map/all_to_all | solution.py:318
  16.5 0.7 slice_bitcast_fusion.3
  17.2 1.0 collective-permute-start
  18.2 5.9 %collective-permute-start.1 = (bf16[32,256]{1,0:T(8,128)(2,1)S(1)}, bf16[32,256]{1,0:T(8,128)(2,1)S(1)}, u32[]{:S(2)}, u32[]{:S(2)}) collective-permute-start(bf16[32,256]{1,0:T(8,128)(2,1)S(1)} %get-tuple-element.75), channel_id=1, source_target_pairs={{0,126},{2,0},{4,2},{6,4},{8,6},{10,8},{12,10},{14,12},{16,14},{18... | collective-permute-start | bytes 49160 | tf_op jit(solution)/shard_map/ppermute | solution.py:310
  24.1 1.3 fusion.39
  27.2 1.1 pad_maximum_fusion
  28.3 1.3 copy-done.5
  29.5 15.6 %conv_sends.1 = (bf16[64,128,256]{2,1,0:T(8,128)(2,1)S(1)}, bf16[64,128,256]{2,1,0:T(8,128)(2,1)S(1)}, bf16[3,1088,256]{2,1,0:T(8,128)(2,1)S(1)}) custom-call(s32[64,2]{1,0:T(8,128)S(1)} %copy.65.req_ref, bf16[1088,256]{1,0:T(8,128)(2,1)S(1)} %bitcast.109, bf16[9,256,256]{2,1,0:T(8,128)(2,1)S(1)} %bitcast.108), custom_call_target="tpu_custom_call" | custom-call | flops 1207959552 | bytes 20000000 | tf_op jit(solution)/shard_map/conv_sends/pallas_call | solution.py:81
  45.2 55.8 %all_to_all.43.h_ref = bf16[64,128,256]{2,1,0:T(8,128)(2,1)} all-to-all(bf16[64,128,256]{2,1,0:T(8,128)(2,1)S(1)} %get-tuple-element.22), channel_id=1, replica_groups=mesh['tile'=64,'win'=2] {'tile'}, dimensions={0} | all-to-all | bytes 8388608 | tf_op jit(solution)/shard_map/all_to_all | solution.py:318
  101.0 11.4 %all-to-all-start.1 = ((bf16[64,128,256]{2,1,0:T(8,128)(2,1)}), bf16[64,128,256]{2,1,0:T(8,128)(2,1)}, u32[]{:S(2)}, u32[]{:S(2)}) async-start(bf16[64,128,256]{2,1,0:T(8,128)(2,1)} %copy-done), calls=%async_computation.1 | async-start | bytes 8388608 | tf_op jit(solution)/shard_map/all_to_all | solution.py:318
  112.5 0.1 copy.68
  112.9 0.1 copy.71.wkv
  113.1 0.1 convert_reduce_fusion.2
  113.2 0.2 convert_reduce_fusion
  113.6 0.2 multiply_reduce_fusion.5
  113.9 2.2 copy-done.1
  116.1 66.5 %attend.2 = (bf16[64,128,256]{2,1,0:T(8,128)(2,1)}, bf16[64,128,256]{2,1,0:T(8,128)(2,1)}, bf16[64,256,128]{2,1,0:T(8,128)(2,1)S(1)}, f32[1024,256]{1,0:T(8,128)S(1)}) custom-call(s32[4,64]{1,0:T(4,128)S(1)} %get-tuple-element.78.meta, bf16[64,128,256]{2,1,0:T(8,128)(2,1)S(1)} %copy-done.1, bf16[64,128,256]{2,1,0:T(8,128)(2,1)} %bitcast.132, ...), custom_call_target="tpu_custom_call" | custom-call | flops 25600000000 | bytes 25600000 | tf_op jit(solution)/shard_map/attend/pallas_call | solution.py:189
  182.6 2.0 copy-done.2
  184.6 1.0 copy-done.9
  185.6 13.5 %all-to-all-start.4 = ((bf16[64,256,128]{2,1,0:T(8,128)(2,1)}), bf16[64,256,128]{2,1,0:T(8,128)(2,1)}, u32[]{:S(2)}, u32[]{:S(2)}) async-start(bf16[64,256,128]{2,1,0:T(8,128)(2,1)} %copy-done.2), calls=%async_computation.4 | async-start | bytes 8388608 | tf_op jit(solution)/shard_map/all_to_all | solution.py:318
  199.2 1.2 copy-done.10
  200.4 67.3 %attend.3 = (bf16[64,128,256]{2,1,0:T(8,128)(2,1)}, bf16[64,128,256]{2,1,0:T(8,128)(2,1)}, bf16[64,256,128]{2,1,0:T(8,128)(2,1)S(1)}, f32[1024,256]{1,0:T(8,128)S(1)}) custom-call(s32[4,64]{1,0:T(4,128)S(1)} %get-tuple-element.79.meta, bf16[64,128,256]{2,1,0:T(8,128)(2,1)} %all-to-all-done.1.h_ref, ...), custom_call_target="tpu_custom_call", output_to_operand_aliasing={{0}: (11, {}), {1}: (12, {})} | custom-call | flops 25600000000 | bytes 25600000 | tf_op jit(solution)/shard_map/attend/pallas_call | solution.py:189
  267.7 1.9 copy-done.3
  269.6 13.4 %all-to-all-start.3 = ((bf16[64,256,128]{2,1,0:T(8,128)(2,1)}), bf16[64,256,128]{2,1,0:T(8,128)(2,1)}, u32[]{:S(2)}, u32[]{:S(2)}) async-start(bf16[64,256,128]{2,1,0:T(8,128)(2,1)} %copy-done.3), calls=%async_computation.3 | async-start | bytes 8388608 | tf_op jit(solution)/shard_map/all_to_all | solution.py:318
  283.1 5.0 %gather_slots.1.acc_in = f32[2048,128]{1,0:T(8,128)S(1)} custom-call(s32[64,2]{1,0:T(8,128)S(1)} %copy.65.req_ref, bf16[64,256,128]{2,1,0:T(8,128)(2,1)} %all-to-all-done.4.slots_ref), custom_call_target="tpu_custom_call" | custom-call | flops 2097152 | bytes 4194304 | tf_op jit(solution)/shard_map/gather_slots/pallas_call | solution.py:270
  288.1 43.8 %all-to-all-done.3.slots_ref = bf16[64,256,128]{2,1,0:T(8,128)(2,1)} async-done(((bf16[64,256,128]{2,1,0:T(8,128)(2,1)}), bf16[64,256,128]{2,1,0:T(8,128)(2,1)}, u32[]{:S(2)}, u32[]{:S(2)}) %all-to-all-start.3) | async-done | bytes 4194336 | tf_op jit(solution)/shard_map/all_to_all | solution.py:318
  331.9 8.3 %finish.1 = (f32[1024,256]{1,0:T(8,128)S(1)}, bf16[3328,256]{1,0:T(8,128)(2,1)}) custom-call(s32[64,2]{1,0:T(8,128)S(1)} %copy.65.req_ref, bf16[64,256,128]{2,1,0:T(8,128)(2,1)} %all-to-all-done.3.slots_ref, f32[2048,128]{1,0:T(8,128)S(1)} %gather_slots.1.acc_in, bf16[3,1088,256]{2,1,0:T(8,128)(2,1)} %copy-done.4, f32[1024,256]{1,0:T(8,128)S(1)} %get-tuple-element.31.grads_ref), custom_call_target="tpu_custom_call" | custom-call | flops 1207959552 | bytes 12000000 | tf_op jit(solution)/shard_map/finish/pallas_call | solution.py:286
  340.2 3.8 all_to_all.33
  343.9 17.5 %all-to-all-start.5 = ((bf16[128,26,256]{2,1,0:T(8,128)(2,1)}), bf16[128,26,256]{2,1,0:T(8,128)(2,1)}, u32[]{:S(2)}, u32[]{:S(2)}) async-start(bf16[128,26,256]{2,1,0:T(8,128)(2,1)} %all_to_all.33), calls=%async_computation.5 | async-start | bytes 4194304 | tf_op jit(solution)/shard_map/all_to_all | solution.py:318
  361.6 0.3 fusion.5
  361.9 0.3 convolution_add_fusion.3
  362.2 0.3 convolution_add_fusion.2
  362.6 1.0 copy-done.11
  363.6 0.8 broadcast_select_fusion.1
  364.4 7.7 %collective-permute-start.2 = (f32[32,256]{1,0:T(8,128)S(1)}, f32[32,256]{1,0:T(8,128)S(1)}, u32[]{:S(2)}, u32[]{:S(2)}) collective-permute-start(f32[32,256]{1,0:T(8,128)S(1)} %broadcast_select_fusion.1), channel_id=1, source_target_pairs={{0,126},{2,0},{4,2},{6,4},{8,6},{10,8},{12,10},{14,12},{16,14},{18... | collective-permute-start | bytes 98312 | tf_op jit(solution)/shard_map/ppermute | solution.py:310
  372.1 1.4 fusion.4
  373.5 18.0 %all-to-all-done.5 = bf16[128,26,256]{2,1,0:T(8,128)(2,1)} async-done(((bf16[128,26,256]{2,1,0:T(8,128)(2,1)}), bf16[128,26,256]{2,1,0:T(8,128)(2,1)}, u32[]{:S(2)}, u32[]{:S(2)}) %all-to-all-start.5) | async-done | bytes 1703968 | tf_op jit(solution)/shard_map/all_to_all | solution.py:318
  391.5 2.0 reduce_sum.117
  393.5 1.6 broadcast_in_dim.37
  395.1 5.6 %all-to-all-start.6 = ((bf16[128,26,256]{2,1,0:T(8,128)(2,1)}), bf16[128,26,256]{2,1,0:T(8,128)(2,1)}, u32[]{:S(2)}, u32[]{:S(2)}) async-start(bf16[128,26,256]{2,1,0:T(8,128)(2,1)} %broadcast_in_dim.37), calls=%async_computation.6 | async-start | bytes 4194304 | tf_op jit(solution)/shard_map/all_to_all | solution.py:318
  400.7 1.5 convolution_add_fusion.1
  402.3 0.4 convolution_add_fusion
  402.6 1.0 copy-done.12
  403.7 0.8 broadcast_select_fusion
  404.4 1.4 collective-permute-start.3
  405.9 0.4 fusion.6
  406.2 0.3 convolution_add_fusion.5
  406.6 25.0 %collective-permute-done.3 = f32[32,256]{1,0:T(8,128)S(1)} collective-permute-done((f32[32,256]{1,0:T(8,128)S(1)}, f32[32,256]{1,0:T(8,128)S(1)}, u32[]{:S(2)}, u32[]{:S(2)}) %collective-permute-start.3) | collective-permute-done | bytes 32800 | tf_op jit(solution)/shard_map/ppermute | solution.py:310
  431.6 1.3 fusion.3
  432.8 2.5 reshape.310
  435.4 1.2 multiply_reduce_fusion
  436.6 0.7 multiply_reduce_fusion.1
  440.7 1.6 slice_divide_fusion
  442.3 3.0 copy.74
  445.3 1.0 slice_divide_fusion.1
  446.3 1.8 copy.75
  448.1 1.8 copy.76
  449.9 1.8 copy.77
  (64 shorter events, 1.3 us)
Async XLA Ops:
  4.5 22.2 %all-to-all-start = ((s32[64,1,2]{2,1,0:T(1,128)}), s32[64,1,2]{2,1,0:T(1,128)S(1)}, u32[]{:S(2)}, u32[]{:S(2)}) async-start(s32[64,1,2]{2,1,0:T(1,128)} %copy.63), calls=%async_computation | async-start | bytes 65536 | tf_op jit(solution)/shard_map/all_to_all | solution.py:318
  17.2 9.7 %collective-permute-start = (bf16[32,256]{1,0:T(8,128)(2,1)S(1)}, bf16[32,256]{1,0:T(8,128)(2,1)S(1)}, u32[]{:S(2)}, u32[]{:S(2)}) collective-permute-start(bf16[32,256]{1,0:T(8,128)(2,1)S(1)} %get-tuple-element.74), channel_id=1, source_target_pairs={{0,2},{2,4},{4,6},{6,8},{8,10},{10,12},{12,14},{14,16},{16,18},{18... | collective-permute-start | bytes 49160 | tf_op jit(solution)/shard_map/ppermute | solution.py:310
  18.2 8.8 %collective-permute-start.1 = (bf16[32,256]{1,0:T(8,128)(2,1)S(1)}, bf16[32,256]{1,0:T(8,128)(2,1)S(1)}, u32[]{:S(2)}, u32[]{:S(2)}) collective-permute-start(bf16[32,256]{1,0:T(8,128)(2,1)S(1)} %get-tuple-element.75), channel_id=1, source_target_pairs={{0,126},{2,0},{4,2},{6,4},{8,6},{10,8},{12,10},{14,12},{16,14},{18... | collective-permute-start | bytes 49160 | tf_op jit(solution)/shard_map/ppermute | solution.py:310
  28.3 1.3 copy-start.5
  45.1 55.8 %copy-start = (bf16[64,128,256]{2,1,0:T(8,128)(2,1)}, bf16[64,128,256]{2,1,0:T(8,128)(2,1)S(1)}, u32[]{:S(2)}) copy-start(bf16[64,128,256]{2,1,0:T(8,128)(2,1)S(1)} %get-tuple-element.21) | copy-start | bytes 12582916
  45.1 55.8 %copy-start.4 = (bf16[3,1088,256]{2,1,0:T(8,128)(2,1)}, bf16[3,1088,256]{2,1,0:T(8,128)(2,1)S(1)}, u32[]{:S(2)}) copy-start(bf16[3,1088,256]{2,1,0:T(8,128)(2,1)S(1)} %get-tuple-element.30.shifts_ref) | copy-start | bytes 5013508
  100.9 11.4 %copy-start.13 = (bf16[256,256]{1,0:T(8,128)(2,1)S(1)}, bf16[256,256]{1,0:T(8,128)(2,1)}, u32[]{:S(2)}) copy-start(bf16[256,256]{1,0:T(8,128)(2,1)} %param.19) | copy-start | bytes 393220
  100.9 11.6 %copy-start.14 = (bf16[256,256]{1,0:T(8,128)(2,1)S(1)}, bf16[256,256]{1,0:T(8,128)(2,1)}, u32[]{:S(2)}) copy-start(bf16[256,256]{1,0:T(8,128)(2,1)} %param.20) | copy-start | bytes 393220
  101.0 11.7 %copy-start.7 = (bf16[256,256]{1,0:T(8,128)(2,1)S(1)}, bf16[256,256]{1,0:T(8,128)(2,1)}, u32[]{:S(2)}) copy-start(bf16[256,256]{1,0:T(8,128)(2,1)} %wq.3) | copy-start | bytes 393220
  101.0 11.8 %copy-start.8 = (bf16[256,256]{1,0:T(8,128)(2,1)S(1)}, bf16[256,256]{1,0:T(8,128)(2,1)}, u32[]{:S(2)}) copy-start(bf16[256,256]{1,0:T(8,128)(2,1)} %wo.3) | copy-start | bytes 393220
  101.0 83.6 %all-to-all-start.1 = ((bf16[64,128,256]{2,1,0:T(8,128)(2,1)}), bf16[64,128,256]{2,1,0:T(8,128)(2,1)}, u32[]{:S(2)}, u32[]{:S(2)}) async-start(bf16[64,128,256]{2,1,0:T(8,128)(2,1)} %copy-done), calls=%async_computation.1 | async-start | bytes 8388608 | tf_op jit(solution)/shard_map/all_to_all | solution.py:318
  112.4 0.7 copy-start.15
  112.4 0.7 copy-start.16
  113.9 2.2 copy-start.1
  182.6 2.0 copy-start.2
  184.6 1.1 copy-start.9
  185.6 84.0 %all-to-all-start.4 = ((bf16[64,256,128]{2,1,0:T(8,128)(2,1)}), bf16[64,256,128]{2,1,0:T(8,128)(2,1)}, u32[]{:S(2)}, u32[]{:S(2)}) async-start(bf16[64,256,128]{2,1,0:T(8,128)(2,1)} %copy-done.2), calls=%async_computation.4 | async-start | bytes 8388608 | tf_op jit(solution)/shard_map/all_to_all | solution.py:318
  199.2 1.2 copy-start.10
  267.7 1.9 copy-start.3
  269.6 62.2 %all-to-all-start.3 = ((bf16[64,256,128]{2,1,0:T(8,128)(2,1)}), bf16[64,256,128]{2,1,0:T(8,128)(2,1)}, u32[]{:S(2)}, u32[]{:S(2)}) async-start(bf16[64,256,128]{2,1,0:T(8,128)(2,1)} %copy-done.3), calls=%async_computation.3 | async-start | bytes 8388608 | tf_op jit(solution)/shard_map/all_to_all | solution.py:318
  343.9 17.6 %copy-start.6 = (bf16[3,3,256,256]{3,2,1,0:T(8,128)(2,1)S(1)}, bf16[3,3,256,256]{3,2,1,0:T(8,128)(2,1)}, u32[]{:S(2)}) copy-start(bf16[3,3,256,256]{3,2,1,0:T(8,128)(2,1)} %param.22) | copy-start | bytes 3538948
  343.9 47.6 %all-to-all-start.5 = ((bf16[128,26,256]{2,1,0:T(8,128)(2,1)}), bf16[128,26,256]{2,1,0:T(8,128)(2,1)}, u32[]{:S(2)}, u32[]{:S(2)}) async-start(bf16[128,26,256]{2,1,0:T(8,128)(2,1)} %all_to_all.33), calls=%async_computation.5 | async-start | bytes 4194304 | tf_op jit(solution)/shard_map/all_to_all | solution.py:318
  362.6 1.0 copy-start.11
  364.4 42.2 %collective-permute-start.2 = (f32[32,256]{1,0:T(8,128)S(1)}, f32[32,256]{1,0:T(8,128)S(1)}, u32[]{:S(2)}, u32[]{:S(2)}) collective-permute-start(f32[32,256]{1,0:T(8,128)S(1)} %broadcast_select_fusion.1), channel_id=1, source_target_pairs={{0,126},{2,0},{4,2},{6,4},{8,6},{10,8},{12,10},{14,12},{16,14},{18... | collective-permute-start | bytes 98312 | tf_op jit(solution)/shard_map/ppermute | solution.py:310
  395.1 37.7 %all-to-all-start.6 = ((bf16[128,26,256]{2,1,0:T(8,128)(2,1)}), bf16[128,26,256]{2,1,0:T(8,128)(2,1)}, u32[]{:S(2)}, u32[]{:S(2)}) async-start(bf16[128,26,256]{2,1,0:T(8,128)(2,1)} %broadcast_in_dim.37), calls=%async_computation.6 | async-start | bytes 4194304 | tf_op jit(solution)/shard_map/all_to_all | solution.py:318
  402.6 1.0 copy-start.12
  404.4 27.1 %collective-permute-start.3 = (f32[32,256]{1,0:T(8,128)S(1)}, f32[32,256]{1,0:T(8,128)S(1)}, u32[]{:S(2)}, u32[]{:S(2)}) collective-permute-start(f32[32,256]{1,0:T(8,128)S(1)} %broadcast_select_fusion), channel_id=1, source_target_pairs={{0,2},{2,4},{4,6},{6,8},{8,10},{10,12},{12,14},{14,16},{16,18},{18... | collective-permute-start | bytes 98312 | tf_op jit(solution)/shard_map/ppermute | solution.py:310
  406.6 25.0 %slice-start = ((f32[32,32,256]{2,1,0:T(8,128)}), f32[31,32,256]{2,1,0:T(8,128)S(1)}, s32[]{:S(2)}) async-start(f32[32,32,256]{2,1,0:T(8,128)} %copy-done.11), calls=%async_computation.7 | async-start | bytes 2031616 | tf_op jit(solution)/shard_map/slice | solution.py:408
  406.6 25.0 %slice-start.1 = ((f32[32,32,256]{2,1,0:T(8,128)}), f32[31,32,256]{2,1,0:T(8,128)S(1)}, s32[]{:S(2)}) async-start(f32[32,32,256]{2,1,0:T(8,128)} %copy-done.12), calls=%async_computation.8 | async-start | bytes 2031616 | tf_op jit(solution)/shard_map/slice | solution.py:409

commit v2 on v1

--- a/solution.py
+++ b/solution.py
@@ -20,6 +20,7 @@
 SCALE = 1.0 / math.sqrt(HD)
 EXP2_SCALE = SCALE * math.log2(math.e)
 STEP = 8
+AHEAD = 2
 
 f32 = jnp.float32
 bf16 = jnp.bfloat16
@@ -87,15 +88,15 @@
             pl.BlockSpec(memory_space=pltpu.VMEM),
         ],
         out_specs=(
-            pl.BlockSpec(memory_space=pl.ANY),
-            pl.BlockSpec(memory_space=pl.ANY),
+            pl.BlockSpec(memory_space=pltpu.HBM),
+            pl.BlockSpec(memory_space=pltpu.HBM),
             pl.BlockSpec(memory_space=pltpu.VMEM),
         ),
         scratch_shapes=[
             pltpu.VMEM((CELLS, D), bf16),
             pltpu.SemaphoreType.DMA((2,)),
         ],
-        compiler_params=pltpu.CompilerParams(vmem_limit_bytes=40 * 1024 * 1024),
+        compiler_params=pltpu.CompilerParams(vmem_limit_bytes=60 * 1024 * 1024),
         cost_estimate=pl.CostEstimate(
             flops=2 * 9 * CELLS * D * D, bytes_accessed=20_000_000, transcendentals=0
         ),
@@ -103,89 +104,174 @@
     )(req, rimmed, w_conv)
 
 
-def attend_kernel(
-    meta, h_ref, x_ref, c_ref, wq, wq_t, wkv, wkv_t, wo, wo_t, grads_in, *rest
-):
-    out_ref, tgrad_ref, hgrad_ref, grads_ref = rest[-4:]
-    i = pl.program_id(0)
-
-    @pl.when(i == 0)
-    def _():
-        grads_ref[...] = grads_in[...]
-
-    @pl.when(i < meta[3, 0])
-    def _():
-        live = meta[2, i]
-        h = h_ref[0]
-        x = x_ref[0]
-        row = lax.broadcasted_iota(jnp.int32, (BT, D), 0)
-        cot = jnp.where(row < live, c_ref[0].astype(f32), 0.0).astype(bf16)
+def attend_kernel(meta, wq, wq_t, wkv, wkv_t, wo, wo_t, grads_in, slots, xs, cots, *rest):
+    outs, tgrads, hgrads, grads_ref, hbuf, xbuf, cbuf, obuf, tbuf, gbuf, in_sems, out_sems = rest[-12:]
+    count = meta[3, 0]
+    steps = (count + 1) // 2
+
+    def loads(i, slot):
+        copies = []
+        for u in range(2):
+            k = jnp.minimum(2 * i + u, count - 1)
+            block, tile = meta[0, k], meta[1, k]
+            rows = pl.ds(u * BT, BT)
+            copies += [
+                pltpu.make_async_copy(slots.at[tile], hbuf.at[slot, rows], in_sems.at[slot, 3 * u]),
+                pltpu.make_async_copy(xs.at[block], xbuf.at[slot, rows], in_sems.at[slot, 3 * u + 1]),
+                pltpu.make_async_copy(cots.at[block], cbuf.at[slot, rows], in_sems.at[slot, 3 * u + 2]),
+            ]
+        return copies
+
+    def stores(i, slot, u):
+        k = jnp.minimum(2 * i + u, count - 1)
+        block, tile = meta[0, k], meta[1, k]
+        rows = pl.ds(u * BT, BT)
+        return [
+            pltpu.make_async_copy(gbuf.at[slot, u], hgrads.at[tile], out_sems.at[slot, 3 * u]),
+            pltpu.make_async_copy(obuf.at[slot, rows], outs.at[block], out_sems.at[slot, 3 * u + 1]),
+            pltpu.make_async_copy(tbuf.at[slot, rows], tgrads.at[block], out_sems.at[slot, 3 * u + 2]),
+        ]
+
+    def start_stores(i, slot):
+        for c in stores(i, slot, 0):
+            c.start()
+
+        @pl.when(2 * i + 1 < count)
+        def _():
+            for c in stores(i, slot, 1):
+                c.start()
+
+    def wait_stores(i, slot):
+        for c in stores(i, slot, 0):
+            c.wait()
+
+        @pl.when(2 * i + 1 < count)
+        def _():
+            for c in stores(i, slot, 1):
+                c.wait()
+
+    for c in loads(0, 0):
+        c.start()
+    grads_ref[...] = grads_in[...]
+    zero = jnp.zeros((HD, BT), bf16)
+    none = jnp.zeros((2 * HD, 2 * BT), bf16)
+
+    def paired(t, p):
+        first = t[2 * HD * p : 2 * HD * p + HD]
+        second = t[2 * HD * p + HD : 2 * HD * p + 2 * HD]
+        return jnp.concatenate(
+            [
+                jnp.concatenate([first, zero], axis=1),
+                jnp.concatenate([zero, second], axis=1),
+            ],
+            axis=0,
+        )
+
+    def deep(pair, p):
+        return jnp.concatenate([pair, none] if p % 2 == 0 else [none, pair], axis=0)
+
+    @pl.loop(0, steps)
+    def _(i):
+        slot = lax.rem(i, 2)
+
+        @pl.when(i + 1 < steps)
+        def _():
+            for c in loads(i + 1, 1 - slot):
+                c.start()
+
+        for c in loads(i, slot):
+            c.wait()
+
+        @pl.when(i >= 2)
+        def _():
+            wait_stores(i - 2, slot)
+
+        live0 = meta[2, 2 * i]
+        live1 = jnp.where(2 * i + 1 < count, meta[2, jnp.minimum(2 * i + 1, count - 1)], 0)
+        h = hbuf[slot]
+        x = xbuf[slot]
+        row = lax.broadcasted_iota(jnp.int32, (2 * BT, D), 0)
+        lane = lax.broadcasted_iota(jnp.int32, (D, 2 * BT), 1)
+        row_live = row < jnp.where(row < BT, live0, live1 + BT)
+        lane_live = lane < jnp.where(lane < BT, live0, live1 + BT)
+        cot = jnp.where(row_live, cbuf[slot].astype(f32), 0.0).astype(bf16)
         kv = mm(h, wkv[...]).astype(bf16)
         kv_t = mm_nt(wkv_t[...], h).astype(bf16)
         q_t = mm_nt(wq_t[...], x).astype(bf16)
         d_t = mm_nt(wo[...], cot).astype(bf16)
-        zero = jnp.zeros((HD, BT), bf16)
-        none = jnp.zeros((2 * HD, 2 * BT), bf16)
-
-        def paired(t, p):
-            first = t[2 * HD * p : 2 * HD * p + HD]
-            second = t[2 * HD * p + HD : 2 * HD * p + 2 * HD]
-            return jnp.concatenate(
-                [
-                    jnp.concatenate([first, zero], axis=1),
-                    jnp.concatenate([zero, second], axis=1),
-                ],
-                axis=0,
-            )
-
-        def deep(pair, p):
-            return jnp.concatenate([pair, none] if p % 2 == 0 else [none, pair], axis=0)
-
-        att_rows, qg_rows, kg_rows, vg_rows = [], [], [], []
-        for p in range(HEADS // 2):
-            lanes = slice(128 * (p // 2), 128 * (p // 2) + 128)
-            feats = slice(2 * HD * p, 2 * HD * p + 2 * HD)
-            q2 = paired(q_t, p)
-            d2 = paired(d_t, p)
-            scores = mm(kv[:, lanes], deep(q2, p))
+        att_rows, qg_rows, kg_rows, vg_rows = [[], []], [[], []], [[], []], [[], []]
+        def first(p, u):
+            rows = slice(u * BT, u * BT + BT)
+            half = 128 * (p // 2)
+            q2 = paired(q_t[:, rows], p)
+            d2 = paired(d_t[:, rows], p)
+            scores = mm(kv[rows, half : half + 128], deep(q2, p))
+            wg = mm(kv[rows, D + half : D + half + 128], deep(d2, p))
+            return q2, d2, scores, wg
+
+        def second(q2, d2, scores, wg):
             top = jnp.max(scores, axis=0, keepdims=True)
             e = jnp.exp2((scores - top) * EXP2_SCALE)
-            w = (e * (1.0 / jnp.sum(e, axis=0, keepdims=True))).astype(bf16)
-            wf = w.astype(f32)
-            wg = mm(kv[:, D + lanes.start : D + lanes.stop], deep(d2, p))
+            wf = e * (1.0 / jnp.sum(e, axis=0, keepdims=True))
             mean = jnp.sum(wf * wg, axis=0, keepdims=True)
             sg = (wf * (wg - mean)).astype(bf16)
-            att = mm(kv_t[D + feats.start : D + feats.stop], w)
-            att_rows += [att[:HD, :BT], att[HD:, BT:]]
-            qg = mm(kv_t[feats], sg)
-            qg_rows += [qg[:HD, :BT], qg[HD:, BT:]]
-            kg_rows.append(mm_nt(q2, sg) * SCALE)
-            vg_rows.append(mm_nt(d2, w))
-        att_t = jnp.concatenate(att_rows, axis=0).astype(bf16)
-        qg_t = (jnp.concatenate(qg_rows, axis=0) * SCALE).astype(bf16)
-        kvg_t = jnp.concatenate(kg_rows + vg_rows, axis=0).astype(bf16)
-        lane = lax.broadcasted_iota(jnp.int32, (D, BT), 1)
-        mixed = jnp.where(lane < live, mm(wo_t[...], att_t), 0.0)
-        out_ref[0] = mixed.T.astype(bf16)
-        tgrad_ref[0] = mm(wq[...], qg_t).T.astype(bf16)
-        hgrad_ref[0] = mm(wkv[...], kvg_t).astype(bf16)
+            return q2, d2, wf.astype(bf16), sg
+
+        def third(p, u, q2, d2, w, sg):
+            rows = slice(u * BT, u * BT + BT)
+            feats = slice(2 * HD * p, 2 * HD * p + 2 * HD)
+            v_feats = slice(D + 2 * HD * p, D + 2 * HD * p + 2 * HD)
+            att = mm(kv_t[v_feats, rows], w)
+            att_rows[u] += [att[:HD, :BT], att[HD:, BT:]]
+            qg = mm(kv_t[feats, rows], sg)
+            qg_rows[u] += [qg[:HD, :BT], qg[HD:, BT:]]
+            kg_rows[u].append(mm_nt(q2, sg) * SCALE)
+            vg_rows[u].append(mm_nt(d2, w))
+
+        units = [(p, u) for p in range(HEADS // 2) for u in range(2)]
+        ready, soft = {}, {}
+        for k in range(len(units) + AHEAD + 1):
+            if k < len(units):
+                ready[k] = first(*units[k])
+            j = k - AHEAD
+            if 0 <= j < len(units):
+                soft[j] = second(*ready.pop(j))
+            if 0 <= j - 1 < len(units):
+                third(*units[j - 1], *soft.pop(j - 1))
+
+        def joined(rows):
+            return jnp.concatenate([jnp.concatenate(r, axis=0) for r in rows], axis=1)
+
+        att_t = joined(att_rows).astype(bf16)
+        qg_t = (joined(qg_rows) * SCALE).astype(bf16)
+        kvg_t = joined([kg_rows[u] + vg_rows[u] for u in range(2)]).astype(bf16)
+        mixed = jnp.where(lane_live, mm(wo_t[...], att_t), 0.0)
+        obuf[slot] = mixed.T.astype(bf16)
+        tbuf[slot] = mm(wq[...], qg_t).T.astype(bf16)
+        back = mm(wkv[...], kvg_t).astype(bf16)
+        gbuf[slot, 0] = back[:, :BT]
+        gbuf[slot, 1] = back[:, BT:]
         grads_ref[0:256] += mm(qg_t, x)
         grads_ref[256:768] += mm(kvg_t, h)
         grads_ref[768:1024] += mm(att_t, cot)
+        start_stores(i, slot)
+
+    @pl.when(steps >= 2)
+    def _():
+        wait_stores(steps - 2, lax.rem(steps, 2))
+
+    wait_stores(steps - 1, lax.rem(steps - 1, 2))
 
 
 def attend(meta, slots, x, cot, weights, grads, kept):
     nblocks = x.shape[0]
     count = slots.shape[0]
-    by_tile = lambda i, m: (m[1, i], 0, 0)
-    by_block = lambda i, m: (m[0, i], 0, 0)
-    rows = pl.BlockSpec((1, BT, D), by_block)
-    in_specs = [pl.BlockSpec((1, KEYS, D), by_tile), rows, rows]
-    in_specs += [whole(w.shape) for w in weights] + [whole((4 * D, D))]
-    in_specs += [pl.BlockSpec(memory_space=pl.ANY)] * len(kept)
-    args = [meta, slots, x, cot, *weights, grads, *kept]
+    vmem = pl.BlockSpec(memory_space=pltpu.VMEM)
+    remote = pl.BlockSpec(memory_space=pltpu.HBM)
+    args = [meta, *weights, grads, slots, x, cot, *kept]
     first_kept = len(args) - len(kept)
     token_shape = jax.ShapeDtypeStruct((nblocks, BT, D), bf16)
+    pair = pltpu.VMEM((2, 2 * BT, D), bf16)
     return pl.pallas_call(
         attend_kernel,
         out_shape=(
@@ -194,21 +280,18 @@
             jax.ShapeDtypeStruct((count, D, KEYS), bf16),
             jax.ShapeDtypeStruct((4 * D, D), f32),
         ),
-        grid_spec=pltpu.PrefetchScalarGridSpec(
-            num_scalar_prefetch=1,
-            grid=(nblocks,),
-            in_specs=in_specs,
-            out_specs=(
-                rows,
-                rows,
-                pl.BlockSpec((1, D, KEYS), by_tile),
-                whole((4 * D, D)),
-            ),
-        ),
+        in_specs=[pl.BlockSpec(memory_space=pltpu.SMEM)]
+        + [vmem] * (len(weights) + 1)
+        + [remote] * (3 + len(kept)),
+        out_specs=(remote, remote, remote, vmem),
+        scratch_shapes=[pair] * 5
+        + [
+            pltpu.VMEM((2, 2, D, KEYS), bf16),
+            pltpu.SemaphoreType.DMA((2, 6)),
+            pltpu.SemaphoreType.DMA((2, 6)),
+        ],
         input_output_aliases={first_kept + j: j for j in range(len(kept))},
-        compiler_params=pltpu.CompilerParams(
-            dimension_semantics=("arbitrary",), vmem_limit_bytes=40 * 1024 * 1024
-        ),
+        compiler_params=pltpu.CompilerParams(vmem_limit_bytes=60 * 1024 * 1024),
         cost_estimate=pl.CostEstimate(
             flops=nblocks * 400_000_000, bytes_accessed=nblocks * 400_000, transcendentals=0
         ),
@@ -247,6 +330,8 @@
     @pl.when(i == pl.num_programs(0) - 1)
     def _():
         sums_ref[0 : 4 * D] = grads_ref[...].astype(bf16)
+        if sums_ref.shape[0] > 13 * D:
+            sums_ref[13 * D :] = jnp.zeros((sums_ref.shape[0] - 13 * D, D), bf16)
         for s in range(SUB):
             part = acc_ref[s * D : (s + 1) * D, :]
             hgrad_ref[s * KEYS : (s + 1) * KEYS, :] = part.T
@@ -273,7 +358,7 @@
         grid=(count // STEP,),
         in_specs=slot_specs(count),
         out_specs=whole((SUB * D, KEYS)),
-        compiler_params=pltpu.CompilerParams(vmem_limit_bytes=40 * 1024 * 1024),
+        compiler_params=pltpu.CompilerParams(vmem_limit_bytes=60 * 1024 * 1024),
         cost_estimate=pl.CostEstimate(
             flops=count * D * KEYS, bytes_accessed=count * D * KEYS * 2, transcendentals=0
         ),
@@ -281,28 +366,63 @@
     )(req, slots)
 
 
-def finish(req, slots, acc, shifts, grads):
+def finish(req, slots, acc, shifts, grads, rows):
     count = slots.shape[0]
     return pl.pallas_call(
         finish_kernel,
         out_shape=(
             jax.ShapeDtypeStruct((CELLS, D), f32),
-            jax.ShapeDtypeStruct((13 * D, D), bf16),
+            jax.ShapeDtypeStruct((rows, D), bf16),
         ),
         grid=(count // STEP,),
         in_specs=slot_specs(count)
         + [whole(acc.shape), whole(shifts.shape), whole(grads.shape)],
-        out_specs=(whole((CELLS, D)), whole((13 * D, D))),
+        out_specs=(whole((CELLS, D)), whole((rows, D))),
         scratch_shapes=[
             pltpu.VMEM((SUB * D, KEYS), f32),
             pltpu.VMEM((D, CELLS), bf16),
         ],
-        compiler_params=pltpu.CompilerParams(vmem_limit_bytes=50 * 1024 * 1024),
+        compiler_params=pltpu.CompilerParams(vmem_limit_bytes=60 * 1024 * 1024),
         cost_estimate=pl.CostEstimate(
             flops=2 * 9 * CELLS * D * D, bytes_accessed=12_000_000, transcendentals=0
         ),
         name="finish",
     )(req, slots, acc, shifts, grads)
+
+
+def normalize_kernel(sums_ref, query_ref, key_ref, value_ref, out_ref, conv_ref):
+    def part(k):
+        return sums_ref[k * D : (k + 1) * D, :].astype(f32)
+
+    def squares(k):
+        item = part(k)
+        return jnp.sum(jnp.sum(item * item, axis=0, keepdims=True), axis=1, keepdims=True)
+
+    def factor(total, size):
+        return 1.0 / jnp.sqrt(total / size + EPSILON)
+
+    for k, ref in enumerate((query_ref, key_ref, value_ref)):
+        ref[...] = (part(k) * factor(squares(k), D * D)).T
+    out_ref[...] = part(3) * factor(squares(3), D * D)
+    total = squares(4)
+    for k in range(5, 13):
+        total = total + squares(k)
+    scale = factor(total, 9 * D * D)
+    for k in range(9):
+        conv_ref[k] = (part(4 + k) * scale).T
+
+
+def normalize(sums):
+    square = jax.ShapeDtypeStruct((D, D), f32)
+    return pl.pallas_call(
+        normalize_kernel,
+        out_shape=(square,) * 4 + (jax.ShapeDtypeStruct((9, D, D), f32),),
+        in_specs=[pl.BlockSpec(memory_space=pltpu.VMEM)],
+        out_specs=(pl.BlockSpec(memory_space=pltpu.VMEM),) * 5,
+        compiler_params=pltpu.CompilerParams(vmem_limit_bytes=60 * 1024 * 1024),
+        cost_estimate=pl.CostEstimate(flops=4_000_000, bytes_accessed=6_000_000, transcendentals=0),
+        name="normalize",
+    )(sums)
 
 
 def ring(value, by):
@@ -386,12 +506,13 @@
     )
     ret_b = exchange(back_b)
     acc = gather_slots(req, ret_a)
-    hidden_grad, sums = finish(req, ret_b, acc, shifts, grads)
+    each = -(-13 * D // (16 * ndev)) * 16
+    hidden_grad, sums = finish(req, ret_b, acc, shifts, grads, ndev * each)
 
     parts = exchange(sums, ("tile", "win")).reshape(ndev, -1, D)
     share = jnp.sum(parts.astype(f32), axis=0).astype(bf16)
     spread = jnp.broadcast_to(share[None], (ndev,) + share.shape).reshape(-1, D)
-    total = exchange(spread, ("tile", "win")).astype(f32).reshape(13, D, D)
+    updates = normalize(exchange(spread, ("tile", "win")))
 
     hidden_back = hidden_grad.astype(bf16).reshape(RY, RX, D)
     padded = jnp.pad(hidden_back, ((0, 0), (1, 1), (0, 0)))
@@ -409,23 +530,12 @@
     field_grad = field_grad + jnp.concatenate([from_above[None], taps[2][:-1]], axis=0)
     grid_grad = field_grad.astype(bf16)[None]
 
-    def scaled(grad):
-        return grad / jnp.sqrt(jnp.mean(grad * grad) + EPSILON)
-
-    upd_query = scaled(total[0]).T
-    upd_key = scaled(total[1]).T
-    upd_value = scaled(total[2]).T
-    upd_out = scaled(total[3])
-    upd_conv = scaled(total[4:]).transpose(0, 2, 1).reshape(3, 3, D, D)
     return (
         token_out.reshape(1, -1, D),
         token_grad.reshape(1, -1, D),
         grid_grad,
-        upd_query,
-        upd_key,
-        upd_value,
-        upd_out,
-        upd_conv,
+        *updates[:4],
+        updates[4].reshape(3, 3, D, D),
     )
 
 

time: 451 us -> 395 us (0.88)
  Pallas kernels: 163 us -> 92.9 us
  waiting for transfers between devices: 86.8 us -> 113 us
  local copies, waits for them, and re-layouts: 31.8 us -> 12.4 us
  matrix products: 6.21 us -> 12.1 us
  starting transfers between devices: 89.5 us -> 95.3 us
    pallas_call x2, Pallas kernels: 134 us -> 65.2 us  [attend(): pl.pallas_call(attend_kernel, out_shape=(token_shape, token_shape, jax.Sh...]
    all_to_all x6, waiting for transfers between devices: 61.8 us -> 91.4 us  [exchange(): return lax.all_to_all(value, axes, split_axis=0, concat_axis=0, tiled=True)]
    unnamed x41 -> x24, local copies, waits for them, and re-layouts: 17.4 us -> 5.05 us
    pallas_call x1, Pallas kernels: 15.6 us -> 8.08 us  [hidden_sends(): pl.pallas_call(hidden_kernel, out_shape=(slots, slots, jax.ShapeDtypeStru...]
    dot_general x9, matrix products: 6.21 us -> 12.1 us  [mm_nt(): lax.dot_general(a, b, (((1,), (1,)), ((), ())), preferred_element_type=f32)]
    all_to_all x6, starting transfers between devices: 73.4 us -> 79.2 us  [exchange(): return lax.all_to_all(value, axes, split_axis=0, concat_axis=0, tiled=True)]
  transfers between devices with their start and end apart: 10 -> 10, of which waited for: 3 -> 5; matrix products, arithmetic and copies ran while one was open for 3% -> 6% of each run, Pallas kernels for 31% -> 18%
where the time goes in v2:
time: 395 us; the launch traced here: 394 us
  waiting for transfers between devices  113 us (29%)
  starting transfers between devices  95.3 us (24%)
  Pallas kernels  92.9 us (24%)
  blocking collectives  55.4 us (14%)
  local copies, waits for them, and re-layouts  12.4 us (3%)
  matrix products  12.1 us (3%)
  other arithmetic  10.2 us (3%)
    all_to_all x6, waiting for transfers between devices, exchange(): return lax.all_to_all(value, axes, split_axis=0, concat_axis=0, tiled=True)  91.4 us
    all_to_all x6, starting transfers between devices, exchange(): return lax.all_to_all(value, axes, split_axis=0, concat_axis=0, tiled=True)  79.2 us
    pallas_call x2, Pallas kernels, attend(): pl.pallas_call(attend_kernel, out_shape=(token_shape, token_shape, jax.Sh...  65.2 us
    all_to_all x1, blocking collectives, exchange(): return lax.all_to_all(value, axes, split_axis=0, concat_axis=0, tiled=True)  55.4 us
    ppermute x4, waiting for transfers between devices, ring(): lax.ppermute(value, 'tile', [(i, (i + by) % length) for i in range(length)])  21.7 us
    ppermute x4, starting transfers between devices, ring(): lax.ppermute(value, 'tile', [(i, (i + by) % length) for i in range(length)])  16 us
    dot_general x9, matrix products, mm_nt(): lax.dot_general(a, b, (((1,), (1,)), ((), ())), preferred_element_type=f32)  12.1 us
    pallas_call x1, Pallas kernels, finish(): pl.pallas_call(finish_kernel, out_shape=(jax.ShapeDtypeStruct((CELLS, D),...  9.33 us
  transfers between devices with their start and end apart: 10, of which 5 were waited for; matrix products, arithmetic and copies ran while one was open for 6% of the time, Pallas kernels for 18%

profile of v2, /device:TPU:1, one launch (start us, length us, event | category | flops | bytes accessed | tf_op | source)
XLA Modules:
  0.0 393.7 jit_solution(6578196755003746716)
XLA Ops:
  0.6 0.9 convert_reduce_fusion.1
  1.5 0.7 iota_compare_fusion
  2.3 0.7 fusion.27
  3.0 0.7 and_select_fusion
  3.7 0.1 select_reduce_fusion
  3.8 0.7 copy.46
  4.5 12.0 %all-to-all-start = ((s32[64,1,2]{2,1,0:T(1,128)}), s32[64,1,2]{2,1,0:T(1,128)S(1)}, u32[]{:S(2)}, u32[]{:S(2)}) async-start(s32[64,1,2]{2,1,0:T(1,128)} %copy.46), calls=%async_computation | async-start | bytes 65536 | tf_op jit(solution)/shard_map/all_to_all | solution.py:438
  16.5 0.7 slice_bitcast_fusion.3
  17.2 1.0 collective-permute-start
  18.2 5.9 %collective-permute-start.1 = (bf16[32,256]{1,0:T(8,128)(2,1)S(1)}, bf16[32,256]{1,0:T(8,128)(2,1)S(1)}, u32[]{:S(2)}, u32[]{:S(2)}) collective-permute-start(bf16[32,256]{1,0:T(8,128)(2,1)S(1)} %get-tuple-element.45), channel_id=1, source_target_pairs={{0,126},{2,0},{4,2},{6,4},{8,6},{10,8},{12,10},{14,12},{16,14},{18... | collective-permute-start | bytes 49160 | tf_op jit(solution)/shard_map/ppermute | solution.py:430
  24.1 1.3 fusion.39
  26.8 0.1 copy.47
  26.8 0.7 copy.48.req_ref
  27.6 0.1 rev.13
  27.7 1.9 pad_maximum_fusion
  29.7 8.1 %conv_sends.1 = (bf16[64,128,256]{2,1,0:T(8,128)(2,1)}, bf16[64,128,256]{2,1,0:T(8,128)(2,1)}, bf16[3,1088,256]{2,1,0:T(8,128)(2,1)}) custom-call(s32[64,2]{1,0:T(8,128)} %copy.48.req_ref, bf16[1088,256]{1,0:T(8,128)(2,1)} %bitcast.114, bf16[9,256,256]{2,1,0:T(8,128)(2,1)} %bitcast.112), custom_call_target="tpu_custom_call" | custom-call | flops 1207959552 | bytes 20000000 | tf_op jit(solution)/shard_map/conv_sends/pallas_call | solution.py:82
  37.8 55.4 %all_to_all.45.slots = bf16[64,128,256]{2,1,0:T(8,128)(2,1)} all-to-all(bf16[64,128,256]{2,1,0:T(8,128)(2,1)} %get-tuple-element.26), channel_id=1, replica_groups=mesh['tile'=64,'win'=2] {'tile'}, dimensions={0} | all-to-all | bytes 8388608 | tf_op jit(solution)/shard_map/all_to_all | solution.py:438
  93.2 11.4 %all-to-all-start.2 = ((bf16[64,128,256]{2,1,0:T(8,128)(2,1)}), bf16[64,128,256]{2,1,0:T(8,128)(2,1)}, u32[]{:S(2)}, u32[]{:S(2)}) async-start(bf16[64,128,256]{2,1,0:T(8,128)(2,1)} %get-tuple-element.28), calls=%async_computation.2 | async-start | bytes 8388608 | tf_op jit(solution)/shard_map/all_to_all | solution.py:438
  104.6 0.1 copy.43
  104.7 0.1 copy.44
  104.8 0.8 copy.42
  105.6 0.8 copy.45
  106.3 0.7 fusion.38
  107.1 0.8 copy.50.wkv
  108.0 0.1 convert_reduce_fusion.2
  108.1 0.2 convert_reduce_fusion
  108.3 0.1 iota_minimum_fusion
  108.3 0.1 and_convert_fusion
  108.4 0.2 multiply_reduce_fusion
  108.7 0.6 fusion.30
  109.3 1.0 broadcast_in_dim.29.grads_in
  110.3 31.7 %attend.2 = (bf16[64,128,256]{2,1,0:T(8,128)(2,1)}, bf16[64,128,256]{2,1,0:T(8,128)(2,1)}, bf16[64,256,128]{2,1,0:T(8,128)(2,1)}, f32[1024,256]{1,0:T(8,128)}) custom-call(s32[4,64]{1,0:T(4,128)} %get-tuple-element.48.meta, bf16[256,256]{1,0:T(8,128)(2,1)} %wq.3, bf16[256,256]{1,0:T(8,128)(2,1)} %bitcast.115, bf16[256,512]{1,0:T(8,128)(2,1)} %copy.50.wkv, ...), custom_call_target="tpu_custom_call" | custom-call | flops 25600000000 | bytes 25600000 | tf_op jit(solution)/shard_map/attend/pallas_call | solution.py:275
  142.1 12.4 %all-to-all-done.2.slots = bf16[64,128,256]{2,1,0:T(8,128)(2,1)} async-done(((bf16[64,128,256]{2,1,0:T(8,128)(2,1)}), bf16[64,128,256]{2,1,0:T(8,128)(2,1)}, u32[]{:S(2)}, u32[]{:S(2)}) %all-to-all-start.2) | async-done | bytes 4194336 | tf_op jit(solution)/shard_map/all_to_all | solution.py:438
  154.5 17.7 %all-to-all-start.4 = ((bf16[64,256,128]{2,1,0:T(8,128)(2,1)}), bf16[64,256,128]{2,1,0:T(8,128)(2,1)}, u32[]{:S(2)}, u32[]{:S(2)}) async-start(bf16[64,256,128]{2,1,0:T(8,128)(2,1)} %get-tuple-element.34), calls=%async_computation.4 | async-start | bytes 8388608 | tf_op jit(solution)/shard_map/all_to_all | solution.py:438
  172.2 33.4 %attend.3 = (bf16[64,128,256]{2,1,0:T(8,128)(2,1)}, bf16[64,128,256]{2,1,0:T(8,128)(2,1)}, bf16[64,256,128]{2,1,0:T(8,128)(2,1)}, f32[1024,256]{1,0:T(8,128)}) custom-call(s32[4,64]{1,0:T(4,128)} %get-tuple-element.49.meta, bf16[256,256]{1,0:T(8,128)(2,1)} %wq.3, bf16[256,256]{1,0:T(8,128)(2,1)} %bitcast.116, ...), custom_call_target="tpu_custom_call", output_to_operand_aliasing={{0}: (11, {}), {1}: (12, {})} | custom-call | flops 25600000000 | bytes 25600000 | tf_op jit(solution)/shard_map/attend/pallas_call | solution.py:275
  205.6 18.0 %all-to-all-done.4.slots_ref = bf16[64,256,128]{2,1,0:T(8,128)(2,1)} async-done(((bf16[64,256,128]{2,1,0:T(8,128)(2,1)}), bf16[64,256,128]{2,1,0:T(8,128)(2,1)}, u32[]{:S(2)}, u32[]{:S(2)}) %all-to-all-start.4) | async-done | bytes 4194336 | tf_op jit(solution)/shard_map/all_to_all | solution.py:438
  223.6 17.4 %all-to-all-start.3 = ((bf16[64,256,128]{2,1,0:T(8,128)(2,1)}), bf16[64,256,128]{2,1,0:T(8,128)(2,1)}, u32[]{:S(2)}, u32[]{:S(2)}) async-start(bf16[64,256,128]{2,1,0:T(8,128)(2,1)} %get-tuple-element.33), calls=%async_computation.3 | async-start | bytes 8388608 | tf_op jit(solution)/shard_map/all_to_all | solution.py:438
  241.1 6.4 %gather_slots.1.acc_in = f32[2048,128]{1,0:T(8,128)} custom-call(s32[64,2]{1,0:T(8,128)} %copy.48.req_ref, bf16[64,256,128]{2,1,0:T(8,128)(2,1)} %all-to-all-done.4.slots_ref), custom_call_target="tpu_custom_call" | custom-call | flops 2097152 | bytes 4194304 | tf_op jit(solution)/shard_map/gather_slots/pallas_call | solution.py:355
  247.4 45.1 %all-to-all-done.3.slots_ref = bf16[64,256,128]{2,1,0:T(8,128)(2,1)} async-done(((bf16[64,256,128]{2,1,0:T(8,128)(2,1)}), bf16[64,256,128]{2,1,0:T(8,128)(2,1)}, u32[]{:S(2)}, u32[]{:S(2)}) %all-to-all-start.3) | async-done | bytes 4194336 | tf_op jit(solution)/shard_map/all_to_all | solution.py:438
  292.5 9.3 %finish.1 = (f32[1024,256]{1,0:T(8,128)}, bf16[4096,256]{1,0:T(8,128)(2,1)}) custom-call(s32[64,2]{1,0:T(8,128)} %copy.48.req_ref, bf16[64,256,128]{2,1,0:T(8,128)(2,1)} %all-to-all-done.3.slots_ref, f32[2048,128]{1,0:T(8,128)} %gather_slots.1.acc_in, bf16[3,1088,256]{2,1,0:T(8,128)(2,1)} %get-tuple-element.35.shifts_ref, ...), custom_call_target="tpu_custom_call" | custom-call | flops 1207959552 | bytes 12000000 | tf_op jit(solution)/shard_map/finish/pallas_call | solution.py:371
  301.8 16.2 %all-to-all-start.5 = ((bf16[128,32,256]{2,1,0:T(8,128)(2,1)}), bf16[128,32,256]{2,1,0:T(8,128)(2,1)S(1)}, u32[]{:S(2)}, u32[]{:S(2)}) async-start(bf16[128,32,256]{2,1,0:T(8,128)(2,1)} %bitcast.111), calls=%async_computation.5 | async-start | bytes 4194304 | tf_op jit(solution)/shard_map/all_to_all | solution.py:438
  318.0 1.3 convert_element_type.30
  319.3 1.3 fusion.5
  320.6 1.2 convolution_add_fusion.3
  321.8 1.3 convolution_add_fusion.2
  323.1 1.0 copy-done.1
  324.1 0.8 broadcast_select_fusion.1
  324.9 7.7 %collective-permute-start.2 = (f32[32,256]{1,0:T(8,128)S(1)}, f32[32,256]{1,0:T(8,128)S(1)}, u32[]{:S(2)}, u32[]{:S(2)}) collective-permute-start(f32[32,256]{1,0:T(8,128)S(1)} %broadcast_select_fusion.1), channel_id=1, source_target_pairs={{0,126},{2,0},{4,2},{6,4},{8,6},{10,8},{12,10},{14,12},{16,14},{18... | collective-permute-start | bytes 98312 | tf_op jit(solution)/shard_map/ppermute | solution.py:430
  332.6 15.8 %all-to-all-done.5 = bf16[128,32,256]{2,1,0:T(8,128)(2,1)S(1)} async-done(((bf16[128,32,256]{2,1,0:T(8,128)(2,1)}), bf16[128,32,256]{2,1,0:T(8,128)(2,1)S(1)}, u32[]{:S(2)}, u32[]{:S(2)}) %all-to-all-start.5) | async-done | bytes 2097184 | tf_op jit(solution)/shard_map/all_to_all | solution.py:438
  348.4 0.3 reduce_sum.72
  348.8 1.6 broadcast_in_dim.37
  350.3 4.6 %all-to-all-start.6 = ((bf16[128,32,256]{2,1,0:T(8,128)(2,1)}), bf16[128,32,256]{2,1,0:T(8,128)(2,1)S(1)}, u32[]{:S(2)}, u32[]{:S(2)}) async-start(bf16[128,32,256]{2,1,0:T(8,128)(2,1)} %broadcast_in_dim.37), calls=%async_computation.6 | async-start | bytes 4194304 | tf_op jit(solution)/shard_map/all_to_all | solution.py:438
  355.0 1.3 fusion.4
  356.2 1.2 convolution_add_fusion.1
  357.5 1.3 convolution_add_fusion
  358.7 1.0 copy-done.2
  359.8 0.8 broadcast_select_fusion
  360.6 1.4 collective-permute-start.3
  361.9 1.2 fusion.6
  363.2 1.2 convolution_add_fusion.5
  364.5 21.7 %collective-permute-done.3 = f32[32,256]{1,0:T(8,128)S(1)} collective-permute-done((f32[32,256]{1,0:T(8,128)S(1)}, f32[32,256]{1,0:T(8,128)S(1)}, u32[]{:S(2)}, u32[]{:S(2)}) %collective-permute-start.3) | collective-permute-done | bytes 32800 | tf_op jit(solution)/shard_map/ppermute | solution.py:430
  386.2 2.1 fusion.3
  388.3 1.3 copy-done
  389.7 4.0 %normalize.1 = (f32[256,256]{1,0:T(8,128)}, f32[256,256]{1,0:T(8,128)}, f32[256,256]{1,0:T(8,128)}, f32[256,256]{1,0:T(8,128)}, f32[9,256,256]{2,1,0:T(8,128)}) custom-call(bf16[4096,256]{1,0:T(8,128)(2,1)} %bitcast.109), custom_call_target="tpu_custom_call" | custom-call | flops 4000000 | bytes 6000000 | tf_op jit(solution)/shard_map/normalize/pallas_call | solution.py:417
  (41 shorter events, 0.3 us)
Async XLA Ops:
  4.5 22.2 %all-to-all-start = ((s32[64,1,2]{2,1,0:T(1,128)}), s32[64,1,2]{2,1,0:T(1,128)S(1)}, u32[]{:S(2)}, u32[]{:S(2)}) async-start(s32[64,1,2]{2,1,0:T(1,128)} %copy.46), calls=%async_computation | async-start | bytes 65536 | tf_op jit(solution)/shard_map/all_to_all | solution.py:438
  17.2 10.3 %collective-permute-start = (bf16[32,256]{1,0:T(8,128)(2,1)S(1)}, bf16[32,256]{1,0:T(8,128)(2,1)S(1)}, u32[]{:S(2)}, u32[]{:S(2)}) collective-permute-start(bf16[32,256]{1,0:T(8,128)(2,1)S(1)} %get-tuple-element.44), channel_id=1, source_target_pairs={{0,2},{2,4},{4,6},{6,8},{8,10},{10,12},{12,14},{14,16},{16,18},{18... | collective-permute-start | bytes 49160 | tf_op jit(solution)/shard_map/ppermute | solution.py:430
  18.2 9.4 %collective-permute-start.1 = (bf16[32,256]{1,0:T(8,128)(2,1)S(1)}, bf16[32,256]{1,0:T(8,128)(2,1)S(1)}, u32[]{:S(2)}, u32[]{:S(2)}) collective-permute-start(bf16[32,256]{1,0:T(8,128)(2,1)S(1)} %get-tuple-element.45), channel_id=1, source_target_pairs={{0,126},{2,0},{4,2},{6,4},{8,6},{10,8},{12,10},{14,12},{16,14},{18... | collective-permute-start | bytes 49160 | tf_op jit(solution)/shard_map/ppermute | solution.py:430
  93.2 11.4 %copy-start.4 = (bf16[256,256]{1,0:T(8,128)(2,1)S(1)}, bf16[256,256]{1,0:T(8,128)(2,1)}, u32[]{:S(2)}) copy-start(bf16[256,256]{1,0:T(8,128)(2,1)} %param.19) | copy-start | bytes 393220
  93.2 11.5 %copy-start.5 = (bf16[256,256]{1,0:T(8,128)(2,1)S(1)}, bf16[256,256]{1,0:T(8,128)(2,1)}, u32[]{:S(2)}) copy-start(bf16[256,256]{1,0:T(8,128)(2,1)} %param.20) | copy-start | bytes 393220
  93.2 11.7 %copy-start.6 = (bf16[256,256]{1,0:T(8,128)(2,1)S(1)}, bf16[256,256]{1,0:T(8,128)(2,1)}, u32[]{:S(2)}) copy-start(bf16[256,256]{1,0:T(8,128)(2,1)} %wq.3) | copy-start | bytes 393220
  93.2 12.4 %copy-start.7 = (bf16[256,256]{1,0:T(8,128)(2,1)S(1)}, bf16[256,256]{1,0:T(8,128)(2,1)}, u32[]{:S(2)}) copy-start(bf16[256,256]{1,0:T(8,128)(2,1)} %wo.3) | copy-start | bytes 393220
  93.2 61.4 %all-to-all-start.2 = ((bf16[64,128,256]{2,1,0:T(8,128)(2,1)}), bf16[64,128,256]{2,1,0:T(8,128)(2,1)}, u32[]{:S(2)}, u32[]{:S(2)}) async-start(bf16[64,128,256]{2,1,0:T(8,128)(2,1)} %get-tuple-element.28), calls=%async_computation.2 | async-start | bytes 8388608 | tf_op jit(solution)/shard_map/all_to_all | solution.py:438
  104.6 3.4 copy-start.8
  104.6 3.4 copy-start.9
  154.5 69.1 %all-to-all-start.4 = ((bf16[64,256,128]{2,1,0:T(8,128)(2,1)}), bf16[64,256,128]{2,1,0:T(8,128)(2,1)}, u32[]{:S(2)}, u32[]{:S(2)}) async-start(bf16[64,256,128]{2,1,0:T(8,128)(2,1)} %get-tuple-element.34), calls=%async_computation.4 | async-start | bytes 8388608 | tf_op jit(solution)/shard_map/all_to_all | solution.py:438
  223.6 68.9 %all-to-all-start.3 = ((bf16[64,256,128]{2,1,0:T(8,128)(2,1)}), bf16[64,256,128]{2,1,0:T(8,128)(2,1)}, u32[]{:S(2)}, u32[]{:S(2)}) async-start(bf16[64,256,128]{2,1,0:T(8,128)(2,1)} %get-tuple-element.33), calls=%async_computation.3 | async-start | bytes 8388608 | tf_op jit(solution)/shard_map/all_to_all | solution.py:438
  301.8 46.6 %all-to-all-start.5 = ((bf16[128,32,256]{2,1,0:T(8,128)(2,1)}), bf16[128,32,256]{2,1,0:T(8,128)(2,1)S(1)}, u32[]{:S(2)}, u32[]{:S(2)}) async-start(bf16[128,32,256]{2,1,0:T(8,128)(2,1)} %bitcast.111), calls=%async_computation.5 | async-start | bytes 4194304 | tf_op jit(solution)/shard_map/all_to_all | solution.py:438
  323.1 1.0 copy-start.1
  324.9 39.6 %collective-permute-start.2 = (f32[32,256]{1,0:T(8,128)S(1)}, f32[32,256]{1,0:T(8,128)S(1)}, u32[]{:S(2)}, u32[]{:S(2)}) collective-permute-start(f32[32,256]{1,0:T(8,128)S(1)} %broadcast_select_fusion.1), channel_id=1, source_target_pairs={{0,126},{2,0},{4,2},{6,4},{8,6},{10,8},{12,10},{14,12},{16,14},{18... | collective-permute-start | bytes 98312 | tf_op jit(solution)/shard_map/ppermute | solution.py:430
  350.3 38.0 %all-to-all-start.6 = ((bf16[128,32,256]{2,1,0:T(8,128)(2,1)}), bf16[128,32,256]{2,1,0:T(8,128)(2,1)S(1)}, u32[]{:S(2)}, u32[]{:S(2)}) async-start(bf16[128,32,256]{2,1,0:T(8,128)(2,1)} %broadcast_in_dim.37), calls=%async_computation.6 | async-start | bytes 4194304 | tf_op jit(solution)/shard_map/all_to_all | solution.py:438
  358.7 1.0 copy-start.2
  360.6 25.6 %collective-permute-start.3 = (f32[32,256]{1,0:T(8,128)S(1)}, f32[32,256]{1,0:T(8,128)S(1)}, u32[]{:S(2)}, u32[]{:S(2)}) collective-permute-start(f32[32,256]{1,0:T(8,128)S(1)} %broadcast_select_fusion), channel_id=1, source_target_pairs={{0,2},{2,4},{4,6},{6,8},{8,10},{10,12},{12,14},{14,16},{16,18},{18... | collective-permute-start | bytes 98312 | tf_op jit(solution)/shard_map/ppermute | solution.py:430
  364.4 21.8 %slice-start = ((f32[32,32,256]{2,1,0:T(8,128)}), f32[31,32,256]{2,1,0:T(8,128)S(1)}, s32[]{:S(2)}) async-start(f32[32,32,256]{2,1,0:T(8,128)} %copy-done.1), calls=%async_computation.7 | async-start | bytes 2031616 | tf_op jit(solution)/shard_map/slice | solution.py:529
  364.5 21.7 %slice-start.1 = ((f32[32,32,256]{2,1,0:T(8,128)}), f32[31,32,256]{2,1,0:T(8,128)S(1)}, s32[]{:S(2)}) async-start(f32[32,32,256]{2,1,0:T(8,128)} %copy-done.2), calls=%async_computation.8 | async-start | bytes 2031616 | tf_op jit(solution)/shard_map/slice | solution.py:530
  364.5 21.7 %copy-start.3 = (f32[1024,256]{1,0:T(8,128)S(1)}, f32[1024,256]{1,0:T(8,128)}, u32[]{:S(2)}) copy-start(f32[1024,256]{1,0:T(8,128)} %get-tuple-element.37) | copy-start | bytes 3145732
  388.3 1.3 copy-start

commit v3 on v2

v3 whole, which is shorter than its diff:
```python
import functools
import math

import jax
import jax.numpy as jnp
from jax import lax
from jax.experimental import pallas as pl
from jax.experimental.pallas import tpu as pltpu
from jax.sharding import PartitionSpec as P

D = 256
HEADS = 8
HD = 32
BT = 128
RY = 32
RX = 32
SUB = 8
KEYS = 128
CELLS = RY * RX
EPSILON = 1e-06
SCALE = 1.0 / math.sqrt(HD)
EXP2_SCALE = SCALE * math.log2(math.e)
AHEAD = 2

f32 = jnp.float32
bf16 = jnp.bfloat16


def mm(a, b):
    return lax.dot_general(a, b, (((1,), (0,)), ((), ())), preferred_element_type=f32)


def mm_nt(a, b):
    return lax.dot_general(a, b, (((1,), (1,)), ((), ())), preferred_element_type=f32)


VMEM = pl.BlockSpec(memory_space=pltpu.VMEM)
HBM = pl.BlockSpec(memory_space=pltpu.HBM)
PARAMS = pltpu.CompilerParams(vmem_limit_bytes=60 * 1024 * 1024)


def hidden_kernel(rim_ref, w_ref, send_ref, shifts_ref):
    rim = rim_ref[...].astype(f32)
    rows = rim.shape[0]
    col = lax.broadcasted_iota(jnp.int32, (rows, D), 0) % RX
    shifts_ref[0] = jnp.where(col == 0, 0.0, pltpu.roll(rim, 1, 0)).astype(bf16)
    shifts_ref[1] = rim_ref[...]
    shifts_ref[2] = jnp.where(col == RX - 1, 0.0, pltpu.roll(rim, rows - 1, 0)).astype(bf16)
    slices = send_ref.shape[1]
    piece = CELLS // 4

    @pl.loop(0, 4)
    def _(i):
        base = i * piece
        total = rim_ref[pl.ds(pl.multiple_of(base + RX, RX), piece), :].astype(f32)
        for a in range(3):
            for b in range(3):
                cells = shifts_ref[b, pl.ds(pl.multiple_of(base + a * RX, RX), piece), :]
                total = total + mm(cells, w_ref[3 * a + b])
        hidden = total.astype(bf16)
        for k in range(piece // KEYS):
            cuts = range(k * KEYS, (k + 1) * KEYS, slices)
            send_ref[i * (piece // KEYS) + k] = jnp.concatenate(
                [hidden[at : at + slices] for at in cuts], axis=1
            )


def hidden_slices(rimmed, w_conv, slices):
    rows = (RY + 2) * RX
    return pl.pallas_call(
        hidden_kernel,
        out_shape=(
            jax.ShapeDtypeStruct((SUB, slices, KEYS * D // slices), bf16),
            jax.ShapeDtypeStruct((3, rows, D), bf16),
        ),
        in_specs=[VMEM, VMEM],
        out_specs=(VMEM, VMEM),
        compiler_params=PARAMS,
        cost_estimate=pl.CostEstimate(
            flops=2 * 9 * CELLS * D * D, bytes_accessed=6_000_000, transcendentals=0
        ),
        name="conv_slices",
    )(rimmed, w_conv)


def pick_kernel(table_ref, ids_ref, out_ref):
    names = table_ref.shape[0]
    blocks, sources = ids_ref.shape
    group = 256 // blocks
    lane = lax.broadcasted_iota(jnp.int32, (blocks, names), 1)
    for g in range(0, sources, group):
        hot = [
            jnp.where(lane == ids_ref[:, g + k : g + k + 1], 1.0, 0.0).astype(bf16)
            for k in range(group)
        ]
        rows = mm(jnp.concatenate(hot, axis=0), table_ref[...]).astype(bf16)
        for k in range(group):
            out_ref[g + k] = rows[k * blocks : (k + 1) * blocks]


def pick(table, ids):
    blocks, sources = ids.shape
    width = table.shape[1]
    return pl.pallas_call(
        pick_kernel,
        out_shape=jax.ShapeDtypeStruct((sources, blocks, width), bf16),
        in_specs=[VMEM, VMEM],
        out_specs=VMEM,
        compiler_params=PARAMS,
        cost_estimate=pl.CostEstimate(
            flops=2 * sources * blocks * table.size, bytes_accessed=4_000_000, transcendentals=0
        ),
        name="pick",
    )(table, ids)


def gather_kernel(ids_ref, slots_ref, *rest):
    acc_ref, out_ref = rest[:-1], rest[-1]
    names = out_ref.shape[0]
    rows = slots_ref.shape[0]
    piece = min(512, rows)
    total = acc_ref[0][...] if acc_ref else None
    name = lax.broadcasted_iota(jnp.int32, (names, piece), 0)
    for at in range(0, rows, piece):
        hot = jnp.where(name == ids_ref[:, at : at + piece], 1.0, 0.0).astype(bf16)
        part = mm(hot, slots_ref[at : at + piece, :])
        total = part if total is None else total + part
    out_ref[...] = total.astype(out_ref.dtype)


def gather(ids, slots, names, acc, dtype):
    width = slots.shape[1]
    return pl.pallas_call(
        gather_kernel,
        out_shape=jax.ShapeDtypeStruct((names, width), dtype),
        in_specs=[VMEM] * (2 + len(acc)),
        out_specs=VMEM,
        compiler_params=PARAMS,
        cost_estimate=pl.CostEstimate(
            flops=2 * slots.size * names, bytes_accessed=4_000_000, transcendentals=0
        ),
        name="gather",
    )(ids, slots, *acc)


def attend_kernel(base, live, wq, wq_t, wkv, wkv_t, wo, wo_t, grads_in, slots, xs, cots, *rest):
    outs, tgrads, hgrads, grads_ref, hbuf, xbuf, cbuf, obuf, tbuf, gbuf, in_sems, out_sems = rest[-12:]
    steps = slots.shape[0] // 2
    slices = slots.shape[1]

    def loads(i, slot):
        blocks = pl.ds(base + 2 * i, 2)
        return [
            pltpu.make_async_copy(slots.at[pl.ds(2 * i, 2)], hbuf.at[slot], in_sems.at[slot, 0]),
            pltpu.make_async_copy(xs.at[blocks], xbuf.at[slot], in_sems.at[slot, 1]),
            pltpu.make_async_copy(cots.at[blocks], cbuf.at[slot], in_sems.at[slot, 2]),
        ]

    def stores(i, slot):
        blocks = pl.ds(base + 2 * i, 2)
        return [
            pltpu.make_async_copy(gbuf.at[slot], hgrads.at[pl.ds(2 * i, 2)], out_sems.at[slot, 0]),
            pltpu.make_async_copy(obuf.at[slot], outs.at[blocks], out_sems.at[slot, 1]),
            pltpu.make_async_copy(tbuf.at[slot], tgrads.at[blocks], out_sems.at[slot, 2]),
        ]

    for c in loads(0, 0):
        c.start()
    grads_ref[...] = grads_in[...]
    zero = jnp.zeros((HD, BT), bf16)
    none = jnp.zeros((2 * HD, 2 * BT), bf16)

    def paired(t, p):
        first = t[2 * HD * p : 2 * HD * p + HD]
        second = t[2 * HD * p + HD : 2 * HD * p + 2 * HD]
        return jnp.concatenate(
            [
                jnp.concatenate([first, zero], axis=1),
                jnp.concatenate([zero, second], axis=1),
            ],
            axis=0,
        )

    def deep(pair, p):
        return jnp.concatenate([pair, none] if p % 2 == 0 else [none, pair], axis=0)

    @pl.loop(0, steps)
    def _(i):
        slot = lax.rem(i, 2)

        @pl.when(i + 1 < steps)
        def _():
            for c in loads(i + 1, 1 - slot):
                c.start()

        for c in loads(i, slot):
            c.wait()

        @pl.when(i >= 2)
        def _():
            for c in stores(i - 2, slot):
                c.wait()

        live0 = live[0, base + 2 * i]
        live1 = live[0, base + 2 * i + 1]
        sliced = hbuf[slot]
        h = jnp.concatenate(
            [sliced[u, :, at : at + D] for u in range(2) for at in range(0, sliced.shape[2], D)],
            axis=0,
        )
        x = xbuf[slot].reshape(2 * BT, D)
        row = lax.broadcasted_iota(jnp.int32, (2 * BT, D), 0)
        lane = lax.broadcasted_iota(jnp.int32, (D, 2 * BT), 1)
        row_live = row < jnp.where(row < BT, live0, live1 + BT)
        lane_live = lane < jnp.where(lane < BT, live0, live1 + BT)
        cot = jnp.where(row_live, cbuf[slot].reshape(2 * BT, D).astype(f32), 0.0).astype(bf16)
        kv = mm(h, wkv[...]).astype(bf16)
        kv_t = mm_nt(wkv_t[...], h).astype(bf16)
        q_t = mm_nt(wq_t[...], x).astype(bf16)
        d_t = mm_nt(wo[...], cot).astype(bf16)
        att_rows, qg_rows, kg_rows, vg_rows = [[], []], [[], []], [[], []], [[], []]
        def first(p, u):
            rows = slice(u * BT, u * BT + BT)
            half = 128 * (p // 2)
            q2 = paired(q_t[:, rows], p)
            d2 = paired(d_t[:, rows], p)
            scores = mm(kv[rows, half : half + 128], deep(q2, p))
            wg = mm(kv[rows, D + half : D + half + 128], deep(d2, p))
            return q2, d2, scores, wg

        def second(q2, d2, scores, wg):
            top = jnp.max(scores, axis=0, keepdims=True)
            e = jnp.exp2((scores - top) * EXP2_SCALE)
            wf = e * (1.0 / jnp.sum(e, axis=0, keepdims=True))
            mean = jnp.sum(wf * wg, axis=0, keepdims=True)
            sg = (wf * (wg - mean)).astype(bf16)
            return q2, d2, wf.astype(bf16), sg

        def third(p, u, q2, d2, w, sg):
            rows = slice(u * BT, u * BT + BT)
            feats = slice(2 * HD * p, 2 * HD * p + 2 * HD)
            v_feats = slice(D + 2 * HD * p, D + 2 * HD * p + 2 * HD)
            att = mm(kv_t[v_feats, rows], w)
            att_rows[u] += [att[:HD, :BT], att[HD:, BT:]]
            qg = mm(kv_t[feats, rows], sg)
            qg_rows[u] += [qg[:HD, :BT], qg[HD:, BT:]]
            kg_rows[u].append(mm_nt(q2, sg) * SCALE)
            vg_rows[u].append(mm_nt(d2, w))

        units = [(p, u) for p in range(HEADS // 2) for u in range(2)]
        ready, soft = {}, {}
        for k in range(len(units) + AHEAD + 1):
            if k < len(units):
                ready[k] = first(*units[k])
            j = k - AHEAD
            if 0 <= j < len(units):
                soft[j] = second(*ready.pop(j))
            if 0 <= j - 1 < len(units):
                third(*units[j - 1], *soft.pop(j - 1))

        def joined(rows):
            return jnp.concatenate([jnp.concatenate(r, axis=0) for r in rows], axis=1)

        att_t = joined(att_rows).astype(bf16)
        qg_t = (joined(qg_rows) * SCALE).astype(bf16)
        kvg_t = joined([kg_rows[u] + vg_rows[u] for u in range(2)]).astype(bf16)
        mixed = jnp.where(lane_live, mm(wo_t[...], att_t), 0.0)
        obuf[slot] = mixed.T.astype(bf16).reshape(2, BT, D)
        tbuf[slot] = mm(wq[...], qg_t).T.astype(bf16).reshape(2, BT, D)
        back = mm(wkv[...], kvg_t).astype(bf16)
        for u in range(2):
            gbuf[slot, u] = jnp.concatenate(
                [back[at : at + slices, u * BT : u * BT + BT] for at in range(0, D, slices)], axis=1
            )
        grads_ref[0:256] += mm(qg_t, x)
        grads_ref[256:768] += mm(kvg_t, h)
        grads_ref[768:1024] += mm(att_t, cot)
        for c in stores(i, slot):
            c.start()

    for i in range(max(0, steps - 2), steps):
        for c in stores(i, i % 2):
            c.wait()


def attend(base, live, slots, x, cot, weights, grads, kept):
    args = [live, *weights, grads, slots, x, cot, *kept]
    first_kept = len(args) - len(kept)
    token_shape = jax.ShapeDtypeStruct(x.shape, bf16)
    sliced = pltpu.VMEM((2, 2) + slots.shape[1:], bf16)
    pair = pltpu.VMEM((2, 2, BT, D), bf16)
    return pl.pallas_call(
        functools.partial(attend_kernel, base),
        out_shape=(
            token_shape,
            token_shape,
            jax.ShapeDtypeStruct(slots.shape, bf16),
            jax.ShapeDtypeStruct((4 * D, D), f32),
        ),
        in_specs=[pl.BlockSpec(memory_space=pltpu.SMEM)]
        + [VMEM] * (len(weights) + 1)
        + [HBM] * (3 + len(kept)),
        out_specs=(HBM, HBM, HBM, VMEM),
        scratch_shapes=[
            sliced,
            pair,
            pair,
            pair,
            pair,
            sliced,
            pltpu.SemaphoreType.DMA((2, 3)),
            pltpu.SemaphoreType.DMA((2, 3)),
        ],
        input_output_aliases={first_kept + j: j for j in range(len(kept))},
        compiler_params=PARAMS,
        cost_estimate=pl.CostEstimate(
            flops=slots.shape[0] * 800_000_000,
            bytes_accessed=slots.shape[0] * 800_000,
            transcendentals=0,
        ),
        name="attend",
    )(*args)


def finish_kernel(slices_ref, shifts_ref, grads_ref, hgrad_ref, sums_ref, back_t):
    slices = slices_ref.shape[1]
    sums_ref[0 : 4 * D] = grads_ref[...].astype(bf16)
    if sums_ref.shape[0] > 13 * D:
        sums_ref[13 * D :] = jnp.zeros((sums_ref.shape[0] - 13 * D, D), bf16)
    for s in range(SUB):
        cells = slice(s * KEYS, (s + 1) * KEYS)
        part = jnp.concatenate(
            [slices_ref[s, :, at : at + KEYS] for at in range(0, D * KEYS // slices, KEYS)], axis=0
        )
        back_t[:, cells] = part
        hgrad_ref[cells, :] = part.astype(f32).T.astype(bf16)
    for a in range(3):
        for b in range(3):
            at = (4 + 3 * a + b) * D
            sums_ref[at : at + D] = mm(
                back_t[...], shifts_ref[b, a * RX : a * RX + CELLS, :]
            ).astype(bf16)


def finish(slices, shifts, grads, rows):
    return pl.pallas_call(
        finish_kernel,
        out_shape=(
            jax.ShapeDtypeStruct((CELLS, D), bf16),
            jax.ShapeDtypeStruct((rows, D), bf16),
        ),
        in_specs=[VMEM] * 3,
        out_specs=(VMEM, VMEM),
        scratch_shapes=[pltpu.VMEM((D, CELLS), bf16)],
        compiler_params=PARAMS,
        cost_estimate=pl.CostEstimate(
            flops=2 * 9 * CELLS * D * D, bytes_accessed=6_000_000, transcendentals=0
        ),
        name="finish",
    )(slices, shifts, grads)


def normalize_kernel(sums_ref, query_ref, key_ref, value_ref, out_ref, conv_ref):
    def part(k):
        return sums_ref[k * D : (k + 1) * D, :].astype(f32)

    def squares(k):
        item = part(k)
        return jnp.sum(jnp.sum(item * item, axis=0, keepdims=True), axis=1, keepdims=True)

    def factor(total, size):
        return 1.0 / jnp.sqrt(total / size + EPSILON)

    for k, ref in enumerate((query_ref, key_ref, value_ref)):
        ref[...] = (part(k) * factor(squares(k), D * D)).T
    out_ref[...] = part(3) * factor(squares(3), D * D)
    total = squares(4)
    for k in range(5, 13):
        total = total + squares(k)
    scale = factor(total, 9 * D * D)
    for k in range(9):
        conv_ref[k] = (part(4 + k) * scale).T


def normalize(sums):
    square = jax.ShapeDtypeStruct((D, D), f32)
    return pl.pallas_call(
        normalize_kernel,
        out_shape=(square,) * 4 + (jax.ShapeDtypeStruct((9, D, D), f32),),
        in_specs=[pl.BlockSpec(memory_space=pltpu.VMEM)],
        out_specs=(pl.BlockSpec(memory_space=pltpu.VMEM),) * 5,
        compiler_params=pltpu.CompilerParams(vmem_limit_bytes=60 * 1024 * 1024),
        cost_estimate=pl.CostEstimate(flops=4_000_000, bytes_accessed=6_000_000, transcendentals=0),
        name="normalize",
    )(sums)


def ring(value, by):
    length = lax.axis_size("tile")
    return lax.ppermute(value, "tile", [(i, (i + by) % length) for i in range(length)])


def turned(row, flag):
    return jnp.where(flag == 1, row[::-1], row)


def exchange(value, axes="tile"):
    return lax.all_to_all(value, axes, split_axis=0, concat_axis=0, tiled=True)


def local(
    grid,
    tokens,
    targets,
    sub_masks,
    live_counts,
    edge_turns,
    w_query,
    w_key,
    w_value,
    w_out,
    w_conv,
    token_cotan,
):
    ntile = lax.axis_size("tile")
    ndev = ntile * lax.axis_size("win")
    turns = edge_turns[0]
    nblocks = tokens.shape[1] // BT

    sub = jnp.sum(sub_masks[0] * jnp.arange(SUB, dtype=jnp.int32)[None, :], axis=1)
    own = targets[0, :, 0] * SUB + sub
    ids = exchange(jnp.broadcast_to(own[None, :], (ntile, nblocks)))

    field = grid[0]
    above = turned(ring(field[-1], 1), turns[0])
    below = turned(ring(field[0], -1), turns[1])
    rimmed = jnp.concatenate([above[None], field, below[None]], axis=0).reshape(-1, D)
    sliced, shifts = hidden_slices(rimmed, w_conv.reshape(9, D, D), ntile)
    table = exchange(sliced.transpose(1, 0, 2)).reshape(ntile * SUB, -1)

    wkv = jnp.concatenate([w_key, w_value], axis=1)
    weights = (w_query, w_query.T, wkv, wkv.T, w_out, w_out.T)
    x = tokens[0].reshape(nblocks, BT, D)
    cot = token_cotan[0].reshape(nblocks, BT, D)
    half = nblocks // 2
    grads = jnp.zeros((4 * D, D), f32)
    got = [exchange(pick(table, ids[:, c * half : (c + 1) * half].T)) for c in range(2)]
    kept, returned = (), []
    for c in range(2):
        token_out, token_grad, back, grads = attend(
            c * half, live_counts, got[c].transpose(1, 0, 2), x, cot, weights, grads, kept
        )
        kept = (token_out, token_grad)
        returned.append(exchange(back.transpose(1, 0, 2)).reshape(ntile * half, -1))
    rows = [ids[:, c * half : (c + 1) * half].reshape(1, -1) for c in range(2)]
    acc = gather(rows[0], returned[0], ntile * SUB, (), f32)
    home = gather(rows[1], returned[1], ntile * SUB, (acc,), bf16)
    home = exchange(home.reshape(ntile, SUB, -1)).transpose(1, 0, 2)
    each = -(-13 * D // (16 * ndev)) * 16
    hidden_back, sums = finish(home, shifts, grads, ndev * each)

    parts = exchange(sums, ("tile", "win")).reshape(ndev, -1, D)
    share = jnp.sum(parts.astype(f32), axis=0).astype(bf16)
    spread = jnp.broadcast_to(share[None], (ndev,) + share.shape).reshape(-1, D)
    updates = normalize(exchange(spread, ("tile", "win")))

    hidden_back = hidden_back.reshape(RY, RX, D)
    padded = jnp.pad(hidden_back, ((0, 0), (1, 1), (0, 0)))
    taps = []
    for a in range(3):
        piece = jnp.zeros((RY, RX, D), f32)
        for b in range(3):
            cells = padded[:, 2 - b : 2 - b + RX].reshape(-1, D)
            piece = piece + mm_nt(cells, w_conv[a, b]).reshape(RY, RX, D)
        taps.append(piece)
    from_below = ring(turned(taps[0][0], turns[0]), -1)
    from_above = ring(turned(taps[2][-1], turns[1]), 1)
    field_grad = hidden_back.astype(f32) + taps[1]
    field_grad = field_grad + jnp.concatenate([taps[0][1:], from_below[None]], axis=0)
    field_grad = field_grad + jnp.concatenate([from_above[None], taps[2][:-1]], axis=0)
    grid_grad = field_grad.astype(bf16)[None]

    return (
        token_out.reshape(1, -1, D),
        token_grad.reshape(1, -1, D),
        grid_grad,
        *updates[:4],
        updates[4].reshape(3, 3, D, D),
    )


def solution(mesh):
    return jax.shard_map(
        local,
        mesh=mesh,
        in_specs=(
            P("win", "tile", None, None),
            P("win", "tile", None),
            P("win", "tile", None),
            P("win", "tile", None),
            P("win", "tile"),
            P("tile", None),
            P(),
            P(),
            P(),
            P(),
            P(),
            P("win", "tile", None),
        ),
        out_specs=(
            P("win", "tile", None),
            P("win", "tile", None),
            P("win", "tile", None, None),
            P(),
            P(),
            P(),
            P(),
            P(),
        ),
        check_vma=False,
    )
```

time: 395 us -> 334 us (0.85)
  blocking collectives: 55.4 us -> 18.9 us
  waiting for transfers between devices: 113 us -> 89.9 us
  local copies, waits for them, and re-layouts: 12.4 us -> 33.7 us
  starting transfers between devices: 95.3 us -> 78.6 us
  other arithmetic: 10.2 us -> 5.91 us
    all_to_all x1, blocking collectives: 55.4 us -> 18.9 us  [exchange(): return lax.all_to_all(value, axes, split_axis=0, concat_axis=0, tiled=True)]
    all_to_all x6 -> x8, waiting for transfers between devices: 91.4 us -> 75.3 us  [exchange(): return lax.all_to_all(value, axes, split_axis=0, concat_axis=0, tiled=True)]
    all_to_all x6 -> x8, starting transfers between devices: 79.2 us -> 63.8 us  [exchange(): return lax.all_to_all(value, axes, split_axis=0, concat_axis=0, tiled=True)]
    transpose x0 -> x3, local copies, waits for them, and re-layouts: none -> 10.3 us  [the longest x2 8.21 us: local(): returned.append(exchange(back.transpose(1, 0, 2)).reshape(ntile * half, -1))]
    ppermute x4, waiting for transfers between devices: 21.7 us -> 14.6 us  [ring(): lax.ppermute(value, 'tile', [(i, (i + by) % length) for i in range(length)])]
    all_to_all x2 -> x4, local copies, waits for them, and re-layouts: 0.79 us -> 7.57 us  [exchange(): return lax.all_to_all(value, axes, split_axis=0, concat_axis=0, tiled=True)]
    pallas_call x1, Pallas kernels: 9.33 us -> 4.77 us  [finish(): pl.pallas_call(finish_kernel, out_shape=(jax.ShapeDtypeStruct((CELLS, D),...]
    pallas_call x4 -> x7, Pallas kernels: 79.6 us -> 82.3 us  [the longest x2 62.6 us: attend(): pl.pallas_call(functools.partial(attend_kernel, base), out_shape=(token_s...]
  transfers between devices with their start and end apart: 10 -> 12, of which waited for: 5 -> 6; matrix products, arithmetic and copies ran while one was open for 6% -> 12% of each run, Pallas kernels for 18% -> 22%
where the time goes in v3:
time: 334 us; the launch traced here: 332 us
  Pallas kernels  91.1 us (27%)
  waiting for transfers between devices  89.9 us (27%)
  starting transfers between devices  78.6 us (24%)
  local copies, waits for them, and re-layouts  33.7 us (10%)
  blocking collectives  18.9 us (6%)
  matrix products  12.1 us (4%)
  other arithmetic  5.91 us (2%)
    all_to_all x8, waiting for transfers between devices, exchange(): return lax.all_to_all(value, axes, split_axis=0, concat_axis=0, tiled=True)  75.3 us
    all_to_all x8, starting transfers between devices, exchange(): return lax.all_to_all(value, axes, split_axis=0, concat_axis=0, tiled=True)  63.8 us
    pallas_call x2, Pallas kernels, attend(): pl.pallas_call(functools.partial(attend_kernel, base), out_shape=(token_s...  62.6 us
    all_to_all x1, blocking collectives, exchange(): return lax.all_to_all(value, axes, split_axis=0, concat_axis=0, tiled=True)  18.9 us
    ppermute x4, starting transfers between devices, ring(): lax.ppermute(value, 'tile', [(i, (i + by) % length) for i in range(length)])  14.8 us
    ppermute x4, waiting for transfers between devices, ring(): lax.ppermute(value, 'tile', [(i, (i + by) % length) for i in range(length)])  14.6 us
    dot_general x9, matrix products, mm_nt(): lax.dot_general(a, b, (((1,), (1,)), ((), ())), preferred_element_type=f32)  12.1 us
    transpose x2, local copies, waits for them, and re-layouts, local(): returned.append(exchange(back.transpose(1, 0, 2)).reshape(ntile * half, -1))  8.21 us
  transfers between devices with their start and end apart: 12, of which 6 were waited for; matrix products, arithmetic and copies ran while one was open for 12% of the time, Pallas kernels for 22%

profile of v3, /device:TPU:1, one launch (start us, length us, event | category | flops | bytes accessed | tf_op | source)
XLA Modules:
  0.0 332.4 jit_solution(13469023419054143019)
XLA Ops:
  0.6 0.7 fusion.25
  1.3 0.7 bitcast_add_fusion
  2.0 0.6 broadcast_in_dim.34
  2.6 12.0 %all-to-all-start.1 = ((s32[64,1,64]{2,1,0:T(1,128)}), s32[64,1,64]{2,1,0:T(1,128)S(1)}, u32[]{:S(2)}, u32[]{:S(2)}) async-start(s32[64,1,64]{2,1,0:T(1,128)} %broadcast_in_dim.34), calls=%async_computation.1 | async-start | bytes 65536 | tf_op jit(solution)/shard_map/all_to_all | solution.py:408
  14.6 0.7 slice_bitcast_fusion.3
  15.3 1.0 collective-permute-start
  16.4 5.9 %collective-permute-start.1 = (bf16[32,256]{1,0:T(8,128)(2,1)S(1)}, bf16[32,256]{1,0:T(8,128)(2,1)S(1)}, u32[]{:S(2)}, u32[]{:S(2)}) collective-permute-start(bf16[32,256]{1,0:T(8,128)(2,1)S(1)} %get-tuple-element.43), channel_id=1, source_target_pairs={{0,126},{2,0},{4,2},{6,4},{8,6},{10,8},{12,10},{14,12},{16,14},{18... | collective-permute-start | bytes 49160 | tf_op jit(solution)/shard_map/ppermute | solution.py:400
  22.2 1.3 fusion.34
  25.1 1.9 pad_maximum_fusion
  27.0 4.6 %conv_slices.1 = (bf16[8,64,512]{2,1,0:T(8,128)(2,1)}, bf16[3,1088,256]{2,1,0:T(8,128)(2,1)}) custom-call(bf16[1088,256]{1,0:T(8,128)(2,1)} %bitcast.130, bf16[9,256,256]{2,1,0:T(8,128)(2,1)} %bitcast.128), custom_call_target="tpu_custom_call" | custom-call | flops 1207959552 | bytes 6000000 | tf_op jit(solution)/shard_map/conv_slices/pallas_call | solution.py:70
  31.6 2.1 copy.53
  33.7 7.6 %all-to-all-start = ((bf16[64,8,512]{2,1,0:T(8,128)(2,1)}), bf16[64,8,512]{2,1,0:T(8,128)(2,1)S(1)}, u32[]{:S(2)}, u32[]{:S(2)}) async-start(bf16[64,8,512]{2,1,0:T(8,128)(2,1)} %copy.53), calls=%async_computation | async-start | bytes 1048576 | tf_op jit(solution)/shard_map/all_to_all | solution.py:408
  41.3 0.6 fusion.33
  42.0 10.0 %all-to-all-done = bf16[64,8,512]{2,1,0:T(8,128)(2,1)S(1)} async-done(((bf16[64,8,512]{2,1,0:T(8,128)(2,1)}), bf16[64,8,512]{2,1,0:T(8,128)(2,1)S(1)}, u32[]{:S(2)}, u32[]{:S(2)}) %all-to-all-start) | async-done | bytes 524320 | tf_op jit(solution)/shard_map/all_to_all | solution.py:408
  51.9 0.8 copy-done.5
  52.7 3.7 %pick.2 = bf16[64,32,512]{2,1,0:T(8,128)(2,1)} custom-call(bf16[512,512]{1,0:T(8,128)(2,1)} %bitcast.131, s32[32,64]{1,0:T(8,128)} %get-tuple-element.47.ids_ref), custom_call_target="tpu_custom_call" | custom-call | flops 1073741824 | bytes 4000000 | tf_op jit(solution)/shard_map/pick/pallas_call | solution.py:104
  56.4 4.9 %all-to-all-start.2 = ((bf16[64,32,512]{2,1,0:T(8,128)(2,1)}), bf16[64,32,512]{2,1,0:T(8,128)(2,1)S(1)}, u32[]{:S(2)}, u32[]{:S(2)}) async-start(bf16[64,32,512]{2,1,0:T(8,128)(2,1)} %pick.2), calls=%async_computation.2 | async-start | bytes 4194304 | tf_op jit(solution)/shard_map/all_to_all | solution.py:408
  61.6 0.8 copy.49
  62.4 0.8 copy.52
  63.1 0.7 fusion.32
  63.9 0.8 copy.58.wkv
  64.7 3.7 %pick.3 = bf16[64,32,512]{2,1,0:T(8,128)(2,1)} custom-call(bf16[512,512]{1,0:T(8,128)(2,1)} %bitcast.132, s32[32,64]{1,0:T(8,128)} %get-tuple-element.48.ids_ref), custom_call_target="tpu_custom_call" | custom-call | flops 1073741824 | bytes 4000000 | tf_op jit(solution)/shard_map/pick/pallas_call | solution.py:104
  68.4 19.2 %all-to-all-done.2 = bf16[64,32,512]{2,1,0:T(8,128)(2,1)S(1)} async-done(((bf16[64,32,512]{2,1,0:T(8,128)(2,1)}), bf16[64,32,512]{2,1,0:T(8,128)(2,1)S(1)}, u32[]{:S(2)}, u32[]{:S(2)}) %all-to-all-start.2) | async-done | bytes 2097184 | tf_op jit(solution)/shard_map/all_to_all | solution.py:408
  87.6 8.4 %all-to-all-start.3 = ((bf16[64,32,512]{2,1,0:T(8,128)(2,1)}), bf16[64,32,512]{2,1,0:T(8,128)(2,1)}, u32[]{:S(2)}, u32[]{:S(2)}) async-start(bf16[64,32,512]{2,1,0:T(8,128)(2,1)} %pick.3), calls=%async_computation.3 | async-start | bytes 4194304 | tf_op jit(solution)/shard_map/all_to_all | solution.py:408
  96.0 2.5 copy.68
  98.5 1.1 broadcast_in_dim.31.grads_in
  99.6 31.3 %attend.2 = (bf16[64,128,256]{2,1,0:T(8,128)(2,1)}, bf16[64,128,256]{2,1,0:T(8,128)(2,1)}, bf16[32,64,512]{2,1,0:T(8,128)(2,1)}, f32[1024,256]{1,0:T(8,128)}) custom-call(s32[1,64]{1,0:T(1,128)} %live.3, bf16[256,256]{1,0:T(8,128)(2,1)} %wq.3, bf16[256,256]{1,0:T(8,128)(2,1)} %bitcast.137, bf16[256,512]{1,0:T(8,128)(2,1)} %copy.58.wkv, ...), custom_call_target="tpu_custom_call" | custom-call | flops 25600000000 | bytes 25600000 | tf_op jit(solution)/shard_map/attend/pallas_call | solution.py:292
  130.9 4.1 %copy.62 = bf16[64,32,512]{2,1,0:T(8,128)(2,1)} copy(bf16[64,32,512]{2,0,1:T(8,128)(2,1)} %bitcast.127) | data formatting | bytes 4194304 | tf_op jit(solution)/shard_map/transpose | solution.py:454
  135.0 9.5 %all-to-all-start.5 = ((bf16[64,32,512]{2,1,0:T(8,128)(2,1)}), bf16[64,32,512]{2,1,0:T(8,128)(2,1)S(1)}, u32[]{:S(2)}, u32[]{:S(2)}) async-start(bf16[64,32,512]{2,1,0:T(8,128)(2,1)} %copy.62), calls=%async_computation.5 | async-start | bytes 4194304 | tf_op jit(solution)/shard_map/all_to_all | solution.py:408
  144.6 4.1 %copy.67 = bf16[64,32,512]{2,0,1:T(8,128)(2,1)} copy(bf16[64,32,512]{2,1,0:T(8,128)(2,1)} %all-to-all-done.3) | data formatting | bytes 4194304 | tf_op jit(solution)/shard_map/all_to_all | solution.py:408
  148.6 31.3 %attend.3 = (bf16[64,128,256]{2,1,0:T(8,128)(2,1)}, bf16[64,128,256]{2,1,0:T(8,128)(2,1)}, bf16[32,64,512]{2,1,0:T(8,128)(2,1)}, f32[1024,256]{1,0:T(8,128)}) custom-call(s32[1,64]{1,0:T(1,128)} %live.3, bf16[256,256]{1,0:T(8,128)(2,1)} %wq.3, bf16[256,256]{1,0:T(8,128)(2,1)} %bitcast.138, ...), custom_call_target="tpu_custom_call", output_to_operand_aliasing={{0}: (11, {}), {1}: (12, {})} | custom-call | flops 25600000000 | bytes 25600000 | tf_op jit(solution)/shard_map/attend/pallas_call | solution.py:292
  179.9 4.1 %copy.60 = bf16[64,32,512]{2,1,0:T(8,128)(2,1)} copy(bf16[64,32,512]{2,0,1:T(8,128)(2,1)} %bitcast.125) | data formatting | bytes 4194304 | tf_op jit(solution)/shard_map/transpose | solution.py:454
  184.0 1.3 copy-done.4
  185.3 10.0 %all-to-all-start.4 = ((bf16[64,32,512]{2,1,0:T(8,128)(2,1)}), bf16[64,32,512]{2,1,0:T(8,128)(2,1)}, u32[]{:S(2)}, u32[]{:S(2)}) async-start(bf16[64,32,512]{2,1,0:T(8,128)(2,1)} %copy.60), calls=%async_computation.4 | async-start | bytes 4194304 | tf_op jit(solution)/shard_map/all_to_all | solution.py:408
  195.4 0.7 reshape.130.ids_ref
  196.2 0.7 reshape.128.ids_ref
  196.9 3.9 %gather.2.rest_0_ = f32[512,512]{1,0:T(8,128)} custom-call(s32[1,2048]{1,0:T(1,128)} %reshape.130.ids_ref, bf16[2048,512]{1,0:T(8,128)(2,1)} %bitcast.122), custom_call_target="tpu_custom_call" | custom-call | flops 1073741824 | bytes 4000000 | tf_op jit(solution)/shard_map/gather/pallas_call | solution.py:133
  200.8 20.3 %all-to-all-done.4 = bf16[64,32,512]{2,1,0:T(8,128)(2,1)} async-done(((bf16[64,32,512]{2,1,0:T(8,128)(2,1)}), bf16[64,32,512]{2,1,0:T(8,128)(2,1)}, u32[]{:S(2)}, u32[]{:S(2)}) %all-to-all-start.4) | async-done | bytes 2097184 | tf_op jit(solution)/shard_map/all_to_all | solution.py:408
  221.1 3.9 %gather.3 = bf16[512,512]{1,0:T(8,128)(2,1)} custom-call(s32[1,2048]{1,0:T(1,128)} %reshape.128.ids_ref, bf16[2048,512]{1,0:T(8,128)(2,1)} %bitcast.26.slots_ref, f32[512,512]{1,0:T(8,128)} %gather.2.rest_0_), custom_call_target="tpu_custom_call" | custom-call | flops 1073741824 | bytes 4000000 | tf_op jit(solution)/shard_map/gather/pallas_call | solution.py:133
  225.1 18.9 %all_to_all.56 = bf16[64,8,512]{2,1,0:T(8,128)(2,1)S(1)} all-to-all(bf16[64,8,512]{2,1,0:T(8,128)(2,1)} %bitcast.135), channel_id=1, replica_groups=mesh['tile'=64,'win'=2] {'tile'}, dimensions={0} | all-to-all | bytes 1048576 | tf_op jit(solution)/shard_map/all_to_all | solution.py:408
  244.0 0.9 copy.69
  244.9 4.8 %finish.1 = (bf16[1024,256]{1,0:T(8,128)(2,1)}, bf16[4096,256]{1,0:T(8,128)(2,1)}) custom-call(bf16[8,64,512]{2,1,0:T(8,128)(2,1)} %bitcast.133, bf16[3,1088,256]{2,1,0:T(8,128)(2,1)} %get-tuple-element.33.shifts_ref, f32[1024,256]{1,0:T(8,128)} %get-tuple-element.34.grads_ref), custom_call_target="tpu_custom_call" | custom-call | flops 1207959552 | bytes 6000000 | tf_op jit(solution)/shard_map/finish/pallas_call | solution.py:346
  249.7 6.9 %all-to-all-start.7 = ((bf16[128,32,256]{2,1,0:T(8,128)(2,1)}), bf16[128,32,256]{2,1,0:T(8,128)(2,1)S(1)}, u32[]{:S(2)}, u32[]{:S(2)}) async-start(bf16[128,32,256]{2,1,0:T(8,128)(2,1)} %bitcast.123), calls=%async_computation.7 | async-start | bytes 4194304 | tf_op jit(solution)/shard_map/all_to_all | solution.py:408
  256.6 1.2 fusion.5
  257.8 1.2 convolution_add_fusion.3
  259.1 1.3 convolution_add_fusion.2
  260.3 1.0 copy-done.2
  261.3 25.7 %all-to-all-done.7 = bf16[128,32,256]{2,1,0:T(8,128)(2,1)S(1)} async-done(((bf16[128,32,256]{2,1,0:T(8,128)(2,1)}), bf16[128,32,256]{2,1,0:T(8,128)(2,1)S(1)}, u32[]{:S(2)}, u32[]{:S(2)}) %all-to-all-start.7) | async-done | bytes 2097184 | tf_op jit(solution)/shard_map/all_to_all | solution.py:408
  287.4 1.6 broadcast_in_dim.38
  289.0 4.6 %all-to-all-start.8 = ((bf16[128,32,256]{2,1,0:T(8,128)(2,1)}), bf16[128,32,256]{2,1,0:T(8,128)(2,1)S(1)}, u32[]{:S(2)}, u32[]{:S(2)}) async-start(bf16[128,32,256]{2,1,0:T(8,128)(2,1)} %broadcast_in_dim.38), calls=%async_computation.8 | async-start | bytes 4194304 | tf_op jit(solution)/shard_map/all_to_all | solution.py:408
  293.6 0.8 broadcast_select_fusion.1
  294.3 7.9 %collective-permute-start.2 = (f32[32,256]{1,0:T(8,128)S(1)}, f32[32,256]{1,0:T(8,128)S(1)}, u32[]{:S(2)}, u32[]{:S(2)}) collective-permute-start(f32[32,256]{1,0:T(8,128)S(1)} %broadcast_select_fusion.1), channel_id=1, source_target_pairs={{0,126},{2,0},{4,2},{6,4},{8,6},{10,8},{12,10},{14,12},{16,14},{18... | collective-permute-start | bytes 98312 | tf_op jit(solution)/shard_map/ppermute | solution.py:400
  302.2 1.2 fusion.4
  303.5 1.2 convolution_add_fusion.1
  304.7 1.3 convolution_add_fusion
  306.0 1.0 copy-done.3
  307.0 0.8 broadcast_select_fusion
  307.8 1.2 fusion.6
  309.0 1.2 convolution_add_fusion.5
  310.3 4.5 %collective-permute-done.2 = f32[32,256]{1,0:T(8,128)S(1)} collective-permute-done((f32[32,256]{1,0:T(8,128)S(1)}, f32[32,256]{1,0:T(8,128)S(1)}, u32[]{:S(2)}, u32[]{:S(2)}) %collective-permute-start.2) | collective-permute-done | bytes 32800 | tf_op jit(solution)/shard_map/ppermute | solution.py:400
  314.7 10.1 %collective-permute-done.3 = f32[32,256]{1,0:T(8,128)S(1)} collective-permute-done((f32[32,256]{1,0:T(8,128)S(1)}, f32[32,256]{1,0:T(8,128)S(1)}, u32[]{:S(2)}, u32[]{:S(2)}) %collective-permute-start.3) | collective-permute-done | bytes 32800 | tf_op jit(solution)/shard_map/ppermute | solution.py:400
  324.9 2.1 fusion.3
  327.0 1.4 copy-done.1
  328.4 4.0 %normalize.1 = (f32[256,256]{1,0:T(8,128)}, f32[256,256]{1,0:T(8,128)}, f32[256,256]{1,0:T(8,128)}, f32[256,256]{1,0:T(8,128)}, f32[9,256,256]{2,1,0:T(8,128)}) custom-call(bf16[4096,256]{1,0:T(8,128)(2,1)} %bitcast.121), custom_call_target="tpu_custom_call" | custom-call | flops 4000000 | bytes 6000000 | tf_op jit(solution)/shard_map/normalize/pallas_call | solution.py:387
  (40 shorter events, 1.1 us)
Async XLA Ops:
  2.6 31.1 %all-to-all-start.1 = ((s32[64,1,64]{2,1,0:T(1,128)}), s32[64,1,64]{2,1,0:T(1,128)S(1)}, u32[]{:S(2)}, u32[]{:S(2)}) async-start(s32[64,1,64]{2,1,0:T(1,128)} %broadcast_in_dim.34), calls=%async_computation.1 | async-start | bytes 65536 | tf_op jit(solution)/shard_map/all_to_all | solution.py:408
  15.3 9.5 %collective-permute-start = (bf16[32,256]{1,0:T(8,128)(2,1)S(1)}, bf16[32,256]{1,0:T(8,128)(2,1)S(1)}, u32[]{:S(2)}, u32[]{:S(2)}) collective-permute-start(bf16[32,256]{1,0:T(8,128)(2,1)S(1)} %get-tuple-element.42), channel_id=1, source_target_pairs={{0,2},{2,4},{4,6},{6,8},{8,10},{10,12},{12,14},{14,16},{16,18},{18... | collective-permute-start | bytes 49160 | tf_op jit(solution)/shard_map/ppermute | solution.py:400
  16.4 8.6 %collective-permute-start.1 = (bf16[32,256]{1,0:T(8,128)(2,1)S(1)}, bf16[32,256]{1,0:T(8,128)(2,1)S(1)}, u32[]{:S(2)}, u32[]{:S(2)}) collective-permute-start(bf16[32,256]{1,0:T(8,128)(2,1)S(1)} %get-tuple-element.43), channel_id=1, source_target_pairs={{0,126},{2,0},{4,2},{6,4},{8,6},{10,8},{12,10},{14,12},{16,14},{18... | collective-permute-start | bytes 49160 | tf_op jit(solution)/shard_map/ppermute | solution.py:400
  33.7 18.2 %all-to-all-start = ((bf16[64,8,512]{2,1,0:T(8,128)(2,1)}), bf16[64,8,512]{2,1,0:T(8,128)(2,1)S(1)}, u32[]{:S(2)}, u32[]{:S(2)}) async-start(bf16[64,8,512]{2,1,0:T(8,128)(2,1)} %copy.53), calls=%async_computation | async-start | bytes 1048576 | tf_op jit(solution)/shard_map/all_to_all | solution.py:408
  51.9 0.8 copy-start.5
  56.4 5.0 %copy-start.6 = (bf16[256,256]{1,0:T(8,128)(2,1)S(1)}, bf16[256,256]{1,0:T(8,128)(2,1)}, u32[]{:S(2)}) copy-start(bf16[256,256]{1,0:T(8,128)(2,1)} %param.19) | copy-start | bytes 393220
  56.4 5.1 %copy-start.7 = (bf16[256,256]{1,0:T(8,128)(2,1)S(1)}, bf16[256,256]{1,0:T(8,128)(2,1)}, u32[]{:S(2)}) copy-start(bf16[256,256]{1,0:T(8,128)(2,1)} %param.20) | copy-start | bytes 393220
  56.4 5.2 %copy-start.8 = (bf16[256,256]{1,0:T(8,128)(2,1)S(1)}, bf16[256,256]{1,0:T(8,128)(2,1)}, u32[]{:S(2)}) copy-start(bf16[256,256]{1,0:T(8,128)(2,1)} %wq.3) | copy-start | bytes 393220
  56.4 6.0 %copy-start.9 = (bf16[256,256]{1,0:T(8,128)(2,1)S(1)}, bf16[256,256]{1,0:T(8,128)(2,1)}, u32[]{:S(2)}) copy-start(bf16[256,256]{1,0:T(8,128)(2,1)} %wo.3) | copy-start | bytes 393220
  56.4 31.2 %all-to-all-start.2 = ((bf16[64,32,512]{2,1,0:T(8,128)(2,1)}), bf16[64,32,512]{2,1,0:T(8,128)(2,1)S(1)}, u32[]{:S(2)}, u32[]{:S(2)}) async-start(bf16[64,32,512]{2,1,0:T(8,128)(2,1)} %pick.2), calls=%async_computation.2 | async-start | bytes 4194304 | tf_op jit(solution)/shard_map/all_to_all | solution.py:408
  87.6 47.4 %all-to-all-start.3 = ((bf16[64,32,512]{2,1,0:T(8,128)(2,1)}), bf16[64,32,512]{2,1,0:T(8,128)(2,1)}, u32[]{:S(2)}, u32[]{:S(2)}) async-start(bf16[64,32,512]{2,1,0:T(8,128)(2,1)} %pick.3), calls=%async_computation.3 | async-start | bytes 4194304 | tf_op jit(solution)/shard_map/all_to_all | solution.py:408
  135.0 49.0 %all-to-all-start.5 = ((bf16[64,32,512]{2,1,0:T(8,128)(2,1)}), bf16[64,32,512]{2,1,0:T(8,128)(2,1)S(1)}, u32[]{:S(2)}, u32[]{:S(2)}) async-start(bf16[64,32,512]{2,1,0:T(8,128)(2,1)} %copy.62), calls=%async_computation.5 | async-start | bytes 4194304 | tf_op jit(solution)/shard_map/all_to_all | solution.py:408
  184.0 1.3 copy-start.4
  185.3 35.8 %all-to-all-start.4 = ((bf16[64,32,512]{2,1,0:T(8,128)(2,1)}), bf16[64,32,512]{2,1,0:T(8,128)(2,1)}, u32[]{:S(2)}, u32[]{:S(2)}) async-start(bf16[64,32,512]{2,1,0:T(8,128)(2,1)} %copy.60), calls=%async_computation.4 | async-start | bytes 4194304 | tf_op jit(solution)/shard_map/all_to_all | solution.py:408
  249.7 6.9 %copy-start = (bf16[1024,256]{1,0:T(8,128)(2,1)S(1)}, bf16[1024,256]{1,0:T(8,128)(2,1)}, u32[]{:S(2)}) copy-start(bf16[1024,256]{1,0:T(8,128)(2,1)} %get-tuple-element.35) | copy-start | bytes 1572868
  249.7 37.4 %all-to-all-start.7 = ((bf16[128,32,256]{2,1,0:T(8,128)(2,1)}), bf16[128,32,256]{2,1,0:T(8,128)(2,1)S(1)}, u32[]{:S(2)}, u32[]{:S(2)}) async-start(bf16[128,32,256]{2,1,0:T(8,128)(2,1)} %bitcast.123), calls=%async_computation.7 | async-start | bytes 4194304 | tf_op jit(solution)/shard_map/all_to_all | solution.py:408
  260.3 1.0 copy-start.2
  289.0 38.0 %all-to-all-start.8 = ((bf16[128,32,256]{2,1,0:T(8,128)(2,1)}), bf16[128,32,256]{2,1,0:T(8,128)(2,1)S(1)}, u32[]{:S(2)}, u32[]{:S(2)}) async-start(bf16[128,32,256]{2,1,0:T(8,128)(2,1)} %broadcast_in_dim.38), calls=%async_computation.8 | async-start | bytes 4194304 | tf_op jit(solution)/shard_map/all_to_all | solution.py:408
  294.3 20.4 %collective-permute-start.2 = (f32[32,256]{1,0:T(8,128)S(1)}, f32[32,256]{1,0:T(8,128)S(1)}, u32[]{:S(2)}, u32[]{:S(2)}) collective-permute-start(f32[32,256]{1,0:T(8,128)S(1)} %broadcast_select_fusion.1), channel_id=1, source_target_pairs={{0,126},{2,0},{4,2},{6,4},{8,6},{10,8},{12,10},{14,12},{16,14},{18... | collective-permute-start | bytes 98312 | tf_op jit(solution)/shard_map/ppermute | solution.py:400
  306.0 1.0 copy-start.3
  307.7 17.1 %collective-permute-start.3 = (f32[32,256]{1,0:T(8,128)S(1)}, f32[32,256]{1,0:T(8,128)S(1)}, u32[]{:S(2)}, u32[]{:S(2)}) collective-permute-start(f32[32,256]{1,0:T(8,128)S(1)} %broadcast_select_fusion), channel_id=1, source_target_pairs={{0,2},{2,4},{4,6},{6,8},{8,10},{10,12},{12,14},{14,16},{16,18},{18... | collective-permute-start | bytes 98312 | tf_op jit(solution)/shard_map/ppermute | solution.py:400
  310.2 14.6 %slice-start = ((f32[32,32,256]{2,1,0:T(8,128)}), f32[31,32,256]{2,1,0:T(8,128)S(1)}, s32[]{:S(2)}) async-start(f32[32,32,256]{2,1,0:T(8,128)} %copy-done.2), calls=%async_computation.9 | async-start | bytes 2031616 | tf_op jit(solution)/shard_map/slice | solution.py:479
  310.2 14.6 %slice-start.1 = ((f32[32,32,256]{2,1,0:T(8,128)}), f32[31,32,256]{2,1,0:T(8,128)S(1)}, s32[]{:S(2)}) async-start(f32[32,32,256]{2,1,0:T(8,128)} %copy-done.3), calls=%async_computation.10 | async-start | bytes 2031616 | tf_op jit(solution)/shard_map/slice | solution.py:480
  327.0 1.4 copy-start.1

commit v4 on v3

--- a/solution.py
+++ b/solution.py
@@ -15,12 +15,13 @@
 RY = 32
 RX = 32
 SUB = 8
+LANES = 128
 KEYS = 128
 CELLS = RY * RX
 EPSILON = 1e-06
 SCALE = 1.0 / math.sqrt(HD)
 EXP2_SCALE = SCALE * math.log2(math.e)
-AHEAD = 2
+AHEAD = 3
 
 f32 = jnp.float32
 bf16 = jnp.bfloat16
@@ -85,6 +86,7 @@
 
 def pick_kernel(table_ref, ids_ref, out_ref):
     names = table_ref.shape[0]
+    width = out_ref.shape[2]
     blocks, sources = ids_ref.shape
     group = 256 // blocks
     lane = lax.broadcasted_iota(jnp.int32, (blocks, names), 1)
@@ -93,14 +95,13 @@
             jnp.where(lane == ids_ref[:, g + k : g + k + 1], 1.0, 0.0).astype(bf16)
             for k in range(group)
         ]
-        rows = mm(jnp.concatenate(hot, axis=0), table_ref[...]).astype(bf16)
+        rows = mm(jnp.concatenate(hot, axis=0), table_ref[:, :width]).astype(bf16)
         for k in range(group):
             out_ref[g + k] = rows[k * blocks : (k + 1) * blocks]
 
 
-def pick(table, ids):
+def pick(table, ids, width):
     blocks, sources = ids.shape
-    width = table.shape[1]
     return pl.pallas_call(
         pick_kernel,
         out_shape=jax.ShapeDtypeStruct((sources, blocks, width), bf16),
@@ -144,88 +145,115 @@
 
 
 def attend_kernel(base, live, wq, wq_t, wkv, wkv_t, wo, wo_t, grads_in, slots, xs, cots, *rest):
-    outs, tgrads, hgrads, grads_ref, hbuf, xbuf, cbuf, obuf, tbuf, gbuf, in_sems, out_sems = rest[-12:]
+    outs, tgrads, hgrads, grads_ref = rest[-19:-15]
+    hbuf, xbuf, cbuf, obuf, tbuf, gbuf = rest[-15:-9]
+    kvs, kvts, qts, dts, att_s, qg_s, kvg_s, in_sems, out_sems = rest[-9:]
     steps = slots.shape[0] // 2
     slices = slots.shape[1]
 
-    def loads(i, slot):
+    def loads(i):
         blocks = pl.ds(base + 2 * i, 2)
+        slot = lax.rem(i, 4)
         return [
             pltpu.make_async_copy(slots.at[pl.ds(2 * i, 2)], hbuf.at[slot], in_sems.at[slot, 0]),
             pltpu.make_async_copy(xs.at[blocks], xbuf.at[slot], in_sems.at[slot, 1]),
             pltpu.make_async_copy(cots.at[blocks], cbuf.at[slot], in_sems.at[slot, 2]),
         ]
 
-    def stores(i, slot):
+    def stores(i):
         blocks = pl.ds(base + 2 * i, 2)
+        slot = lax.rem(i, 2)
         return [
             pltpu.make_async_copy(gbuf.at[slot], hgrads.at[pl.ds(2 * i, 2)], out_sems.at[slot, 0]),
             pltpu.make_async_copy(obuf.at[slot], outs.at[blocks], out_sems.at[slot, 1]),
             pltpu.make_async_copy(tbuf.at[slot], tgrads.at[blocks], out_sems.at[slot, 2]),
         ]
 
-    for c in loads(0, 0):
-        c.start()
-    grads_ref[...] = grads_in[...]
     zero = jnp.zeros((HD, BT), bf16)
-    none = jnp.zeros((2 * HD, 2 * BT), bf16)
 
     def paired(t, p):
-        first = t[2 * HD * p : 2 * HD * p + HD]
-        second = t[2 * HD * p + HD : 2 * HD * p + 2 * HD]
+        top = t[2 * HD * p : 2 * HD * p + HD]
+        low = t[2 * HD * p + HD : 2 * HD * p + 2 * HD]
         return jnp.concatenate(
-            [
-                jnp.concatenate([first, zero], axis=1),
-                jnp.concatenate([zero, second], axis=1),
-            ],
-            axis=0,
+            [jnp.concatenate([top, zero], axis=1), jnp.concatenate([zero, low], axis=1)], axis=0
         )
 
-    def deep(pair, p):
-        return jnp.concatenate([pair, none] if p % 2 == 0 else [none, pair], axis=0)
-
-    @pl.loop(0, steps)
-    def _(i):
-        slot = lax.rem(i, 2)
-
-        @pl.when(i + 1 < steps)
-        def _():
-            for c in loads(i + 1, 1 - slot):
-                c.start()
-
-        for c in loads(i, slot):
-            c.wait()
-
-        @pl.when(i >= 2)
-        def _():
-            for c in stores(i - 2, slot):
-                c.wait()
-
-        live0 = live[0, base + 2 * i]
-        live1 = live[0, base + 2 * i + 1]
-        sliced = hbuf[slot]
-        h = jnp.concatenate(
+    def lives(i):
+        at = base + 2 * jnp.minimum(i, steps - 1)
+        return live[0, at], live[0, at + 1]
+
+    def cells(i):
+        sliced = hbuf[lax.rem(i, 4)]
+        return jnp.concatenate(
             [sliced[u, :, at : at + D] for u in range(2) for at in range(0, sliced.shape[2], D)],
             axis=0,
         )
-        x = xbuf[slot].reshape(2 * BT, D)
-        row = lax.broadcasted_iota(jnp.int32, (2 * BT, D), 0)
-        lane = lax.broadcasted_iota(jnp.int32, (D, 2 * BT), 1)
-        row_live = row < jnp.where(row < BT, live0, live1 + BT)
-        lane_live = lane < jnp.where(lane < BT, live0, live1 + BT)
-        cot = jnp.where(row_live, cbuf[slot].reshape(2 * BT, D).astype(f32), 0.0).astype(bf16)
-        kv = mm(h, wkv[...]).astype(bf16)
-        kv_t = mm_nt(wkv_t[...], h).astype(bf16)
-        q_t = mm_nt(wq_t[...], x).astype(bf16)
-        d_t = mm_nt(wo[...], cot).astype(bf16)
+
+    def rows_of(buf, i):
+        return buf[lax.rem(i, 4)].reshape(2 * BT, D)
+
+    def head(i):
+        slot = lax.rem(i, 2)
+
+        def keys():
+            kvs[slot] = mm(cells(i), wkv[...]).astype(bf16)
+
+        def keys_t():
+            kvts[slot] = mm_nt(wkv_t[...], cells(i)).astype(bf16)
+
+        def queries():
+            qts[slot] = mm_nt(wq_t[...], rows_of(xbuf, i)).astype(bf16)
+
+        def cotangents():
+            live0, live1 = lives(i)
+            row = lax.broadcasted_iota(jnp.int32, (2 * BT, D), 0)
+            row_live = row < jnp.where(row < BT, live0, live1 + BT)
+            cot = jnp.where(row_live, rows_of(cbuf, i).astype(f32), 0.0).astype(bf16)
+            cbuf[lax.rem(i, 4)] = cot.reshape(2, BT, D)
+            dts[slot] = mm_nt(wo[...], cot).astype(bf16)
+
+        return [cotangents, queries, keys, keys_t]
+
+    def tail(i):
+        slot = lax.rem(i + 2, 2)
+
+        def mixed():
+            live0, live1 = lives(i)
+            lane = lax.broadcasted_iota(jnp.int32, (D, 2 * BT), 1)
+            lane_live = lane < jnp.where(lane < BT, live0, live1 + BT)
+            out = jnp.where(lane_live, mm(wo_t[...], att_s[...]), 0.0)
+            obuf[slot] = out.T.astype(bf16).reshape(2, BT, D)
+
+        def token_grad():
+            tbuf[slot] = mm(wq[...], qg_s[...]).T.astype(bf16).reshape(2, BT, D)
+
+        def hidden_grad():
+            back = mm(wkv[...], kvg_s[...]).astype(bf16)
+            for u in range(2):
+                gbuf[slot, u] = jnp.concatenate(
+                    [back[at : at + slices, u * BT : u * BT + BT] for at in range(0, D, slices)],
+                    axis=1,
+                )
+
+        def weight_grads():
+            grads_ref[0:256] += mm(qg_s[...], rows_of(xbuf, i + 4))
+            grads_ref[256:768] += mm(kvg_s[...], cells(i + 4))
+            grads_ref[768:1024] += mm(att_s[...], rows_of(cbuf, i + 4))
+
+        return [hidden_grad, mixed, token_grad, weight_grads]
+
+    def attention(i, between):
+        slot = lax.rem(i, 2)
+        kv, kv_t, q_t, d_t = kvs[slot], kvts[slot], qts[slot], dts[slot]
         att_rows, qg_rows, kg_rows, vg_rows = [[], []], [[], []], [[], []], [[], []]
+
         def first(p, u):
             rows = slice(u * BT, u * BT + BT)
-            half = 128 * (p // 2)
+            at = 2 * HD * p
             q2 = paired(q_t[:, rows], p)
             d2 = paired(d_t[:, rows], p)
-            scores = mm(kv[rows, half : half + 128], deep(q2, p))
-            wg = mm(kv[rows, D + half : D + half + 128], deep(d2, p))
+            scores = mm(kv[rows, at : at + 2 * HD], q2)
+            wg = mm(kv[rows, D + at : D + at + 2 * HD], d2)
             return q2, d2, scores, wg
 
         def second(q2, d2, scores, wg):
@@ -249,37 +277,73 @@
 
         units = [(p, u) for p in range(HEADS // 2) for u in range(2)]
         ready, soft = {}, {}
+        between = list(between)
         for k in range(len(units) + AHEAD + 1):
             if k < len(units):
                 ready[k] = first(*units[k])
+            if between and k >= 1:
+                between.pop(0)()
             j = k - AHEAD
             if 0 <= j < len(units):
                 soft[j] = second(*ready.pop(j))
             if 0 <= j - 1 < len(units):
                 third(*units[j - 1], *soft.pop(j - 1))
+        for piece in between:
+            piece()
 
         def joined(rows):
             return jnp.concatenate([jnp.concatenate(r, axis=0) for r in rows], axis=1)
 
-        att_t = joined(att_rows).astype(bf16)
-        qg_t = (joined(qg_rows) * SCALE).astype(bf16)
-        kvg_t = joined([kg_rows[u] + vg_rows[u] for u in range(2)]).astype(bf16)
-        mixed = jnp.where(lane_live, mm(wo_t[...], att_t), 0.0)
-        obuf[slot] = mixed.T.astype(bf16).reshape(2, BT, D)
-        tbuf[slot] = mm(wq[...], qg_t).T.astype(bf16).reshape(2, BT, D)
-        back = mm(wkv[...], kvg_t).astype(bf16)
-        for u in range(2):
-            gbuf[slot, u] = jnp.concatenate(
-                [back[at : at + slices, u * BT : u * BT + BT] for at in range(0, D, slices)], axis=1
-            )
-        grads_ref[0:256] += mm(qg_t, x)
-        grads_ref[256:768] += mm(kvg_t, h)
-        grads_ref[768:1024] += mm(att_t, cot)
-        for c in stores(i, slot):
-            c.start()
-
-    for i in range(max(0, steps - 2), steps):
-        for c in stores(i, i % 2):
+        att_s[...] = joined(att_rows).astype(bf16)
+        qg_s[...] = (joined(qg_rows) * SCALE).astype(bf16)
+        kvg_s[...] = joined([kg_rows[u] + vg_rows[u] for u in range(2)]).astype(bf16)
+
+    for c in loads(0):
+        c.start()
+    for c in loads(1):
+        c.start()
+    grads_ref[...] = grads_in[...]
+    for ref in (att_s, qg_s, kvg_s):
+        ref[...] = jnp.zeros_like(ref)
+    for ref in (hbuf, xbuf, cbuf):
+        ref[3] = jnp.zeros(ref.shape[1:], bf16)
+    for c in loads(0):
+        c.wait()
+    for piece in head(0):
+        piece()
+
+    @pl.loop(0, steps)
+    def _(i):
+        @pl.when(i + 2 < steps)
+        def _():
+            for c in loads(i + 2):
+                c.start()
+
+        @pl.when(i + 1 < steps)
+        def _():
+            for c in loads(i + 1):
+                c.wait()
+
+        @pl.when(i >= 3)
+        def _():
+            for c in stores(i - 3):
+                c.wait()
+
+        attention(i, [piece for two in zip(tail(i - 1), head(i + 1)) for piece in two])
+
+        @pl.when(i >= 1)
+        def _():
+            for c in stores(i - 1):
+                c.start()
+
+    for c in stores(steps - 3):
+        c.wait()
+    for piece in tail(steps - 1):
+        piece()
+    for c in stores(steps - 1):
+        c.start()
+    for i in (steps - 2, steps - 1):
+        for c in stores(i):
             c.wait()
 
 
@@ -287,8 +351,6 @@
     args = [live, *weights, grads, slots, x, cot, *kept]
     first_kept = len(args) - len(kept)
     token_shape = jax.ShapeDtypeStruct(x.shape, bf16)
-    sliced = pltpu.VMEM((2, 2) + slots.shape[1:], bf16)
-    pair = pltpu.VMEM((2, 2, BT, D), bf16)
     return pl.pallas_call(
         functools.partial(attend_kernel, base),
         out_shape=(
@@ -302,13 +364,20 @@
         + [HBM] * (3 + len(kept)),
         out_specs=(HBM, HBM, HBM, VMEM),
         scratch_shapes=[
-            sliced,
-            pair,
-            pair,
-            pair,
-            pair,
-            sliced,
-            pltpu.SemaphoreType.DMA((2, 3)),
+            pltpu.VMEM((4, 2) + slots.shape[1:], bf16),
+            pltpu.VMEM((4, 2, BT, D), bf16),
+            pltpu.VMEM((4, 2, BT, D), bf16),
+            pltpu.VMEM((2, 2, BT, D), bf16),
+            pltpu.VMEM((2, 2, BT, D), bf16),
+            pltpu.VMEM((2, 2) + slots.shape[1:], bf16),
+            pltpu.VMEM((2, 2 * KEYS, 2 * D), bf16),
+            pltpu.VMEM((2, 2 * D, 2 * KEYS), bf16),
+            pltpu.VMEM((2, D, 2 * BT), bf16),
+            pltpu.VMEM((2, D, 2 * BT), bf16),
+            pltpu.VMEM((D, 2 * BT), bf16),
+            pltpu.VMEM((D, 2 * BT), bf16),
+            pltpu.VMEM((2 * D, 2 * KEYS), bf16),
+            pltpu.SemaphoreType.DMA((4, 3)),
             pltpu.SemaphoreType.DMA((2, 3)),
         ],
         input_output_aliases={first_kept + j: j for j in range(len(kept))},
@@ -324,9 +393,17 @@
 
 def finish_kernel(slices_ref, shifts_ref, grads_ref, hgrad_ref, sums_ref, back_t):
     slices = slices_ref.shape[1]
-    sums_ref[0 : 4 * D] = grads_ref[...].astype(bf16)
-    if sums_ref.shape[0] > 13 * D:
-        sums_ref[13 * D :] = jnp.zeros((sums_ref.shape[0] - 13 * D, D), bf16)
+    used = 13 * D * D // LANES
+
+    def put(k, grad):
+        for j, at in enumerate(range(0, D, LANES)):
+            row = (k * (D // LANES) + j) * D
+            sums_ref[row : row + D] = grad[:, at : at + LANES].astype(bf16)
+
+    for k in range(4):
+        put(k, grads_ref[k * D : (k + 1) * D])
+    if sums_ref.shape[0] > used:
+        sums_ref[used:] = jnp.zeros((sums_ref.shape[0] - used, LANES), bf16)
     for s in range(SUB):
         cells = slice(s * KEYS, (s + 1) * KEYS)
         part = jnp.concatenate(
@@ -336,10 +413,7 @@
         hgrad_ref[cells, :] = part.astype(f32).T.astype(bf16)
     for a in range(3):
         for b in range(3):
-            at = (4 + 3 * a + b) * D
-            sums_ref[at : at + D] = mm(
-                back_t[...], shifts_ref[b, a * RX : a * RX + CELLS, :]
-            ).astype(bf16)
+            put(4 + 3 * a + b, mm(back_t[...], shifts_ref[b, a * RX : a * RX + CELLS, :]))
 
 
 def finish(slices, shifts, grads, rows):
@@ -347,7 +421,7 @@
         finish_kernel,
         out_shape=(
             jax.ShapeDtypeStruct((CELLS, D), bf16),
-            jax.ShapeDtypeStruct((rows, D), bf16),
+            jax.ShapeDtypeStruct((rows, LANES), bf16),
         ),
         in_specs=[VMEM] * 3,
         out_specs=(VMEM, VMEM),
@@ -362,7 +436,8 @@
 
 def normalize_kernel(sums_ref, query_ref, key_ref, value_ref, out_ref, conv_ref):
     def part(k):
-        return sums_ref[k * D : (k + 1) * D, :].astype(f32)
+        rows = [(k * (D // LANES) + j) * D for j in range(D // LANES)]
+        return jnp.concatenate([sums_ref[r : r + D].astype(f32) for r in rows], axis=1)
 
     def squares(k):
         item = part(k)
@@ -428,15 +503,22 @@
     nblocks = tokens.shape[1] // BT
 
     sub = jnp.sum(sub_masks[0] * jnp.arange(SUB, dtype=jnp.int32)[None, :], axis=1)
-    own = targets[0, :, 0] * SUB + sub
-    ids = exchange(jnp.broadcast_to(own[None, :], (ntile, nblocks)))
+    names = jnp.concatenate([targets[0, :, 0], sub]).astype(bf16)
+    names = jnp.pad(names[None], ((0, SUB - 1), (0, 0)))
 
     field = grid[0]
     above = turned(ring(field[-1], 1), turns[0])
     below = turned(ring(field[0], -1), turns[1])
     rimmed = jnp.concatenate([above[None], field, below[None]], axis=0).reshape(-1, D)
     sliced, shifts = hidden_slices(rimmed, w_conv.reshape(9, D, D), ntile)
-    table = exchange(sliced.transpose(1, 0, 2)).reshape(ntile * SUB, -1)
+    width = sliced.shape[2]
+    sliced = jnp.concatenate(
+        [sliced.transpose(1, 0, 2), jnp.broadcast_to(names[None], (ntile,) + names.shape)], axis=2
+    )
+    table = exchange(sliced)
+    ids = table[:, 0, width:].astype(jnp.int32)
+    ids = ids[:, :nblocks] * SUB + ids[:, nblocks:]
+    table = table.reshape(ntile * SUB, -1)
 
     wkv = jnp.concatenate([w_key, w_value], axis=1)
     weights = (w_query, w_query.T, wkv, wkv.T, w_out, w_out.T)
@@ -444,7 +526,7 @@
     cot = token_cotan[0].reshape(nblocks, BT, D)
     half = nblocks // 2
     grads = jnp.zeros((4 * D, D), f32)
-    got = [exchange(pick(table, ids[:, c * half : (c + 1) * half].T)) for c in range(2)]
+    got = [exchange(pick(table, ids[:, c * half : (c + 1) * half].T, width)) for c in range(2)]
     kept, returned = (), []
     for c in range(2):
         token_out, token_grad, back, grads = attend(
@@ -456,13 +538,11 @@
     acc = gather(rows[0], returned[0], ntile * SUB, (), f32)
     home = gather(rows[1], returned[1], ntile * SUB, (acc,), bf16)
     home = exchange(home.reshape(ntile, SUB, -1)).transpose(1, 0, 2)
-    each = -(-13 * D // (16 * ndev)) * 16
+    each = -(-13 * D * D // LANES // (8 * ndev)) * 8
     hidden_back, sums = finish(home, shifts, grads, ndev * each)
 
-    parts = exchange(sums, ("tile", "win")).reshape(ndev, -1, D)
+    parts = exchange(sums.reshape(ndev, -1, LANES), ("tile", "win"))
     share = jnp.sum(parts.astype(f32), axis=0).astype(bf16)
-    spread = jnp.broadcast_to(share[None], (ndev,) + share.shape).reshape(-1, D)
-    updates = normalize(exchange(spread, ("tile", "win")))
 
     hidden_back = hidden_back.reshape(RY, RX, D)
     padded = jnp.pad(hidden_back, ((0, 0), (1, 1), (0, 0)))
@@ -479,6 +559,9 @@
     field_grad = field_grad + jnp.concatenate([taps[0][1:], from_below[None]], axis=0)
     field_grad = field_grad + jnp.concatenate([from_above[None], taps[2][:-1]], axis=0)
     grid_grad = field_grad.astype(bf16)[None]
+    share, grid_grad = lax.optimization_barrier((share, grid_grad))
+    spread = jnp.broadcast_to(share[None], (ndev,) + share.shape)
+    updates = normalize(exchange(spread, ("tile", "win")).reshape(-1, LANES))
 
     return (
         token_out.reshape(1, -1, D),

time: 334 us -> 314 us (0.940)
  blocking collectives: 18.9 us -> 68.8 us
  waiting for transfers between devices: 89.9 us -> 50.2 us
  starting transfers between devices: 78.6 us -> 58.1 us
  local copies, waits for them, and re-layouts: 33.7 us -> 26.9 us
  Pallas kernels: 91.1 us -> 86 us
    all_to_all x1 -> x3, blocking collectives: 18.9 us -> 68.8 us  [exchange(): return lax.all_to_all(value, axes, split_axis=0, concat_axis=0, tiled=True)]
    all_to_all x8 -> x5, waiting for transfers between devices: 75.3 us -> 39.5 us  [exchange(): return lax.all_to_all(value, axes, split_axis=0, concat_axis=0, tiled=True)]
    all_to_all x8 -> x5, starting transfers between devices: 63.8 us -> 41 us  [exchange(): return lax.all_to_all(value, axes, split_axis=0, concat_axis=0, tiled=True)]
    pallas_call x2, Pallas kernels: 62.6 us -> 57.3 us  [attend(): pl.pallas_call(functools.partial(attend_kernel, base), out_shape=(token_s...]
    ppermute x4, waiting for transfers between devices: 14.6 us -> 10.7 us  [ring(): lax.ppermute(value, 'tile', [(i, (i + by) % length) for i in range(length)])]
    unnamed x24 -> x23, local copies, waits for them, and re-layouts: 7.15 us -> 4.13 us
    all_to_all x4 -> x3, local copies, waits for them, and re-layouts: 7.57 us -> 7.5 us  [exchange(): return lax.all_to_all(value, axes, split_axis=0, concat_axis=0, tiled=True)]
  transfers between devices with their start and end apart: 12 -> 9, of which waited for: 6 -> 4; matrix products, arithmetic and copies ran while one was open for 12% -> 11% of each run, Pallas kernels for 22% -> 21%
where the time goes in v4:
time: 314 us; the launch traced here: 312 us
  Pallas kernels  86 us (27%)
  blocking collectives  68.8 us (22%)
  starting transfers between devices  58.1 us (19%)
  waiting for transfers between devices  50.2 us (16%)
  local copies, waits for them, and re-layouts  26.9 us (9%)
  matrix products  13.7 us (4%)
  other arithmetic  6.33 us (2%)
    all_to_all x3, blocking collectives, exchange(): return lax.all_to_all(value, axes, split_axis=0, concat_axis=0, tiled=True)  68.8 us
    pallas_call x2, Pallas kernels, attend(): pl.pallas_call(functools.partial(attend_kernel, base), out_shape=(token_s...  57.3 us
    all_to_all x5, starting transfers between devices, exchange(): return lax.all_to_all(value, axes, split_axis=0, concat_axis=0, tiled=True)  41 us
    all_to_all x5, waiting for transfers between devices, exchange(): return lax.all_to_all(value, axes, split_axis=0, concat_axis=0, tiled=True)  39.5 us
    ppermute x4, starting transfers between devices, ring(): lax.ppermute(value, 'tile', [(i, (i + by) % length) for i in range(length)])  17.1 us
    dot_general x9, matrix products, mm_nt(): lax.dot_general(a, b, (((1,), (1,)), ((), ())), preferred_element_type=f32)  13.7 us
    ppermute x4, waiting for transfers between devices, ring(): lax.ppermute(value, 'tile', [(i, (i + by) % length) for i in range(length)])  10.7 us
    transpose x2, local copies, waits for them, and re-layouts, local(): returned.append(exchange(back.transpose(1, 0, 2)).reshape(ntile * half, -1))  8.18 us
  transfers between devices with their start and end apart: 9, of which 4 were waited for; matrix products, arithmetic and copies ran while one was open for 11% of the time, Pallas kernels for 21%

profile of v4, /device:TPU:1, one launch (start us, length us, event | category | flops | bytes accessed | tf_op | source)
XLA Modules:
  0.0 312.3 jit_solution(11473113608066479077)
XLA Ops:
  0.6 0.7 slice_bitcast_fusion.3
  1.4 2.1 collective-permute-start
  3.5 7.1 %collective-permute-start.1 = (bf16[32,256]{1,0:T(8,128)(2,1)S(1)}, bf16[32,256]{1,0:T(8,128)(2,1)S(1)}, u32[]{:S(2)}, u32[]{:S(2)}) collective-permute-start(bf16[32,256]{1,0:T(8,128)(2,1)S(1)} %get-tuple-element.47), channel_id=1, source_target_pairs={{0,126},{2,0},{4,2},{6,4},{8,6},{10,8},{12,10},{14,12},{16,14},{18... | collective-permute-start | bytes 49160 | tf_op jit(solution)/shard_map/ppermute | solution.py:475
  10.6 0.7 convert_bitcast_fusion.1
  11.3 0.7 fusion.27
  12.0 1.3 fusion.37
  14.7 0.1 rev.12
  14.8 0.1 rev.13
  14.9 1.9 pad_maximum_fusion.1
  16.8 4.6 %conv_slices.1 = (bf16[8,64,512]{2,1,0:T(8,128)(2,1)}, bf16[3,1088,256]{2,1,0:T(8,128)(2,1)}) custom-call(bf16[1088,256]{1,0:T(8,128)(2,1)} %bitcast.136, bf16[9,256,256]{2,1,0:T(8,128)(2,1)} %bitcast.132), custom_call_target="tpu_custom_call" | custom-call | flops 1207959552 | bytes 6000000 | tf_op jit(solution)/shard_map/conv_slices/pallas_call | solution.py:71
  21.4 1.1 pad_maximum_fusion
  22.5 0.4 copy.54
  22.9 17.9 %all_to_all.40 = bf16[64,8,640]{2,1,0:T(8,128)(2,1)S(1)} all-to-all(bf16[64,8,640]{2,1,0:T(8,128)(2,1)S(1)} %copy.54), channel_id=1, replica_groups=mesh['tile'=64,'win'=2] {'tile'}, dimensions={0} | all-to-all | bytes 1310720 | tf_op jit(solution)/shard_map/all_to_all | solution.py:483
  40.8 0.1 copy.65
  41.0 0.6 fusion.36
  41.6 3.7 %pick.2 = bf16[64,32,512]{2,1,0:T(8,128)(2,1)} custom-call(bf16[512,640]{1,0:T(8,128)(2,1)} %bitcast.133, s32[32,64]{1,0:T(8,128)} %get-tuple-element.51.ids_ref), custom_call_target="tpu_custom_call" | custom-call | flops 1342177280 | bytes 4000000 | tf_op jit(solution)/shard_map/pick/pallas_call | solution.py:105
  45.4 6.1 %all-to-all-start.1 = ((bf16[64,32,512]{2,1,0:T(8,128)(2,1)}), bf16[64,32,512]{2,1,0:T(8,128)(2,1)S(1)}, u32[]{:S(2)}, u32[]{:S(2)}) async-start(bf16[64,32,512]{2,1,0:T(8,128)(2,1)} %pick.2), calls=%async_computation.1 | async-start | bytes 4194304 | tf_op jit(solution)/shard_map/all_to_all | solution.py:483
  51.4 0.1 copy.51
  51.6 0.1 copy.52
  51.7 0.8 copy.50
  52.4 0.8 copy.53
  53.2 0.7 fusion.35
  53.9 0.8 copy.59.wkv
  54.8 3.7 %pick.3 = bf16[64,32,512]{2,1,0:T(8,128)(2,1)} custom-call(bf16[512,640]{1,0:T(8,128)(2,1)} %bitcast.134, s32[32,64]{1,0:T(8,128)} %get-tuple-element.52.ids_ref), custom_call_target="tpu_custom_call" | custom-call | flops 1342177280 | bytes 4000000 | tf_op jit(solution)/shard_map/pick/pallas_call | solution.py:105
  58.5 19.5 %all-to-all-done.1 = bf16[64,32,512]{2,1,0:T(8,128)(2,1)S(1)} async-done(((bf16[64,32,512]{2,1,0:T(8,128)(2,1)}), bf16[64,32,512]{2,1,0:T(8,128)(2,1)S(1)}, u32[]{:S(2)}, u32[]{:S(2)}) %all-to-all-start.1) | async-done | bytes 2097184 | tf_op jit(solution)/shard_map/all_to_all | solution.py:483
  77.9 8.4 %all-to-all-start.2 = ((bf16[64,32,512]{2,1,0:T(8,128)(2,1)}), bf16[64,32,512]{2,1,0:T(8,128)(2,1)}, u32[]{:S(2)}, u32[]{:S(2)}) async-start(bf16[64,32,512]{2,1,0:T(8,128)(2,1)} %pick.3), calls=%async_computation.2 | async-start | bytes 4194304 | tf_op jit(solution)/shard_map/all_to_all | solution.py:483
  86.4 2.5 copy.70
  88.9 1.1 broadcast_in_dim.32.grads_in
  89.9 28.7 %attend.2 = (bf16[64,128,256]{2,1,0:T(8,128)(2,1)}, bf16[64,128,256]{2,1,0:T(8,128)(2,1)}, bf16[32,64,512]{2,1,0:T(8,128)(2,1)}, f32[1024,256]{1,0:T(8,128)}) custom-call(s32[1,64]{1,0:T(1,128)} %live.3, bf16[256,256]{1,0:T(8,128)(2,1)} %wq.3, bf16[256,256]{1,0:T(8,128)(2,1)} %bitcast.140, bf16[256,512]{1,0:T(8,128)(2,1)} %copy.59.wkv, ...), custom_call_target="tpu_custom_call" | custom-call | flops 25600000000 | bytes 25600000 | tf_op jit(solution)/shard_map/attend/pallas_call | solution.py:354
  118.6 4.1 %copy.63 = bf16[64,32,512]{2,1,0:T(8,128)(2,1)} copy(bf16[64,32,512]{2,0,1:T(8,128)(2,1)} %bitcast.130) | data formatting | bytes 4194304 | tf_op jit(solution)/shard_map/transpose | solution.py:536
  122.7 9.5 %all-to-all-start.4 = ((bf16[64,32,512]{2,1,0:T(8,128)(2,1)}), bf16[64,32,512]{2,1,0:T(8,128)(2,1)S(1)}, u32[]{:S(2)}, u32[]{:S(2)}) async-start(bf16[64,32,512]{2,1,0:T(8,128)(2,1)} %copy.63), calls=%async_computation.4 | async-start | bytes 4194304 | tf_op jit(solution)/shard_map/all_to_all | solution.py:483
  132.3 4.1 %copy.69 = bf16[64,32,512]{2,0,1:T(8,128)(2,1)} copy(bf16[64,32,512]{2,1,0:T(8,128)(2,1)} %all-to-all-done.2) | data formatting | bytes 4194304 | tf_op jit(solution)/shard_map/all_to_all | solution.py:483
  136.3 28.6 %attend.3 = (bf16[64,128,256]{2,1,0:T(8,128)(2,1)}, bf16[64,128,256]{2,1,0:T(8,128)(2,1)}, bf16[32,64,512]{2,1,0:T(8,128)(2,1)}, f32[1024,256]{1,0:T(8,128)}) custom-call(s32[1,64]{1,0:T(1,128)} %live.3, bf16[256,256]{1,0:T(8,128)(2,1)} %wq.3, bf16[256,256]{1,0:T(8,128)(2,1)} %bitcast.141, ...), custom_call_target="tpu_custom_call", output_to_operand_aliasing={{0}: (11, {}), {1}: (12, {})} | custom-call | flops 25600000000 | bytes 25600000 | tf_op jit(solution)/shard_map/attend/pallas_call | solution.py:354
  165.0 4.1 %copy.61 = bf16[64,32,512]{2,1,0:T(8,128)(2,1)} copy(bf16[64,32,512]{2,0,1:T(8,128)(2,1)} %bitcast.128) | data formatting | bytes 4194304 | tf_op jit(solution)/shard_map/transpose | solution.py:536
  169.1 1.3 copy-done.3
  170.4 10.3 %all-to-all-start.3 = ((bf16[64,32,512]{2,1,0:T(8,128)(2,1)}), bf16[64,32,512]{2,1,0:T(8,128)(2,1)}, u32[]{:S(2)}, u32[]{:S(2)}) async-start(bf16[64,32,512]{2,1,0:T(8,128)(2,1)} %copy.61), calls=%async_computation.3 | async-start | bytes 4194304 | tf_op jit(solution)/shard_map/all_to_all | solution.py:483
  180.6 0.1 copy.62
  180.7 0.7 reshape.147.ids_ref
  181.5 0.7 reshape.145.ids_ref
  182.2 3.9 %gather.2.rest_0_ = f32[512,512]{1,0:T(8,128)} custom-call(s32[1,2048]{1,0:T(1,128)} %reshape.147.ids_ref, bf16[2048,512]{1,0:T(8,128)(2,1)} %bitcast.126), custom_call_target="tpu_custom_call" | custom-call | flops 1073741824 | bytes 4000000 | tf_op jit(solution)/shard_map/gather/pallas_call | solution.py:134
  186.1 20.1 %all-to-all-done.3 = bf16[64,32,512]{2,1,0:T(8,128)(2,1)} async-done(((bf16[64,32,512]{2,1,0:T(8,128)(2,1)}), bf16[64,32,512]{2,1,0:T(8,128)(2,1)}, u32[]{:S(2)}, u32[]{:S(2)}) %all-to-all-start.3) | async-done | bytes 2097184 | tf_op jit(solution)/shard_map/all_to_all | solution.py:483
  206.2 3.9 %gather.3 = bf16[512,512]{1,0:T(8,128)(2,1)} custom-call(s32[1,2048]{1,0:T(1,128)} %reshape.145.ids_ref, bf16[2048,512]{1,0:T(8,128)(2,1)} %bitcast.28.slots_ref, f32[512,512]{1,0:T(8,128)} %gather.2.rest_0_), custom_call_target="tpu_custom_call" | custom-call | flops 1073741824 | bytes 4000000 | tf_op jit(solution)/shard_map/gather/pallas_call | solution.py:134
  210.1 19.0 %all_to_all.41 = bf16[64,8,512]{2,1,0:T(8,128)(2,1)S(1)} all-to-all(bf16[64,8,512]{2,1,0:T(8,128)(2,1)} %bitcast.139), channel_id=1, replica_groups=mesh['tile'=64,'win'=2] {'tile'}, dimensions={0} | all-to-all | bytes 1048576 | tf_op jit(solution)/shard_map/all_to_all | solution.py:483
  229.1 0.9 copy.71
  230.1 4.7 %finish.1 = (bf16[1024,256]{1,0:T(8,128)(2,1)}, bf16[7168,128]{1,0:T(8,128)(2,1)}) custom-call(bf16[8,64,512]{2,1,0:T(8,128)(2,1)} %bitcast.137, bf16[3,1088,256]{2,1,0:T(8,128)(2,1)} %get-tuple-element.35.shifts_ref, f32[1024,256]{1,0:T(8,128)} %get-tuple-element.36.grads_ref), custom_call_target="tpu_custom_call" | custom-call | flops 1207959552 | bytes 6000000 | tf_op jit(solution)/shard_map/finish/pallas_call | solution.py:420
  234.7 1.5 fusion.5
  236.2 2.2 fusion.4
  238.4 6.7 %all-to-all-start.6 = ((bf16[128,56,128]{2,1,0:T(8,128)(2,1)}), bf16[128,56,128]{2,1,0:T(8,128)(2,1)S(1)}, u32[]{:S(2)}, u32[]{:S(2)}) async-start(bf16[128,56,128]{2,1,0:T(8,128)(2,1)} %bitcast.131), calls=%async_computation.6 | async-start | bytes 3670016 | tf_op jit(solution)/shard_map/all_to_all | solution.py:483
  245.1 1.2 convolution_add_fusion.3
  246.4 1.3 convolution_add_fusion.2
  247.7 7.9 %collective-permute-start.2 = (f32[32,256]{1,0:T(8,128)S(1)}, f32[32,256]{1,0:T(8,128)S(1)}, u32[]{:S(2)}, u32[]{:S(2)}) collective-permute-start(f32[32,256]{1,0:T(8,128)S(1)} %broadcast_select_fusion.1), channel_id=1, source_target_pairs={{0,126},{2,0},{4,2},{6,4},{8,6},{10,8},{12,10},{14,12},{16,14},{18... | collective-permute-start | bytes 98312 | tf_op jit(solution)/shard_map/ppermute | solution.py:475
  255.6 1.6 convolution_add_fusion.1
  257.3 1.3 convolution_add_fusion
  258.5 1.0 copy-done.2
  259.6 0.8 broadcast_select_fusion
  260.3 1.2 fusion.6
  261.6 1.2 convolution_add_fusion.5
  262.8 0.7 collective-permute-done.2
  263.5 10.0 %collective-permute-done.3 = f32[32,256]{1,0:T(8,128)S(1)} collective-permute-done((f32[32,256]{1,0:T(8,128)S(1)}, f32[32,256]{1,0:T(8,128)S(1)}, u32[]{:S(2)}, u32[]{:S(2)}) %collective-permute-start.3) | collective-permute-done | bytes 32800 | tf_op jit(solution)/shard_map/ppermute | solution.py:475
  273.5 2.1 fusion.3
  275.7 0.3 reduce_sum.22
  276.0 0.2 broadcast_in_dim.39
  276.2 31.9 %all_to_all.42 = bf16[128,56,128]{2,1,0:T(8,128)(2,1)} all-to-all(bf16[128,56,128]{2,1,0:T(8,128)(2,1)S(1)} %broadcast_in_dim.39), channel_id=1, replica_groups=mesh['tile'=64,'win'=2] {'tile','win'}, dimensions={0} | all-to-all | bytes 3670016 | tf_op jit(solution)/shard_map/all_to_all | solution.py:483
  308.1 4.2 %normalize.1 = (f32[256,256]{1,0:T(8,128)}, f32[256,256]{1,0:T(8,128)}, f32[256,256]{1,0:T(8,128)}, f32[256,256]{1,0:T(8,128)}, f32[9,256,256]{2,1,0:T(8,128)}) custom-call(bf16[7168,128]{1,0:T(8,128)(2,1)} %bitcast.125), custom_call_target="tpu_custom_call" | custom-call | flops 4000000 | bytes 6000000 | tf_op jit(solution)/shard_map/normalize/pallas_call | solution.py:462
  (40 shorter events, 0.4 us)
Async XLA Ops:
  1.4 13.3 %collective-permute-start = (bf16[32,256]{1,0:T(8,128)(2,1)S(1)}, bf16[32,256]{1,0:T(8,128)(2,1)S(1)}, u32[]{:S(2)}, u32[]{:S(2)}) collective-permute-start(bf16[32,256]{1,0:T(8,128)(2,1)S(1)} %get-tuple-element.46), channel_id=1, source_target_pairs={{0,2},{2,4},{4,6},{6,8},{8,10},{10,12},{12,14},{14,16},{16,18},{18... | collective-permute-start | bytes 49160 | tf_op jit(solution)/shard_map/ppermute | solution.py:475
  3.5 11.3 %collective-permute-start.1 = (bf16[32,256]{1,0:T(8,128)(2,1)S(1)}, bf16[32,256]{1,0:T(8,128)(2,1)S(1)}, u32[]{:S(2)}, u32[]{:S(2)}) collective-permute-start(bf16[32,256]{1,0:T(8,128)(2,1)S(1)} %get-tuple-element.47), channel_id=1, source_target_pairs={{0,126},{2,0},{4,2},{6,4},{8,6},{10,8},{12,10},{14,12},{16,14},{18... | collective-permute-start | bytes 49160 | tf_op jit(solution)/shard_map/ppermute | solution.py:475
  40.8 0.8 copy-start.4
  45.4 6.1 %copy-start.5 = (bf16[256,256]{1,0:T(8,128)(2,1)S(1)}, bf16[256,256]{1,0:T(8,128)(2,1)}, u32[]{:S(2)}) copy-start(bf16[256,256]{1,0:T(8,128)(2,1)} %param.19) | copy-start | bytes 393220
  45.4 6.2 %copy-start.6 = (bf16[256,256]{1,0:T(8,128)(2,1)S(1)}, bf16[256,256]{1,0:T(8,128)(2,1)}, u32[]{:S(2)}) copy-start(bf16[256,256]{1,0:T(8,128)(2,1)} %param.20) | copy-start | bytes 393220
  45.4 6.3 %copy-start.7 = (bf16[256,256]{1,0:T(8,128)(2,1)S(1)}, bf16[256,256]{1,0:T(8,128)(2,1)}, u32[]{:S(2)}) copy-start(bf16[256,256]{1,0:T(8,128)(2,1)} %wq.3) | copy-start | bytes 393220
  45.4 7.1 %copy-start.8 = (bf16[256,256]{1,0:T(8,128)(2,1)S(1)}, bf16[256,256]{1,0:T(8,128)(2,1)}, u32[]{:S(2)}) copy-start(bf16[256,256]{1,0:T(8,128)(2,1)} %wo.3) | copy-start | bytes 393220
  45.4 32.6 %all-to-all-start.1 = ((bf16[64,32,512]{2,1,0:T(8,128)(2,1)}), bf16[64,32,512]{2,1,0:T(8,128)(2,1)S(1)}, u32[]{:S(2)}, u32[]{:S(2)}) async-start(bf16[64,32,512]{2,1,0:T(8,128)(2,1)} %pick.2), calls=%async_computation.1 | async-start | bytes 4194304 | tf_op jit(solution)/shard_map/all_to_all | solution.py:483
  77.9 44.8 %all-to-all-start.2 = ((bf16[64,32,512]{2,1,0:T(8,128)(2,1)}), bf16[64,32,512]{2,1,0:T(8,128)(2,1)}, u32[]{:S(2)}, u32[]{:S(2)}) async-start(bf16[64,32,512]{2,1,0:T(8,128)(2,1)} %pick.3), calls=%async_computation.2 | async-start | bytes 4194304 | tf_op jit(solution)/shard_map/all_to_all | solution.py:483
  122.7 46.3 %all-to-all-start.4 = ((bf16[64,32,512]{2,1,0:T(8,128)(2,1)}), bf16[64,32,512]{2,1,0:T(8,128)(2,1)S(1)}, u32[]{:S(2)}, u32[]{:S(2)}) async-start(bf16[64,32,512]{2,1,0:T(8,128)(2,1)} %copy.63), calls=%async_computation.4 | async-start | bytes 4194304 | tf_op jit(solution)/shard_map/all_to_all | solution.py:483
  169.1 1.3 copy-start.3
  170.4 35.8 %all-to-all-start.3 = ((bf16[64,32,512]{2,1,0:T(8,128)(2,1)}), bf16[64,32,512]{2,1,0:T(8,128)(2,1)}, u32[]{:S(2)}, u32[]{:S(2)}) async-start(bf16[64,32,512]{2,1,0:T(8,128)(2,1)} %copy.61), calls=%async_computation.3 | async-start | bytes 4194304 | tf_op jit(solution)/shard_map/all_to_all | solution.py:483
  234.7 1.5 copy-start
  238.4 37.2 %all-to-all-start.6 = ((bf16[128,56,128]{2,1,0:T(8,128)(2,1)}), bf16[128,56,128]{2,1,0:T(8,128)(2,1)S(1)}, u32[]{:S(2)}, u32[]{:S(2)}) async-start(bf16[128,56,128]{2,1,0:T(8,128)(2,1)} %bitcast.131), calls=%async_computation.6 | async-start | bytes 3670016 | tf_op jit(solution)/shard_map/all_to_all | solution.py:483
  247.6 15.2 %copy-start.1 = (f32[32,32,256]{2,1,0:T(8,128)}, f32[32,32,256]{2,1,0:T(8,128)S(1)}, u32[]{:S(2)}) copy-start(f32[32,32,256]{2,1,0:T(8,128)S(1)} %convolution_add_fusion.2) | copy-start | bytes 3145732
  247.7 15.8 %collective-permute-start.2 = (f32[32,256]{1,0:T(8,128)S(1)}, f32[32,256]{1,0:T(8,128)S(1)}, u32[]{:S(2)}, u32[]{:S(2)}) collective-permute-start(f32[32,256]{1,0:T(8,128)S(1)} %broadcast_select_fusion.1), channel_id=1, source_target_pairs={{0,126},{2,0},{4,2},{6,4},{8,6},{10,8},{12,10},{14,12},{16,14},{18... | collective-permute-start | bytes 98312 | tf_op jit(solution)/shard_map/ppermute | solution.py:475
  258.5 1.0 copy-start.2
  260.3 13.2 %collective-permute-start.3 = (f32[32,256]{1,0:T(8,128)S(1)}, f32[32,256]{1,0:T(8,128)S(1)}, u32[]{:S(2)}, u32[]{:S(2)}) collective-permute-start(f32[32,256]{1,0:T(8,128)S(1)} %broadcast_select_fusion), channel_id=1, source_target_pairs={{0,2},{2,4},{4,6},{6,8},{8,10},{10,12},{12,14},{14,16},{16,18},{18... | collective-permute-start | bytes 98312 | tf_op jit(solution)/shard_map/ppermute | solution.py:475
  262.8 10.7 %slice-start.1 = ((f32[32,32,256]{2,1,0:T(8,128)}), f32[31,32,256]{2,1,0:T(8,128)S(1)}, s32[]{:S(2)}) async-start(f32[32,32,256]{2,1,0:T(8,128)} %copy-done.2), calls=%async_computation.9 | async-start | bytes 2031616 | tf_op jit(solution)/shard_map/slice | solution.py:560
  262.8 10.7 %slice-start = ((f32[32,32,256]{2,1,0:T(8,128)}), f32[31,32,256]{2,1,0:T(8,128)S(1)}, s32[]{:S(2)}) async-start(f32[32,32,256]{2,1,0:T(8,128)} %copy-done.1), calls=%async_computation.8 | async-start | bytes 2031616 | tf_op jit(solution)/shard_map/slice | solution.py:559

commit v5 on v4

--- a/solution.py
+++ b/solution.py
@@ -22,6 +22,7 @@
 SCALE = 1.0 / math.sqrt(HD)
 EXP2_SCALE = SCALE * math.log2(math.e)
 AHEAD = 3
+PAIRS = 2
 
 f32 = jnp.float32
 bf16 = jnp.bfloat16
@@ -144,29 +145,126 @@
     )(ids, slots, *acc)
 
 
-def attend_kernel(base, live, wq, wq_t, wkv, wkv_t, wo, wo_t, grads_in, slots, xs, cots, *rest):
-    outs, tgrads, hgrads, grads_ref = rest[-19:-15]
-    hbuf, xbuf, cbuf, obuf, tbuf, gbuf = rest[-15:-9]
-    kvs, kvts, qts, dts, att_s, qg_s, kvg_s, in_sems, out_sems = rest[-9:]
+def head_kernel(live, wq_t, wo, x_ref, c_ref, q_ref, d_ref):
+    i = pl.program_id(0)
+    pairs = q_ref.shape[0]
+    for k in range(pairs):
+        at = 2 * (pairs * i + k)
+        q_ref[k] = mm_nt(wq_t[...], x_ref[2 * k : 2 * k + 2].reshape(2 * BT, D)).astype(bf16)
+        cot = live_rows(c_ref[2 * k : 2 * k + 2].reshape(2 * BT, D), live[0, at], live[0, at + 1])
+        d_ref[k] = mm_nt(wo[...], cot).astype(bf16)
+
+
+def live_rows(cot, live0, live1):
+    row = lax.broadcasted_iota(jnp.int32, (2 * BT, D), 0)
+    kept = row < jnp.where(row < BT, live0, live1 + BT)
+    return jnp.where(kept, cot.astype(f32), 0.0).astype(bf16)
+
+
+def constant(shape):
+    return pl.BlockSpec(shape, lambda i: (0,) * len(shape))
+
+
+def project(live, wq_t, wo, x, cot):
+    pairs = x.shape[0] // 2
+    blocks = pl.BlockSpec((2 * PAIRS, BT, D), lambda i: (i, 0, 0))
+    squares = pl.BlockSpec((PAIRS, D, 2 * BT), lambda i: (i, 0, 0))
+    return pl.pallas_call(
+        head_kernel,
+        out_shape=(jax.ShapeDtypeStruct((pairs, D, 2 * BT), bf16),) * 2,
+        grid=(pairs // PAIRS,),
+        in_specs=[pl.BlockSpec(memory_space=pltpu.SMEM), constant((D, D)), constant((D, D))]
+        + [blocks, blocks],
+        out_specs=(squares, squares),
+        compiler_params=PARAMS,
+        cost_estimate=pl.CostEstimate(
+            flops=8 * x.size * D, bytes_accessed=10 * x.size, transcendentals=0
+        ),
+        name="project",
+    )(live, wq_t, wo, x, cot)
+
+
+def tail_kernel(live, wq, wo_t, x_ref, c_ref, *rest):
+    att_a, qg_a, att_b, qg_b, out_ref, tgrad_ref, grads_ref = rest
+    i = pl.program_id(0)
+    pairs = att_a.shape[0]
+
+    @pl.when(i == 0)
+    def _():
+        grads_ref[...] = jnp.zeros_like(grads_ref)
+
+    def work(att_ref, qg_ref):
+        for k in range(pairs):
+            at = 2 * (pairs * i + k)
+            live0, live1 = live[0, at], live[0, at + 1]
+            att, qg = att_ref[k], qg_ref[k]
+            blocks = slice(2 * k, 2 * k + 2)
+            lane = lax.broadcasted_iota(jnp.int32, (D, 2 * BT), 1)
+            kept = lane < jnp.where(lane < BT, live0, live1 + BT)
+            out = jnp.where(kept, mm(wo_t[...], att), 0.0)
+            out_ref[blocks] = out.T.astype(bf16).reshape(2, BT, D)
+            tgrad_ref[blocks] = mm(wq[...], qg).T.astype(bf16).reshape(2, BT, D)
+            grads_ref[0:D] += mm(qg, x_ref[blocks].reshape(2 * BT, D))
+            cot = live_rows(c_ref[blocks].reshape(2 * BT, D), live0, live1)
+            grads_ref[D : 2 * D] += mm(att, cot)
+
+    first = i < pl.num_programs(0) // 2
+
+    @pl.when(first)
+    def _():
+        work(att_a, qg_a)
+
+    @pl.when(jnp.logical_not(first))
+    def _():
+        work(att_b, qg_b)
+
+
+def tokens_back(live, wq, wo_t, x, cot, halves):
+    steps = x.shape[0] // 2 // PAIRS
+    blocks = pl.BlockSpec((2 * PAIRS, BT, D), lambda i: (i, 0, 0))
+    low = pl.BlockSpec((PAIRS, D, 2 * BT), lambda i: (jnp.minimum(i, steps // 2 - 1), 0, 0))
+    high = pl.BlockSpec((PAIRS, D, 2 * BT), lambda i: (jnp.maximum(i - steps // 2, 0), 0, 0))
+    tokens = jax.ShapeDtypeStruct(x.shape, bf16)
+    return pl.pallas_call(
+        tail_kernel,
+        out_shape=(tokens, tokens, jax.ShapeDtypeStruct((2 * D, D), f32)),
+        grid=(steps,),
+        in_specs=[pl.BlockSpec(memory_space=pltpu.SMEM), constant((D, D)), constant((D, D))]
+        + [blocks, blocks, low, low, high, high],
+        out_specs=(blocks, blocks, constant((2 * D, D))),
+        compiler_params=PARAMS,
+        cost_estimate=pl.CostEstimate(
+            flops=8 * x.size * D, bytes_accessed=12 * x.size, transcendentals=0
+        ),
+        name="tokens_back",
+    )(live, wq, wo_t, x, cot, *halves)
+
+
+def attend_kernel(base, wkv, wkv_t, grads_in, slots, queries, cot_grads, *rest):
+    atts, qgs, hgrads, grads_ref = rest[:4]
+    hbuf, qbuf, dbuf, abuf, tbuf, gbuf, kvs, kvts, kvg_s, in_sems, out_sems = rest[4:]
     steps = slots.shape[0] // 2
     slices = slots.shape[1]
 
     def loads(i):
-        blocks = pl.ds(base + 2 * i, 2)
         slot = lax.rem(i, 4)
         return [
             pltpu.make_async_copy(slots.at[pl.ds(2 * i, 2)], hbuf.at[slot], in_sems.at[slot, 0]),
-            pltpu.make_async_copy(xs.at[blocks], xbuf.at[slot], in_sems.at[slot, 1]),
-            pltpu.make_async_copy(cots.at[blocks], cbuf.at[slot], in_sems.at[slot, 2]),
+            pltpu.make_async_copy(queries.at[base + i], qbuf.at[slot], in_sems.at[slot, 1]),
+            pltpu.make_async_copy(cot_grads.at[base + i], dbuf.at[slot], in_sems.at[slot, 2]),
         ]
 
+    def store_back(i):
+        slot = lax.rem(i, 2)
+        return pltpu.make_async_copy(
+            gbuf.at[slot], hgrads.at[pl.ds(2 * i, 2)], out_sems.at[slot, 0]
+        )
+
     def stores(i):
-        blocks = pl.ds(base + 2 * i, 2)
         slot = lax.rem(i, 2)
         return [
-            pltpu.make_async_copy(gbuf.at[slot], hgrads.at[pl.ds(2 * i, 2)], out_sems.at[slot, 0]),
-            pltpu.make_async_copy(obuf.at[slot], outs.at[blocks], out_sems.at[slot, 1]),
-            pltpu.make_async_copy(tbuf.at[slot], tgrads.at[blocks], out_sems.at[slot, 2]),
+            pltpu.make_async_copy(abuf.at[slot], atts.at[i], out_sems.at[slot, 1]),
+            pltpu.make_async_copy(tbuf.at[slot], qgs.at[i], out_sems.at[slot, 2]),
         ]
 
     zero = jnp.zeros((HD, BT), bf16)
@@ -178,10 +276,6 @@
             [jnp.concatenate([top, zero], axis=1), jnp.concatenate([zero, low], axis=1)], axis=0
         )
 
-    def lives(i):
-        at = base + 2 * jnp.minimum(i, steps - 1)
-        return live[0, at], live[0, at + 1]
-
     def cells(i):
         sliced = hbuf[lax.rem(i, 4)]
         return jnp.concatenate(
@@ -189,9 +283,6 @@
             axis=0,
         )
 
-    def rows_of(buf, i):
-        return buf[lax.rem(i, 4)].reshape(2 * BT, D)
-
     def head(i):
         slot = lax.rem(i, 2)
 
@@ -201,31 +292,10 @@
         def keys_t():
             kvts[slot] = mm_nt(wkv_t[...], cells(i)).astype(bf16)
 
-        def queries():
-            qts[slot] = mm_nt(wq_t[...], rows_of(xbuf, i)).astype(bf16)
-
-        def cotangents():
-            live0, live1 = lives(i)
-            row = lax.broadcasted_iota(jnp.int32, (2 * BT, D), 0)
-            row_live = row < jnp.where(row < BT, live0, live1 + BT)
-            cot = jnp.where(row_live, rows_of(cbuf, i).astype(f32), 0.0).astype(bf16)
-            cbuf[lax.rem(i, 4)] = cot.reshape(2, BT, D)
-            dts[slot] = mm_nt(wo[...], cot).astype(bf16)
-
-        return [cotangents, queries, keys, keys_t]
+        return [keys, keys_t]
 
     def tail(i):
         slot = lax.rem(i + 2, 2)
-
-        def mixed():
-            live0, live1 = lives(i)
-            lane = lax.broadcasted_iota(jnp.int32, (D, 2 * BT), 1)
-            lane_live = lane < jnp.where(lane < BT, live0, live1 + BT)
-            out = jnp.where(lane_live, mm(wo_t[...], att_s[...]), 0.0)
-            obuf[slot] = out.T.astype(bf16).reshape(2, BT, D)
-
-        def token_grad():
-            tbuf[slot] = mm(wq[...], qg_s[...]).T.astype(bf16).reshape(2, BT, D)
 
         def hidden_grad():
             back = mm(wkv[...], kvg_s[...]).astype(bf16)
@@ -236,15 +306,14 @@
                 )
 
         def weight_grads():
-            grads_ref[0:256] += mm(qg_s[...], rows_of(xbuf, i + 4))
-            grads_ref[256:768] += mm(kvg_s[...], cells(i + 4))
-            grads_ref[768:1024] += mm(att_s[...], rows_of(cbuf, i + 4))
-
-        return [hidden_grad, mixed, token_grad, weight_grads]
+            grads_ref[...] += mm(kvg_s[...], cells(i + 4))
+
+        return [hidden_grad, weight_grads]
 
     def attention(i, between):
         slot = lax.rem(i, 2)
-        kv, kv_t, q_t, d_t = kvs[slot], kvts[slot], qts[slot], dts[slot]
+        kv, kv_t = kvs[slot], kvts[slot]
+        q_t, d_t = qbuf[lax.rem(i, 4)], dbuf[lax.rem(i, 4)]
         att_rows, qg_rows, kg_rows, vg_rows = [[], []], [[], []], [[], []], [[], []]
 
         def first(p, u):
@@ -294,19 +363,15 @@
         def joined(rows):
             return jnp.concatenate([jnp.concatenate(r, axis=0) for r in rows], axis=1)
 
-        att_s[...] = joined(att_rows).astype(bf16)
-        qg_s[...] = (joined(qg_rows) * SCALE).astype(bf16)
+        abuf[slot] = joined(att_rows).astype(bf16)
+        tbuf[slot] = (joined(qg_rows) * SCALE).astype(bf16)
         kvg_s[...] = joined([kg_rows[u] + vg_rows[u] for u in range(2)]).astype(bf16)
 
-    for c in loads(0):
-        c.start()
-    for c in loads(1):
+    for c in loads(0) + loads(1):
         c.start()
     grads_ref[...] = grads_in[...]
-    for ref in (att_s, qg_s, kvg_s):
-        ref[...] = jnp.zeros_like(ref)
-    for ref in (hbuf, xbuf, cbuf):
-        ref[3] = jnp.zeros(ref.shape[1:], bf16)
+    kvg_s[...] = jnp.zeros_like(kvg_s)
+    hbuf[3] = jnp.zeros(hbuf.shape[1:], bf16)
     for c in loads(0):
         c.wait()
     for piece in head(0):
@@ -326,61 +391,58 @@
 
         @pl.when(i >= 3)
         def _():
-            for c in stores(i - 3):
+            store_back(i - 3).wait()
+
+        @pl.when(i >= 2)
+        def _():
+            for c in stores(i - 2):
                 c.wait()
 
         attention(i, [piece for two in zip(tail(i - 1), head(i + 1)) for piece in two])
+        for c in stores(i):
+            c.start()
 
         @pl.when(i >= 1)
         def _():
-            for c in stores(i - 1):
-                c.start()
-
-    for c in stores(steps - 3):
-        c.wait()
+            store_back(i - 1).start()
+
+    store_back(steps - 3).wait()
     for piece in tail(steps - 1):
         piece()
-    for c in stores(steps - 1):
-        c.start()
+    store_back(steps - 1).start()
     for i in (steps - 2, steps - 1):
+        store_back(i).wait()
         for c in stores(i):
             c.wait()
 
 
-def attend(base, live, slots, x, cot, weights, grads, kept):
-    args = [live, *weights, grads, slots, x, cot, *kept]
-    first_kept = len(args) - len(kept)
-    token_shape = jax.ShapeDtypeStruct(x.shape, bf16)
+def attend(base, slots, queries, cot_grads, wkv, wkv_t, grads):
+    steps = slots.shape[0] // 2
+    square = jax.ShapeDtypeStruct((steps, D, 2 * BT), bf16)
+    sliced = (2,) + slots.shape[1:]
     return pl.pallas_call(
         functools.partial(attend_kernel, base),
         out_shape=(
-            token_shape,
-            token_shape,
+            square,
+            square,
             jax.ShapeDtypeStruct(slots.shape, bf16),
-            jax.ShapeDtypeStruct((4 * D, D), f32),
-        ),
-        in_specs=[pl.BlockSpec(memory_space=pltpu.SMEM)]
-        + [VMEM] * (len(weights) + 1)
-        + [HBM] * (3 + len(kept)),
+            jax.ShapeDtypeStruct((2 * D, D), f32),
+        ),
+        in_specs=[VMEM] * 3 + [HBM] * 3,
         out_specs=(HBM, HBM, HBM, VMEM),
         scratch_shapes=[
-            pltpu.VMEM((4, 2) + slots.shape[1:], bf16),
-            pltpu.VMEM((4, 2, BT, D), bf16),
-            pltpu.VMEM((4, 2, BT, D), bf16),
-            pltpu.VMEM((2, 2, BT, D), bf16),
-            pltpu.VMEM((2, 2, BT, D), bf16),
-            pltpu.VMEM((2, 2) + slots.shape[1:], bf16),
+            pltpu.VMEM((4,) + sliced, bf16),
+            pltpu.VMEM((4, D, 2 * BT), bf16),
+            pltpu.VMEM((4, D, 2 * BT), bf16),
+            pltpu.VMEM((2, D, 2 * BT), bf16),
+            pltpu.VMEM((2, D, 2 * BT), bf16),
+            pltpu.VMEM((2,) + sliced, bf16),
             pltpu.VMEM((2, 2 * KEYS, 2 * D), bf16),
             pltpu.VMEM((2, 2 * D, 2 * KEYS), bf16),
-            pltpu.VMEM((2, D, 2 * BT), bf16),
-            pltpu.VMEM((2, D, 2 * BT), bf16),
-            pltpu.VMEM((D, 2 * BT), bf16),
-            pltpu.VMEM((D, 2 * BT), bf16),
             pltpu.VMEM((2 * D, 2 * KEYS), bf16),
             pltpu.SemaphoreType.DMA((4, 3)),
             pltpu.SemaphoreType.DMA((2, 3)),
         ],
-        input_output_aliases={first_kept + j: j for j in range(len(kept))},
         compiler_params=PARAMS,
         cost_estimate=pl.CostEstimate(
             flops=slots.shape[0] * 800_000_000,
@@ -388,10 +450,10 @@
             transcendentals=0,
         ),
         name="attend",
-    )(*args)
-
-
-def finish_kernel(slices_ref, shifts_ref, grads_ref, hgrad_ref, sums_ref, back_t):
+    )(wkv, wkv_t, grads, slots, queries, cot_grads)
+
+
+def finish_kernel(slices_ref, shifts_ref, kv_grads, token_grads, hgrad_ref, sums_ref, back_t):
     slices = slices_ref.shape[1]
     used = 13 * D * D // LANES
 
@@ -400,8 +462,10 @@
             row = (k * (D // LANES) + j) * D
             sums_ref[row : row + D] = grad[:, at : at + LANES].astype(bf16)
 
-    for k in range(4):
-        put(k, grads_ref[k * D : (k + 1) * D])
+    put(0, token_grads[0:D])
+    put(1, kv_grads[0:D])
+    put(2, kv_grads[D : 2 * D])
+    put(3, token_grads[D : 2 * D])
     if sums_ref.shape[0] > used:
         sums_ref[used:] = jnp.zeros((sums_ref.shape[0] - used, LANES), bf16)
     for s in range(SUB):
@@ -416,14 +480,14 @@
             put(4 + 3 * a + b, mm(back_t[...], shifts_ref[b, a * RX : a * RX + CELLS, :]))
 
 
-def finish(slices, shifts, grads, rows):
+def finish(slices, shifts, kv_grads, token_grads, rows):
     return pl.pallas_call(
         finish_kernel,
         out_shape=(
             jax.ShapeDtypeStruct((CELLS, D), bf16),
             jax.ShapeDtypeStruct((rows, LANES), bf16),
         ),
-        in_specs=[VMEM] * 3,
+        in_specs=[VMEM] * 4,
         out_specs=(VMEM, VMEM),
         scratch_shapes=[pltpu.VMEM((D, CELLS), bf16)],
         compiler_params=PARAMS,
@@ -431,7 +495,7 @@
             flops=2 * 9 * CELLS * D * D, bytes_accessed=6_000_000, transcendentals=0
         ),
         name="finish",
-    )(slices, shifts, grads)
+    )(slices, shifts, kv_grads, token_grads)
 
 
 def normalize_kernel(sums_ref, query_ref, key_ref, value_ref, out_ref, conv_ref):
@@ -521,25 +585,28 @@
     table = table.reshape(ntile * SUB, -1)
 
     wkv = jnp.concatenate([w_key, w_value], axis=1)
-    weights = (w_query, w_query.T, wkv, wkv.T, w_out, w_out.T)
     x = tokens[0].reshape(nblocks, BT, D)
     cot = token_cotan[0].reshape(nblocks, BT, D)
     half = nblocks // 2
-    grads = jnp.zeros((4 * D, D), f32)
+    queries, cot_grads = project(live_counts, w_query.T, w_out, x, cot)
+    grads = jnp.zeros((2 * D, D), f32)
     got = [exchange(pick(table, ids[:, c * half : (c + 1) * half].T, width)) for c in range(2)]
-    kept, returned = (), []
+    halves, returned = [], []
     for c in range(2):
-        token_out, token_grad, back, grads = attend(
-            c * half, live_counts, got[c].transpose(1, 0, 2), x, cot, weights, grads, kept
+        att, query_grad, back, grads = attend(
+            c * half // 2, got[c].transpose(1, 0, 2), queries, cot_grads, wkv, wkv.T, grads
         )
-        kept = (token_out, token_grad)
+        halves += [att, query_grad]
         returned.append(exchange(back.transpose(1, 0, 2)).reshape(ntile * half, -1))
+    token_out, token_grad, token_grads = tokens_back(
+        live_counts, w_query, w_out.T, x, cot, halves
+    )
     rows = [ids[:, c * half : (c + 1) * half].reshape(1, -1) for c in range(2)]
     acc = gather(rows[0], returned[0], ntile * SUB, (), f32)
     home = gather(rows[1], returned[1], ntile * SUB, (acc,), bf16)
     home = exchange(home.reshape(ntile, SUB, -1)).transpose(1, 0, 2)
     each = -(-13 * D * D // LANES // (8 * ndev)) * 8
-    hidden_back, sums = finish(home, shifts, grads, ndev * each)
+    hidden_back, sums = finish(home, shifts, grads, token_grads, ndev * each)
 
     parts = exchange(sums.reshape(ndev, -1, LANES), ("tile", "win"))
     share = jnp.sum(parts.astype(f32), axis=0).astype(bf16)

time: 314 us -> 324 us (1.032)
  Pallas kernels: 86 us -> 110 us
  blocking collectives: 68.8 us -> 49.5 us
  starting transfers between devices: 58.1 us -> 69.8 us
  waiting for transfers between devices: 50.2 us -> 43.6 us
    pallas_call x2 -> x4, Pallas kernels: 57.3 us -> 81.6 us  [the longest x2 49.9 us: attend(): pl.pallas_call(functools.partial(attend_kernel, base), out_shape=(square,...]
    all_to_all x3 -> x2, blocking collectives: 68.8 us -> 49.5 us  [exchange(): return lax.all_to_all(value, axes, split_axis=0, concat_axis=0, tiled=True)]
    all_to_all x5 -> x6, waiting for transfers between devices: 39.5 us -> 26.4 us  [exchange(): return lax.all_to_all(value, axes, split_axis=0, concat_axis=0, tiled=True)]
    all_to_all x5 -> x6, starting transfers between devices: 41 us -> 52.8 us  [exchange(): return lax.all_to_all(value, axes, split_axis=0, concat_axis=0, tiled=True)]
    ppermute x4, waiting for transfers between devices: 10.7 us -> 17.1 us  [ring(): lax.ppermute(value, 'tile', [(i, (i + by) % length) for i in range(length)])]
  transfers between devices with their start and end apart: 9 -> 10, of which waited for: 4 -> 5; matrix products, arithmetic and copies ran while one was open for 11% -> 10% of each run, Pallas kernels for 21% -> 28%
where the time goes in v5:
time: 324 us; the launch traced here: 322 us
  Pallas kernels  110 us (34%)
  starting transfers between devices  69.8 us (22%)
  blocking collectives  49.5 us (15%)
  waiting for transfers between devices  43.6 us (13%)
  local copies, waits for them, and re-layouts  26.7 us (8%)
  matrix products  13.7 us (4%)
  other arithmetic  6.33 us (2%)
    all_to_all x6, starting transfers between devices, exchange(): return lax.all_to_all(value, axes, split_axis=0, concat_axis=0, tiled=True)  52.8 us
    pallas_call x2, Pallas kernels, attend(): pl.pallas_call(functools.partial(attend_kernel, base), out_shape=(square,...  49.9 us
    all_to_all x2, blocking collectives, exchange(): return lax.all_to_all(value, axes, split_axis=0, concat_axis=0, tiled=True)  49.5 us
    all_to_all x6, waiting for transfers between devices, exchange(): return lax.all_to_all(value, axes, split_axis=0, concat_axis=0, tiled=True)  26.4 us
    pallas_call x1, Pallas kernels, tokens_back(): pl.pallas_call(tail_kernel, out_shape=(tokens, tokens, jax.ShapeDtypeStru...  17.6 us
    ppermute x4, waiting for transfers between devices, ring(): lax.ppermute(value, 'tile', [(i, (i + by) % length) for i in range(length)])  17.1 us
    ppermute x4, starting transfers between devices, ring(): lax.ppermute(value, 'tile', [(i, (i + by) % length) for i in range(length)])  17 us
    pallas_call x1, Pallas kernels, project(): pl.pallas_call(head_kernel, out_shape=(jax.ShapeDtypeStruct((pairs, D, 2...  14.1 us
  transfers between devices with their start and end apart: 10, of which 5 were waited for; matrix products, arithmetic and copies ran while one was open for 10% of the time, Pallas kernels for 28%

profile of v5, /device:TPU:1, one launch (start us, length us, event | category | flops | bytes accessed | tf_op | source)
XLA Modules:
  0.0 322.0 jit_solution(13188509246020724606)
XLA Ops:
  0.6 0.7 slice_bitcast_fusion.3
  1.4 9.2 %collective-permute-start.1 = (bf16[32,256]{1,0:T(8,128)(2,1)S(1)}, bf16[32,256]{1,0:T(8,128)(2,1)S(1)}, u32[]{:S(2)}, u32[]{:S(2)}) collective-permute-start(bf16[32,256]{1,0:T(8,128)(2,1)S(1)} %get-tuple-element.57), channel_id=1, source_target_pairs={{0,126},{2,0},{4,2},{6,4},{8,6},{10,8},{12,10},{14,12},{16,14},{18... | collective-permute-start | bytes 49160 | tf_op jit(solution)/shard_map/ppermute | solution.py:539
  10.6 1.3 fusion.37
  11.9 0.7 fusion.27
  12.6 0.7 convert_bitcast_fusion.1
  14.7 0.1 rev.13
  14.8 3.9 %collective-permute-done = bf16[32,256]{1,0:T(8,128)(2,1)S(1)} collective-permute-done((bf16[32,256]{1,0:T(8,128)(2,1)S(1)}, bf16[32,256]{1,0:T(8,128)(2,1)S(1)}, u32[]{:S(2)}, u32[]{:S(2)}) %collective-permute-start) | collective-permute-done | bytes 16416 | tf_op jit(solution)/shard_map/ppermute | solution.py:539
  18.7 1.9 pad_maximum_fusion.1
  20.6 4.6 %conv_slices.1 = (bf16[8,64,512]{2,1,0:T(8,128)(2,1)}, bf16[3,1088,256]{2,1,0:T(8,128)(2,1)}) custom-call(bf16[1088,256]{1,0:T(8,128)(2,1)} %bitcast.140, bf16[9,256,256]{2,1,0:T(8,128)(2,1)} %bitcast.136), custom_call_target="tpu_custom_call" | custom-call | flops 1207959552 | bytes 6000000 | tf_op jit(solution)/shard_map/conv_slices/pallas_call | solution.py:72
  25.2 1.1 pad_maximum_fusion
  26.3 0.4 copy.51
  26.7 17.6 %all_to_all.40 = bf16[64,8,640]{2,1,0:T(8,128)(2,1)S(1)} all-to-all(bf16[64,8,640]{2,1,0:T(8,128)(2,1)S(1)} %copy.51), channel_id=1, replica_groups=mesh['tile'=64,'win'=2] {'tile'}, dimensions={0} | all-to-all | bytes 1310720 | tf_op jit(solution)/shard_map/all_to_all | solution.py:547
  44.3 0.1 copy.63
  44.5 0.6 fusion.36
  45.1 3.7 %pick.2 = bf16[64,32,512]{2,1,0:T(8,128)(2,1)} custom-call(bf16[512,640]{1,0:T(8,128)(2,1)} %bitcast.137, s32[32,64]{1,0:T(8,128)} %get-tuple-element.61.ids_ref), custom_call_target="tpu_custom_call" | custom-call | flops 1342177280 | bytes 4000000 | tf_op jit(solution)/shard_map/pick/pallas_call | solution.py:106
  48.8 5.7 %all-to-all-start.1 = ((bf16[64,32,512]{2,1,0:T(8,128)(2,1)}), bf16[64,32,512]{2,1,0:T(8,128)(2,1)S(1)}, u32[]{:S(2)}, u32[]{:S(2)}) async-start(bf16[64,32,512]{2,1,0:T(8,128)(2,1)} %pick.2), calls=%async_computation.1 | async-start | bytes 4194304 | tf_op jit(solution)/shard_map/all_to_all | solution.py:547
  54.5 0.8 copy.54
  55.3 0.1 copy.49
  55.4 0.1 copy.50
  55.5 0.7 fusion.35
  56.2 0.8 copy.55.wkv
  57.1 14.1 %project.1 = (bf16[32,256,256]{2,1,0:T(8,128)(2,1)}, bf16[32,256,256]{2,1,0:T(8,128)(2,1)}) custom-call(s32[1,64]{1,0:T(1,128)} %live.3, bf16[256,256]{1,0:T(8,128)(2,1)} %bitcast.145, bf16[256,256]{1,0:T(8,128)(2,1)} %wo.1, bf16[64,128,256]{2,1,0:T(8,128)(2,1)} %bitcast.126, bf16[64,128,256]{2,1,0:T(8,128)(2,1)} %bitcast.128), custom_call_target="tpu_custom_call" | custom-call | flops 4294967296 | bytes 20971520 | tf_op jit(solution)/shard_map/project/pallas_call | solution.py:172
  71.2 3.8 %pick.3 = bf16[64,32,512]{2,1,0:T(8,128)(2,1)} custom-call(bf16[512,640]{1,0:T(8,128)(2,1)} %bitcast.138, s32[32,64]{1,0:T(8,128)} %get-tuple-element.62.ids_ref), custom_call_target="tpu_custom_call" | custom-call | flops 1342177280 | bytes 4000000 | tf_op jit(solution)/shard_map/pick/pallas_call | solution.py:106
  74.9 6.1 %all-to-all-done.1 = bf16[64,32,512]{2,1,0:T(8,128)(2,1)S(1)} async-done(((bf16[64,32,512]{2,1,0:T(8,128)(2,1)}), bf16[64,32,512]{2,1,0:T(8,128)(2,1)S(1)}, u32[]{:S(2)}, u32[]{:S(2)}) %all-to-all-start.1) | async-done | bytes 2097184 | tf_op jit(solution)/shard_map/all_to_all | solution.py:547
  81.0 8.5 %all-to-all-start.2 = ((bf16[64,32,512]{2,1,0:T(8,128)(2,1)}), bf16[64,32,512]{2,1,0:T(8,128)(2,1)}, u32[]{:S(2)}, u32[]{:S(2)}) async-start(bf16[64,32,512]{2,1,0:T(8,128)(2,1)} %pick.3), calls=%async_computation.2 | async-start | bytes 4194304 | tf_op jit(solution)/shard_map/all_to_all | solution.py:547
  89.5 2.5 copy.68
  91.9 0.8 broadcast_in_dim.32.grads_in
  92.8 25.0 %attend.2 = (bf16[16,256,256]{2,1,0:T(8,128)(2,1)}, bf16[16,256,256]{2,1,0:T(8,128)(2,1)}, bf16[32,64,512]{2,1,0:T(8,128)(2,1)}, f32[512,256]{1,0:T(8,128)}) custom-call(bf16[256,512]{1,0:T(8,128)(2,1)} %copy.55.wkv, bf16[512,256]{1,0:T(8,128)(2,1)} %get-tuple-element.58.wkv_t, f32[512,256]{1,0:T(8,128)} %broadcast_in_dim.32.grads_in, ...), custom_call_target="tpu_custom_call" | custom-call | flops 25600000000 | bytes 25600000 | tf_op jit(solution)/shard_map/attend/pallas_call | solution.py:423
  117.7 4.1 %copy.61 = bf16[64,32,512]{2,1,0:T(8,128)(2,1)} copy(bf16[64,32,512]{2,0,1:T(8,128)(2,1)} %bitcast.134) | data formatting | bytes 4194304 | tf_op jit(solution)/shard_map/transpose | solution.py:600
  121.9 9.5 %all-to-all-start.4 = ((bf16[64,32,512]{2,1,0:T(8,128)(2,1)}), bf16[64,32,512]{2,1,0:T(8,128)(2,1)S(1)}, u32[]{:S(2)}, u32[]{:S(2)}) async-start(bf16[64,32,512]{2,1,0:T(8,128)(2,1)} %copy.61), calls=%async_computation.4 | async-start | bytes 4194304 | tf_op jit(solution)/shard_map/all_to_all | solution.py:547
  131.4 4.1 %copy.67 = bf16[64,32,512]{2,0,1:T(8,128)(2,1)} copy(bf16[64,32,512]{2,1,0:T(8,128)(2,1)} %all-to-all-done.2) | data formatting | bytes 4194304 | tf_op jit(solution)/shard_map/all_to_all | solution.py:547
  135.5 24.9 %attend.3 = (bf16[16,256,256]{2,1,0:T(8,128)(2,1)}, bf16[16,256,256]{2,1,0:T(8,128)(2,1)}, bf16[32,64,512]{2,1,0:T(8,128)(2,1)}, f32[512,256]{1,0:T(8,128)}) custom-call(bf16[256,512]{1,0:T(8,128)(2,1)} %copy.55.wkv, bf16[512,256]{1,0:T(8,128)(2,1)} %get-tuple-element.58.wkv_t, f32[512,256]{1,0:T(8,128)} %get-tuple-element.37.grads_in, ...), custom_call_target="tpu_custom_call" | custom-call | flops 25600000000 | bytes 25600000 | tf_op jit(solution)/shard_map/attend/pallas_call | solution.py:423
  160.4 4.1 %copy.59 = bf16[64,32,512]{2,1,0:T(8,128)(2,1)} copy(bf16[64,32,512]{2,0,1:T(8,128)(2,1)} %bitcast.132) | data formatting | bytes 4194304 | tf_op jit(solution)/shard_map/transpose | solution.py:600
  164.5 1.3 copy-done.3
  165.8 10.0 %all-to-all-start.3 = ((bf16[64,32,512]{2,1,0:T(8,128)(2,1)}), bf16[64,32,512]{2,1,0:T(8,128)(2,1)}, u32[]{:S(2)}, u32[]{:S(2)}) async-start(bf16[64,32,512]{2,1,0:T(8,128)(2,1)} %copy.59), calls=%async_computation.3 | async-start | bytes 4194304 | tf_op jit(solution)/shard_map/all_to_all | solution.py:547
  175.9 0.7 reshape.147.ids_ref
  176.7 0.7 reshape.145.ids_ref
  177.4 3.8 %gather.2.rest_0_ = f32[512,512]{1,0:T(8,128)} custom-call(s32[1,2048]{1,0:T(1,128)} %reshape.147.ids_ref, bf16[2048,512]{1,0:T(8,128)(2,1)} %bitcast.130), custom_call_target="tpu_custom_call" | custom-call | flops 1073741824 | bytes 4000000 | tf_op jit(solution)/shard_map/gather/pallas_call | solution.py:135
  181.2 20.4 %all-to-all-done.3 = bf16[64,32,512]{2,1,0:T(8,128)(2,1)} async-done(((bf16[64,32,512]{2,1,0:T(8,128)(2,1)}), bf16[64,32,512]{2,1,0:T(8,128)(2,1)}, u32[]{:S(2)}, u32[]{:S(2)}) %all-to-all-start.3) | async-done | bytes 2097184 | tf_op jit(solution)/shard_map/all_to_all | solution.py:547
  201.6 3.9 %gather.3 = bf16[512,512]{1,0:T(8,128)(2,1)} custom-call(s32[1,2048]{1,0:T(1,128)} %reshape.145.ids_ref, bf16[2048,512]{1,0:T(8,128)(2,1)} %bitcast.28.slots_ref, f32[512,512]{1,0:T(8,128)} %gather.2.rest_0_), custom_call_target="tpu_custom_call" | custom-call | flops 1073741824 | bytes 4000000 | tf_op jit(solution)/shard_map/gather/pallas_call | solution.py:135
  205.5 8.4 %all-to-all-start.5 = ((bf16[64,8,512]{2,1,0:T(8,128)(2,1)}), bf16[64,8,512]{2,1,0:T(8,128)(2,1)S(1)}, u32[]{:S(2)}, u32[]{:S(2)}) async-start(bf16[64,8,512]{2,1,0:T(8,128)(2,1)} %bitcast.142), calls=%async_computation.5 | async-start | bytes 1048576 | tf_op jit(solution)/shard_map/all_to_all | solution.py:547
  214.0 0.8 copy.48
  214.7 17.6 %tokens_back.1 = (bf16[64,128,256]{2,1,0:T(8,128)(2,1)}, bf16[64,128,256]{2,1,0:T(8,128)(2,1)}, f32[512,256]{1,0:T(8,128)}) custom-call(s32[1,64]{1,0:T(1,128)} %live.3, bf16[256,256]{1,0:T(8,128)(2,1)} %wq.1, bf16[256,256]{1,0:T(8,128)(2,1)} %bitcast.141, bf16[64,128,256]{2,1,0:T(8,128)(2,1)} %bitcast.127, bf16[64,128,256]{2,1,0:T(8,128)(2,1)} %bitcast.129, ...), custom_call_target="tpu_custom_call" | custom-call | flops 4294967296 | bytes 25165824 | tf_op jit(solution)/shard_map/tokens_back/pallas_call | solution.py:228
  232.3 1.0 copy.69
  233.3 4.6 %finish.1 = (bf16[1024,256]{1,0:T(8,128)(2,1)}, bf16[7168,128]{1,0:T(8,128)(2,1)}) custom-call(bf16[8,64,512]{2,1,0:T(8,128)(2,1)} %bitcast.143, bf16[3,1088,256]{2,1,0:T(8,128)(2,1)} %get-tuple-element.44.shifts_ref, f32[512,256]{1,0:T(8,128)} %get-tuple-element.45.kv_grads, f32[512,256]{1,0:T(8,128)} %get-tuple-element.46.token_grads), custom_call_target="tpu_custom_call" | custom-call | flops 1207959552 | bytes 6000000 | tf_op jit(solution)/shard_map/finish/pallas_call | solution.py:484
  237.9 1.5 fusion.5
  239.4 2.2 fusion.4
  241.6 1.2 convolution_add_fusion.3
  242.9 1.3 convolution_add_fusion.2
  244.2 10.7 %all-to-all-start.6 = ((bf16[128,56,128]{2,1,0:T(8,128)(2,1)}), bf16[128,56,128]{2,1,0:T(8,128)(2,1)S(1)}, u32[]{:S(2)}, u32[]{:S(2)}) async-start(bf16[128,56,128]{2,1,0:T(8,128)(2,1)} %bitcast.135), calls=%async_computation.6 | async-start | bytes 3670016 | tf_op jit(solution)/shard_map/all_to_all | solution.py:547
  254.9 7.8 %collective-permute-start.2 = (f32[32,256]{1,0:T(8,128)S(1)}, f32[32,256]{1,0:T(8,128)S(1)}, u32[]{:S(2)}, u32[]{:S(2)}) collective-permute-start(f32[32,256]{1,0:T(8,128)S(1)} %broadcast_select_fusion.1), channel_id=1, source_target_pairs={{0,126},{2,0},{4,2},{6,4},{8,6},{10,8},{12,10},{14,12},{16,14},{18... | collective-permute-start | bytes 98312 | tf_op jit(solution)/shard_map/ppermute | solution.py:539
  262.7 1.6 convolution_add_fusion.1
  264.4 1.3 convolution_add_fusion
  265.6 1.0 copy-done.2
  266.7 0.8 broadcast_select_fusion
  267.4 1.3 fusion.6
  268.7 1.2 convolution_add_fusion.5
  269.9 3.5 %collective-permute-done.2 = f32[32,256]{1,0:T(8,128)S(1)} collective-permute-done((f32[32,256]{1,0:T(8,128)S(1)}, f32[32,256]{1,0:T(8,128)S(1)}, u32[]{:S(2)}, u32[]{:S(2)}) %collective-permute-start.2) | collective-permute-done | bytes 32800 | tf_op jit(solution)/shard_map/ppermute | solution.py:539
  273.4 9.8 %collective-permute-done.3 = f32[32,256]{1,0:T(8,128)S(1)} collective-permute-done((f32[32,256]{1,0:T(8,128)S(1)}, f32[32,256]{1,0:T(8,128)S(1)}, u32[]{:S(2)}, u32[]{:S(2)}) %collective-permute-start.3) | collective-permute-done | bytes 32800 | tf_op jit(solution)/shard_map/ppermute | solution.py:539
  283.2 2.1 fusion.3
  285.4 0.3 reduce_sum.22
  285.7 0.2 broadcast_in_dim.39
  285.9 31.9 %all_to_all.41 = bf16[128,56,128]{2,1,0:T(8,128)(2,1)} all-to-all(bf16[128,56,128]{2,1,0:T(8,128)(2,1)S(1)} %broadcast_in_dim.39), channel_id=1, replica_groups=mesh['tile'=64,'win'=2] {'tile','win'}, dimensions={0} | all-to-all | bytes 3670016 | tf_op jit(solution)/shard_map/all_to_all | solution.py:547
  317.8 4.2 %normalize.1 = (f32[256,256]{1,0:T(8,128)}, f32[256,256]{1,0:T(8,128)}, f32[256,256]{1,0:T(8,128)}, f32[256,256]{1,0:T(8,128)}, f32[9,256,256]{2,1,0:T(8,128)}) custom-call(bf16[7168,128]{1,0:T(8,128)(2,1)} %bitcast.125), custom_call_target="tpu_custom_call" | custom-call | flops 4000000 | bytes 6000000 | tf_op jit(solution)/shard_map/normalize/pallas_call | solution.py:526
  (43 shorter events, 0.6 us)
Async XLA Ops:
  1.4 13.3 %collective-permute-start.1 = (bf16[32,256]{1,0:T(8,128)(2,1)S(1)}, bf16[32,256]{1,0:T(8,128)(2,1)S(1)}, u32[]{:S(2)}, u32[]{:S(2)}) collective-permute-start(bf16[32,256]{1,0:T(8,128)(2,1)S(1)} %get-tuple-element.57), channel_id=1, source_target_pairs={{0,126},{2,0},{4,2},{6,4},{8,6},{10,8},{12,10},{14,12},{16,14},{18... | collective-permute-start | bytes 49160 | tf_op jit(solution)/shard_map/ppermute | solution.py:539
  10.6 8.0 %collective-permute-start = (bf16[32,256]{1,0:T(8,128)(2,1)S(1)}, bf16[32,256]{1,0:T(8,128)(2,1)S(1)}, u32[]{:S(2)}, u32[]{:S(2)}) collective-permute-start(bf16[32,256]{1,0:T(8,128)(2,1)S(1)} %get-tuple-element.56), channel_id=1, source_target_pairs={{0,2},{2,4},{4,6},{6,8},{8,10},{10,12},{12,14},{14,16},{16,18},{18... | collective-permute-start | bytes 49160 | tf_op jit(solution)/shard_map/ppermute | solution.py:539
  44.3 0.8 copy-start.4
  48.8 5.7 %copy-start.5 = (bf16[256,256]{1,0:T(8,128)(2,1)S(1)}, bf16[256,256]{1,0:T(8,128)(2,1)}, u32[]{:S(2)}) copy-start(bf16[256,256]{1,0:T(8,128)(2,1)} %wq.1) | copy-start | bytes 393220
  48.8 6.5 %copy-start.6 = (bf16[256,256]{1,0:T(8,128)(2,1)S(1)}, bf16[256,256]{1,0:T(8,128)(2,1)}, u32[]{:S(2)}) copy-start(bf16[256,256]{1,0:T(8,128)(2,1)} %param.19) | copy-start | bytes 393220
  48.8 6.6 %copy-start.7 = (bf16[256,256]{1,0:T(8,128)(2,1)S(1)}, bf16[256,256]{1,0:T(8,128)(2,1)}, u32[]{:S(2)}) copy-start(bf16[256,256]{1,0:T(8,128)(2,1)} %param.20) | copy-start | bytes 393220
  48.8 32.2 %all-to-all-start.1 = ((bf16[64,32,512]{2,1,0:T(8,128)(2,1)}), bf16[64,32,512]{2,1,0:T(8,128)(2,1)S(1)}, u32[]{:S(2)}, u32[]{:S(2)}) async-start(bf16[64,32,512]{2,1,0:T(8,128)(2,1)} %pick.2), calls=%async_computation.1 | async-start | bytes 4194304 | tf_op jit(solution)/shard_map/all_to_all | solution.py:547
  81.0 40.9 %all-to-all-start.2 = ((bf16[64,32,512]{2,1,0:T(8,128)(2,1)}), bf16[64,32,512]{2,1,0:T(8,128)(2,1)}, u32[]{:S(2)}, u32[]{:S(2)}) async-start(bf16[64,32,512]{2,1,0:T(8,128)(2,1)} %pick.3), calls=%async_computation.2 | async-start | bytes 4194304 | tf_op jit(solution)/shard_map/all_to_all | solution.py:547
  121.9 42.6 %all-to-all-start.4 = ((bf16[64,32,512]{2,1,0:T(8,128)(2,1)}), bf16[64,32,512]{2,1,0:T(8,128)(2,1)S(1)}, u32[]{:S(2)}, u32[]{:S(2)}) async-start(bf16[64,32,512]{2,1,0:T(8,128)(2,1)} %copy.61), calls=%async_computation.4 | async-start | bytes 4194304 | tf_op jit(solution)/shard_map/all_to_all | solution.py:547
  164.5 1.3 copy-start.3
  165.8 35.8 %all-to-all-start.3 = ((bf16[64,32,512]{2,1,0:T(8,128)(2,1)}), bf16[64,32,512]{2,1,0:T(8,128)(2,1)}, u32[]{:S(2)}, u32[]{:S(2)}) async-start(bf16[64,32,512]{2,1,0:T(8,128)(2,1)} %copy.59), calls=%async_computation.3 | async-start | bytes 4194304 | tf_op jit(solution)/shard_map/all_to_all | solution.py:547
  201.6 12.4 %copy-start.8 = (bf16[256,256]{1,0:T(8,128)(2,1)S(1)}, bf16[256,256]{1,0:T(8,128)(2,1)}, u32[]{:S(2)}) copy-start(bf16[256,256]{1,0:T(8,128)(2,1)} %wo.1) | copy-start | bytes 393220
  205.5 26.8 %all-to-all-start.5 = ((bf16[64,8,512]{2,1,0:T(8,128)(2,1)}), bf16[64,8,512]{2,1,0:T(8,128)(2,1)S(1)}, u32[]{:S(2)}, u32[]{:S(2)}) async-start(bf16[64,8,512]{2,1,0:T(8,128)(2,1)} %bitcast.142), calls=%async_computation.5 | async-start | bytes 1048576 | tf_op jit(solution)/shard_map/all_to_all | solution.py:547
  237.9 1.5 copy-start
  244.1 25.8 %copy-start.1 = (f32[32,32,256]{2,1,0:T(8,128)}, f32[32,32,256]{2,1,0:T(8,128)S(1)}, u32[]{:S(2)}) copy-start(f32[32,32,256]{2,1,0:T(8,128)S(1)} %convolution_add_fusion.2) | copy-start | bytes 3145732
  244.2 41.1 %all-to-all-start.6 = ((bf16[128,56,128]{2,1,0:T(8,128)(2,1)}), bf16[128,56,128]{2,1,0:T(8,128)(2,1)S(1)}, u32[]{:S(2)}, u32[]{:S(2)}) async-start(bf16[128,56,128]{2,1,0:T(8,128)(2,1)} %bitcast.135), calls=%async_computation.6 | async-start | bytes 3670016 | tf_op jit(solution)/shard_map/all_to_all | solution.py:547
  254.9 18.5 %collective-permute-start.2 = (f32[32,256]{1,0:T(8,128)S(1)}, f32[32,256]{1,0:T(8,128)S(1)}, u32[]{:S(2)}, u32[]{:S(2)}) collective-permute-start(f32[32,256]{1,0:T(8,128)S(1)} %broadcast_select_fusion.1), channel_id=1, source_target_pairs={{0,126},{2,0},{4,2},{6,4},{8,6},{10,8},{12,10},{14,12},{16,14},{18... | collective-permute-start | bytes 98312 | tf_op jit(solution)/shard_map/ppermute | solution.py:539
  265.6 1.0 copy-start.2
  267.4 15.8 %collective-permute-start.3 = (f32[32,256]{1,0:T(8,128)S(1)}, f32[32,256]{1,0:T(8,128)S(1)}, u32[]{:S(2)}, u32[]{:S(2)}) collective-permute-start(f32[32,256]{1,0:T(8,128)S(1)} %broadcast_select_fusion), channel_id=1, source_target_pairs={{0,2},{2,4},{4,6},{6,8},{8,10},{10,12},{12,14},{14,16},{16,18},{18... | collective-permute-start | bytes 98312 | tf_op jit(solution)/shard_map/ppermute | solution.py:539
  269.9 13.3 %slice-start.1 = ((f32[32,32,256]{2,1,0:T(8,128)}), f32[31,32,256]{2,1,0:T(8,128)S(1)}, s32[]{:S(2)}) async-start(f32[32,32,256]{2,1,0:T(8,128)} %copy-done.2), calls=%async_computation.9 | async-start | bytes 2031616 | tf_op jit(solution)/shard_map/slice | solution.py:627
  269.9 13.3 %slice-start = ((f32[32,32,256]{2,1,0:T(8,128)}), f32[31,32,256]{2,1,0:T(8,128)S(1)}, s32[]{:S(2)}) async-start(f32[32,32,256]{2,1,0:T(8,128)} %copy-done.1), calls=%async_computation.8 | async-start | bytes 2031616 | tf_op jit(solution)/shard_map/slice | solution.py:626

commit v6 on v4

--- a/solution.py
+++ b/solution.py
@@ -555,11 +555,11 @@
         taps.append(piece)
     from_below = ring(turned(taps[0][0], turns[0]), -1)
     from_above = ring(turned(taps[2][-1], turns[1]), 1)
+    share, from_below, from_above = lax.optimization_barrier((share, from_below, from_above))
     field_grad = hidden_back.astype(f32) + taps[1]
     field_grad = field_grad + jnp.concatenate([taps[0][1:], from_below[None]], axis=0)
     field_grad = field_grad + jnp.concatenate([from_above[None], taps[2][:-1]], axis=0)
     grid_grad = field_grad.astype(bf16)[None]
-    share, grid_grad = lax.optimization_barrier((share, grid_grad))
     spread = jnp.broadcast_to(share[None], (ndev,) + share.shape)
     updates = normalize(exchange(spread, ("tile", "win")).reshape(-1, LANES))
 

time: 314 us -> 310 us (0.987)
  blocking collectives: 68.8 us -> 36.9 us
  waiting for transfers between devices: 50.2 us -> 72.5 us
  starting transfers between devices: 58.1 us -> 62.5 us
    all_to_all x5 -> x6, waiting for transfers between devices: 39.5 us -> 72 us  [exchange(): return lax.all_to_all(value, axes, split_axis=0, concat_axis=0, tiled=True)]
    all_to_all x3 -> x2, blocking collectives: 68.8 us -> 36.9 us  [exchange(): return lax.all_to_all(value, axes, split_axis=0, concat_axis=0, tiled=True)]
    ppermute x4, waiting for transfers between devices: 10.7 us -> 0.44 us  [ring(): lax.ppermute(value, 'tile', [(i, (i + by) % length) for i in range(length)])]
    all_to_all x5 -> x6, starting transfers between devices: 41 us -> 45.3 us  [exchange(): return lax.all_to_all(value, axes, split_axis=0, concat_axis=0, tiled=True)]
  transfers between devices with their start and end apart: 9 -> 10, of which waited for: 4 -> 5; matrix products, arithmetic and copies ran while one was open for 11% -> 12% of each run, Pallas kernels for 21% -> 21%
where the time goes in v6:
time: 310 us; the launch traced here: 309 us
  Pallas kernels  86 us (28%)
  waiting for transfers between devices  72.5 us (23%)
  starting transfers between devices  62.5 us (20%)
  blocking collectives  36.9 us (12%)
  local copies, waits for them, and re-layouts  29.5 us (10%)
  matrix products  12.3 us (4%)
  other arithmetic  6.94 us (2%)
    all_to_all x6, waiting for transfers between devices, exchange(): return lax.all_to_all(value, axes, split_axis=0, concat_axis=0, tiled=True)  72 us
    pallas_call x2, Pallas kernels, attend(): pl.pallas_call(functools.partial(attend_kernel, base), out_shape=(token_s...  57.3 us
    all_to_all x6, starting transfers between devices, exchange(): return lax.all_to_all(value, axes, split_axis=0, concat_axis=0, tiled=True)  45.3 us
    all_to_all x2, blocking collectives, exchange(): return lax.all_to_all(value, axes, split_axis=0, concat_axis=0, tiled=True)  36.9 us
    ppermute x4, starting transfers between devices, ring(): lax.ppermute(value, 'tile', [(i, (i + by) % length) for i in range(length)])  17.2 us
    dot_general x9, matrix products, mm_nt(): lax.dot_general(a, b, (((1,), (1,)), ((), ())), preferred_element_type=f32)  12.3 us
    transpose x2, local copies, waits for them, and re-layouts, local(): returned.append(exchange(back.transpose(1, 0, 2)).reshape(ntile * half, -1))  8.21 us
    pallas_call x2, Pallas kernels, gather(): pl.pallas_call(gather_kernel, out_shape=jax.ShapeDtypeStruct((names, widt...  7.85 us
  transfers between devices with their start and end apart: 10, of which 5 were waited for; matrix products, arithmetic and copies ran while one was open for 12% of the time, Pallas kernels for 21%

profile of v6, /device:TPU:1, one launch (start us, length us, event | category | flops | bytes accessed | tf_op | source)
XLA Modules:
  0.0 308.8 jit_solution(11171406827979479842)
XLA Ops:
  0.6 0.7 slice_bitcast_fusion.3
  1.4 2.1 collective-permute-start
  3.5 7.1 %collective-permute-start.1 = (bf16[32,256]{1,0:T(8,128)(2,1)S(1)}, bf16[32,256]{1,0:T(8,128)(2,1)S(1)}, u32[]{:S(2)}, u32[]{:S(2)}) collective-permute-start(bf16[32,256]{1,0:T(8,128)(2,1)S(1)} %get-tuple-element.49), channel_id=1, source_target_pairs={{0,126},{2,0},{4,2},{6,4},{8,6},{10,8},{12,10},{14,12},{16,14},{18... | collective-permute-start | bytes 49160 | tf_op jit(solution)/shard_map/ppermute | solution.py:475
  10.6 0.7 convert_bitcast_fusion.1
  11.3 0.7 fusion.28
  12.0 1.3 fusion.38
  14.8 0.1 rev.13
  14.9 1.9 pad_maximum_fusion.1
  16.8 4.6 %conv_slices.1 = (bf16[8,64,512]{2,1,0:T(8,128)(2,1)}, bf16[3,1088,256]{2,1,0:T(8,128)(2,1)}) custom-call(bf16[1088,256]{1,0:T(8,128)(2,1)} %bitcast.136, bf16[9,256,256]{2,1,0:T(8,128)(2,1)} %bitcast.132), custom_call_target="tpu_custom_call" | custom-call | flops 1207959552 | bytes 6000000 | tf_op jit(solution)/shard_map/conv_slices/pallas_call | solution.py:71
  21.4 1.1 pad_maximum_fusion
  22.5 0.4 copy.54
  22.9 17.9 %all_to_all.40 = bf16[64,8,640]{2,1,0:T(8,128)(2,1)S(1)} all-to-all(bf16[64,8,640]{2,1,0:T(8,128)(2,1)S(1)} %copy.54), channel_id=1, replica_groups=mesh['tile'=64,'win'=2] {'tile'}, dimensions={0} | all-to-all | bytes 1310720 | tf_op jit(solution)/shard_map/all_to_all | solution.py:483
  40.8 0.1 copy.65
  41.0 0.6 fusion.37
  41.6 3.7 %pick.2 = bf16[64,32,512]{2,1,0:T(8,128)(2,1)} custom-call(bf16[512,640]{1,0:T(8,128)(2,1)} %bitcast.133, s32[32,64]{1,0:T(8,128)} %get-tuple-element.53.ids_ref), custom_call_target="tpu_custom_call" | custom-call | flops 1342177280 | bytes 4000000 | tf_op jit(solution)/shard_map/pick/pallas_call | solution.py:105
  45.4 6.1 %all-to-all-start.1 = ((bf16[64,32,512]{2,1,0:T(8,128)(2,1)}), bf16[64,32,512]{2,1,0:T(8,128)(2,1)S(1)}, u32[]{:S(2)}, u32[]{:S(2)}) async-start(bf16[64,32,512]{2,1,0:T(8,128)(2,1)} %pick.2), calls=%async_computation.1 | async-start | bytes 4194304 | tf_op jit(solution)/shard_map/all_to_all | solution.py:483
  51.4 0.1 copy.51
  51.6 0.1 copy.52
  51.7 0.8 copy.50
  52.4 0.8 copy.53
  53.2 0.7 fusion.36
  53.9 0.8 copy.59.wkv
  54.8 3.7 %pick.3 = bf16[64,32,512]{2,1,0:T(8,128)(2,1)} custom-call(bf16[512,640]{1,0:T(8,128)(2,1)} %bitcast.134, s32[32,64]{1,0:T(8,128)} %get-tuple-element.54.ids_ref), custom_call_target="tpu_custom_call" | custom-call | flops 1342177280 | bytes 4000000 | tf_op jit(solution)/shard_map/pick/pallas_call | solution.py:105
  58.5 19.4 %all-to-all-done.1 = bf16[64,32,512]{2,1,0:T(8,128)(2,1)S(1)} async-done(((bf16[64,32,512]{2,1,0:T(8,128)(2,1)}), bf16[64,32,512]{2,1,0:T(8,128)(2,1)S(1)}, u32[]{:S(2)}, u32[]{:S(2)}) %all-to-all-start.1) | async-done | bytes 2097184 | tf_op jit(solution)/shard_map/all_to_all | solution.py:483
  77.9 8.4 %all-to-all-start.2 = ((bf16[64,32,512]{2,1,0:T(8,128)(2,1)}), bf16[64,32,512]{2,1,0:T(8,128)(2,1)}, u32[]{:S(2)}, u32[]{:S(2)}) async-start(bf16[64,32,512]{2,1,0:T(8,128)(2,1)} %pick.3), calls=%async_computation.2 | async-start | bytes 4194304 | tf_op jit(solution)/shard_map/all_to_all | solution.py:483
  86.4 2.5 copy.70
  88.9 1.1 broadcast_in_dim.32.grads_in
  89.9 28.7 %attend.2 = (bf16[64,128,256]{2,1,0:T(8,128)(2,1)}, bf16[64,128,256]{2,1,0:T(8,128)(2,1)}, bf16[32,64,512]{2,1,0:T(8,128)(2,1)}, f32[1024,256]{1,0:T(8,128)}) custom-call(s32[1,64]{1,0:T(1,128)} %live.3, bf16[256,256]{1,0:T(8,128)(2,1)} %wq.3, bf16[256,256]{1,0:T(8,128)(2,1)} %bitcast.140, bf16[256,512]{1,0:T(8,128)(2,1)} %copy.59.wkv, ...), custom_call_target="tpu_custom_call" | custom-call | flops 25600000000 | bytes 25600000 | tf_op jit(solution)/shard_map/attend/pallas_call | solution.py:354
  118.6 4.1 %copy.63 = bf16[64,32,512]{2,1,0:T(8,128)(2,1)} copy(bf16[64,32,512]{2,0,1:T(8,128)(2,1)} %bitcast.130) | data formatting | bytes 4194304 | tf_op jit(solution)/shard_map/transpose | solution.py:536
  122.8 9.5 %all-to-all-start.4 = ((bf16[64,32,512]{2,1,0:T(8,128)(2,1)}), bf16[64,32,512]{2,1,0:T(8,128)(2,1)S(1)}, u32[]{:S(2)}, u32[]{:S(2)}) async-start(bf16[64,32,512]{2,1,0:T(8,128)(2,1)} %copy.63), calls=%async_computation.4 | async-start | bytes 4194304 | tf_op jit(solution)/shard_map/all_to_all | solution.py:483
  132.3 4.1 %copy.69 = bf16[64,32,512]{2,0,1:T(8,128)(2,1)} copy(bf16[64,32,512]{2,1,0:T(8,128)(2,1)} %all-to-all-done.2) | data formatting | bytes 4194304 | tf_op jit(solution)/shard_map/all_to_all | solution.py:483
  136.4 28.6 %attend.3 = (bf16[64,128,256]{2,1,0:T(8,128)(2,1)}, bf16[64,128,256]{2,1,0:T(8,128)(2,1)}, bf16[32,64,512]{2,1,0:T(8,128)(2,1)}, f32[1024,256]{1,0:T(8,128)}) custom-call(s32[1,64]{1,0:T(1,128)} %live.3, bf16[256,256]{1,0:T(8,128)(2,1)} %wq.3, bf16[256,256]{1,0:T(8,128)(2,1)} %bitcast.141, ...), custom_call_target="tpu_custom_call", output_to_operand_aliasing={{0}: (11, {}), {1}: (12, {})} | custom-call | flops 25600000000 | bytes 25600000 | tf_op jit(solution)/shard_map/attend/pallas_call | solution.py:354
  165.0 4.1 %copy.61 = bf16[64,32,512]{2,1,0:T(8,128)(2,1)} copy(bf16[64,32,512]{2,0,1:T(8,128)(2,1)} %bitcast.128) | data formatting | bytes 4194304 | tf_op jit(solution)/shard_map/transpose | solution.py:536
  169.1 1.3 copy-done.4
  170.4 10.3 %all-to-all-start.3 = ((bf16[64,32,512]{2,1,0:T(8,128)(2,1)}), bf16[64,32,512]{2,1,0:T(8,128)(2,1)}, u32[]{:S(2)}, u32[]{:S(2)}) async-start(bf16[64,32,512]{2,1,0:T(8,128)(2,1)} %copy.61), calls=%async_computation.3 | async-start | bytes 4194304 | tf_op jit(solution)/shard_map/all_to_all | solution.py:483
  180.8 0.7 reshape.147.ids_ref
  181.6 0.7 reshape.145.ids_ref
  182.2 3.9 %gather.2.rest_0_ = f32[512,512]{1,0:T(8,128)} custom-call(s32[1,2048]{1,0:T(1,128)} %reshape.147.ids_ref, bf16[2048,512]{1,0:T(8,128)(2,1)} %bitcast.126), custom_call_target="tpu_custom_call" | custom-call | flops 1073741824 | bytes 4000000 | tf_op jit(solution)/shard_map/gather/pallas_call | solution.py:134
  186.2 20.1 %all-to-all-done.3 = bf16[64,32,512]{2,1,0:T(8,128)(2,1)} async-done(((bf16[64,32,512]{2,1,0:T(8,128)(2,1)}), bf16[64,32,512]{2,1,0:T(8,128)(2,1)}, u32[]{:S(2)}, u32[]{:S(2)}) %all-to-all-start.3) | async-done | bytes 2097184 | tf_op jit(solution)/shard_map/all_to_all | solution.py:483
  206.2 3.9 %gather.3 = bf16[512,512]{1,0:T(8,128)(2,1)} custom-call(s32[1,2048]{1,0:T(1,128)} %reshape.145.ids_ref, bf16[2048,512]{1,0:T(8,128)(2,1)} %bitcast.28.slots_ref, f32[512,512]{1,0:T(8,128)} %gather.2.rest_0_), custom_call_target="tpu_custom_call" | custom-call | flops 1073741824 | bytes 4000000 | tf_op jit(solution)/shard_map/gather/pallas_call | solution.py:134
  210.2 19.0 %all_to_all.41 = bf16[64,8,512]{2,1,0:T(8,128)(2,1)S(1)} all-to-all(bf16[64,8,512]{2,1,0:T(8,128)(2,1)} %bitcast.139), channel_id=1, replica_groups=mesh['tile'=64,'win'=2] {'tile'}, dimensions={0} | all-to-all | bytes 1048576 | tf_op jit(solution)/shard_map/all_to_all | solution.py:483
  229.2 0.9 copy.71
  230.1 4.7 %finish.1 = (bf16[1024,256]{1,0:T(8,128)(2,1)}, bf16[7168,128]{1,0:T(8,128)(2,1)}) custom-call(bf16[8,64,512]{2,1,0:T(8,128)(2,1)} %bitcast.137, bf16[3,1088,256]{2,1,0:T(8,128)(2,1)} %get-tuple-element.36.shifts_ref, f32[1024,256]{1,0:T(8,128)} %get-tuple-element.37.grads_ref), custom_call_target="tpu_custom_call" | custom-call | flops 1207959552 | bytes 6000000 | tf_op jit(solution)/shard_map/finish/pallas_call | solution.py:420
  234.8 6.8 %all-to-all-start.6 = ((bf16[128,56,128]{2,1,0:T(8,128)(2,1)}), bf16[128,56,128]{2,1,0:T(8,128)(2,1)S(1)}, u32[]{:S(2)}, u32[]{:S(2)}) async-start(bf16[128,56,128]{2,1,0:T(8,128)(2,1)} %bitcast.131), calls=%async_computation.6 | async-start | bytes 3670016 | tf_op jit(solution)/shard_map/all_to_all | solution.py:483
  241.6 1.3 fusion.6
  242.8 1.2 convolution_add_fusion.3
  244.1 1.3 convolution_add_fusion.2
  245.5 7.9 %collective-permute-start.2 = (f32[32,256]{1,0:T(8,128)S(1)}, f32[32,256]{1,0:T(8,128)S(1)}, u32[]{:S(2)}, u32[]{:S(2)}) collective-permute-start(f32[32,256]{1,0:T(8,128)S(1)} %broadcast_select_fusion.1), channel_id=1, source_target_pairs={{0,126},{2,0},{4,2},{6,4},{8,6},{10,8},{12,10},{14,12},{16,14},{18... | collective-permute-start | bytes 98312 | tf_op jit(solution)/shard_map/ppermute | solution.py:475
  253.4 1.2 fusion.5
  254.6 1.2 convolution_add_fusion.1
  255.9 1.3 convolution_add_fusion
  257.2 1.0 copy-done.3
  258.2 1.4 broadcast_select_fusion
  259.6 9.7 %all-to-all-done.6 = bf16[128,56,128]{2,1,0:T(8,128)(2,1)S(1)} async-done(((bf16[128,56,128]{2,1,0:T(8,128)(2,1)}), bf16[128,56,128]{2,1,0:T(8,128)(2,1)S(1)}, u32[]{:S(2)}, u32[]{:S(2)}) %all-to-all-start.6) | async-done | bytes 1835040 | tf_op jit(solution)/shard_map/all_to_all | solution.py:483
  269.2 0.3 reduce_sum.22
  269.6 0.4 collective-permute-done.3
  270.0 1.5 broadcast_in_dim.39
  271.5 4.2 %all-to-all-start.7 = ((bf16[128,56,128]{2,1,0:T(8,128)(2,1)}), bf16[128,56,128]{2,1,0:T(8,128)(2,1)S(1)}, u32[]{:S(2)}, u32[]{:S(2)}) async-start(bf16[128,56,128]{2,1,0:T(8,128)(2,1)} %broadcast_in_dim.39), calls=%async_computation.7 | async-start | bytes 3670016 | tf_op jit(solution)/shard_map/all_to_all | solution.py:483
  275.7 1.4 fusion.7
  277.1 1.2 convolution_add_fusion.5
  278.4 2.1 fusion.4
  280.5 22.8 %all-to-all-done.7 = bf16[128,56,128]{2,1,0:T(8,128)(2,1)S(1)} async-done(((bf16[128,56,128]{2,1,0:T(8,128)(2,1)}), bf16[128,56,128]{2,1,0:T(8,128)(2,1)S(1)}, u32[]{:S(2)}, u32[]{:S(2)}) %all-to-all-start.7) | async-done | bytes 1835040 | tf_op jit(solution)/shard_map/all_to_all | solution.py:483
  303.4 1.3 copy-done.1
  304.6 4.2 %normalize.1 = (f32[256,256]{1,0:T(8,128)}, f32[256,256]{1,0:T(8,128)}, f32[256,256]{1,0:T(8,128)}, f32[256,256]{1,0:T(8,128)}, f32[9,256,256]{2,1,0:T(8,128)}) custom-call(bf16[7168,128]{1,0:T(8,128)(2,1)} %bitcast.125), custom_call_target="tpu_custom_call" | custom-call | flops 4000000 | bytes 6000000 | tf_op jit(solution)/shard_map/normalize/pallas_call | solution.py:462
  (43 shorter events, 0.6 us)
Async XLA Ops:
  1.4 13.3 %collective-permute-start = (bf16[32,256]{1,0:T(8,128)(2,1)S(1)}, bf16[32,256]{1,0:T(8,128)(2,1)S(1)}, u32[]{:S(2)}, u32[]{:S(2)}) collective-permute-start(bf16[32,256]{1,0:T(8,128)(2,1)S(1)} %get-tuple-element.48), channel_id=1, source_target_pairs={{0,2},{2,4},{4,6},{6,8},{8,10},{10,12},{12,14},{14,16},{16,18},{18... | collective-permute-start | bytes 49160 | tf_op jit(solution)/shard_map/ppermute | solution.py:475
  3.5 11.3 %collective-permute-start.1 = (bf16[32,256]{1,0:T(8,128)(2,1)S(1)}, bf16[32,256]{1,0:T(8,128)(2,1)S(1)}, u32[]{:S(2)}, u32[]{:S(2)}) collective-permute-start(bf16[32,256]{1,0:T(8,128)(2,1)S(1)} %get-tuple-element.49), channel_id=1, source_target_pairs={{0,126},{2,0},{4,2},{6,4},{8,6},{10,8},{12,10},{14,12},{16,14},{18... | collective-permute-start | bytes 49160 | tf_op jit(solution)/shard_map/ppermute | solution.py:475
  40.8 0.8 copy-start.5
  45.4 6.1 %copy-start.6 = (bf16[256,256]{1,0:T(8,128)(2,1)S(1)}, bf16[256,256]{1,0:T(8,128)(2,1)}, u32[]{:S(2)}) copy-start(bf16[256,256]{1,0:T(8,128)(2,1)} %param.19) | copy-start | bytes 393220
  45.4 6.2 %copy-start.7 = (bf16[256,256]{1,0:T(8,128)(2,1)S(1)}, bf16[256,256]{1,0:T(8,128)(2,1)}, u32[]{:S(2)}) copy-start(bf16[256,256]{1,0:T(8,128)(2,1)} %param.20) | copy-start | bytes 393220
  45.4 6.3 %copy-start.8 = (bf16[256,256]{1,0:T(8,128)(2,1)S(1)}, bf16[256,256]{1,0:T(8,128)(2,1)}, u32[]{:S(2)}) copy-start(bf16[256,256]{1,0:T(8,128)(2,1)} %wq.3) | copy-start | bytes 393220
  45.4 7.1 %copy-start.9 = (bf16[256,256]{1,0:T(8,128)(2,1)S(1)}, bf16[256,256]{1,0:T(8,128)(2,1)}, u32[]{:S(2)}) copy-start(bf16[256,256]{1,0:T(8,128)(2,1)} %wo.3) | copy-start | bytes 393220
  45.4 32.6 %all-to-all-start.1 = ((bf16[64,32,512]{2,1,0:T(8,128)(2,1)}), bf16[64,32,512]{2,1,0:T(8,128)(2,1)S(1)}, u32[]{:S(2)}, u32[]{:S(2)}) async-start(bf16[64,32,512]{2,1,0:T(8,128)(2,1)} %pick.2), calls=%async_computation.1 | async-start | bytes 4194304 | tf_op jit(solution)/shard_map/all_to_all | solution.py:483
  77.9 44.8 %all-to-all-start.2 = ((bf16[64,32,512]{2,1,0:T(8,128)(2,1)}), bf16[64,32,512]{2,1,0:T(8,128)(2,1)}, u32[]{:S(2)}, u32[]{:S(2)}) async-start(bf16[64,32,512]{2,1,0:T(8,128)(2,1)} %pick.3), calls=%async_computation.2 | async-start | bytes 4194304 | tf_op jit(solution)/shard_map/all_to_all | solution.py:483
  122.8 46.3 %all-to-all-start.4 = ((bf16[64,32,512]{2,1,0:T(8,128)(2,1)}), bf16[64,32,512]{2,1,0:T(8,128)(2,1)S(1)}, u32[]{:S(2)}, u32[]{:S(2)}) async-start(bf16[64,32,512]{2,1,0:T(8,128)(2,1)} %copy.63), calls=%async_computation.4 | async-start | bytes 4194304 | tf_op jit(solution)/shard_map/all_to_all | solution.py:483
  169.1 1.3 copy-start.4
  170.4 35.8 %all-to-all-start.3 = ((bf16[64,32,512]{2,1,0:T(8,128)(2,1)}), bf16[64,32,512]{2,1,0:T(8,128)(2,1)}, u32[]{:S(2)}, u32[]{:S(2)}) async-start(bf16[64,32,512]{2,1,0:T(8,128)(2,1)} %copy.61), calls=%async_computation.3 | async-start | bytes 4194304 | tf_op jit(solution)/shard_map/all_to_all | solution.py:483
  234.8 6.8 %copy-start = (bf16[1024,256]{1,0:T(8,128)(2,1)S(1)}, bf16[1024,256]{1,0:T(8,128)(2,1)}, u32[]{:S(2)}) copy-start(bf16[1024,256]{1,0:T(8,128)(2,1)} %get-tuple-element.38) | copy-start | bytes 1572868
  234.8 34.5 %all-to-all-start.6 = ((bf16[128,56,128]{2,1,0:T(8,128)(2,1)}), bf16[128,56,128]{2,1,0:T(8,128)(2,1)S(1)}, u32[]{:S(2)}, u32[]{:S(2)}) async-start(bf16[128,56,128]{2,1,0:T(8,128)(2,1)} %bitcast.131), calls=%async_computation.6 | async-start | bytes 3670016 | tf_op jit(solution)/shard_map/all_to_all | solution.py:483
  245.3 30.4 %copy-start.2 = (f32[32,32,256]{2,1,0:T(8,128)}, f32[32,32,256]{2,1,0:T(8,128)S(1)}, u32[]{:S(2)}) copy-start(f32[32,32,256]{2,1,0:T(8,128)S(1)} %convolution_add_fusion.2) | copy-start | bytes 3145732
  245.5 24.1 %collective-permute-start.2 = (f32[32,256]{1,0:T(8,128)S(1)}, f32[32,256]{1,0:T(8,128)S(1)}, u32[]{:S(2)}, u32[]{:S(2)}) collective-permute-start(f32[32,256]{1,0:T(8,128)S(1)} %broadcast_select_fusion.1), channel_id=1, source_target_pairs={{0,126},{2,0},{4,2},{6,4},{8,6},{10,8},{12,10},{14,12},{16,14},{18... | collective-permute-start | bytes 98312 | tf_op jit(solution)/shard_map/ppermute | solution.py:475
  257.1 1.0 copy-start.3
  259.6 10.4 %collective-permute-start.3 = (f32[32,256]{1,0:T(8,128)}, f32[32,256]{1,0:T(8,128)S(1)}, u32[]{:S(2)}, u32[]{:S(2)}) collective-permute-start(f32[32,256]{1,0:T(8,128)} %broadcast_select_fusion), channel_id=1, source_target_pairs={{0,2},{2,4},{4,6},{6,8},{8,10},{10,12},{12,14},{14,16},{16,18},{18... | collective-permute-start | bytes 98312 | tf_op jit(solution)/shard_map/ppermute | solution.py:475
  271.5 31.9 %all-to-all-start.7 = ((bf16[128,56,128]{2,1,0:T(8,128)(2,1)}), bf16[128,56,128]{2,1,0:T(8,128)(2,1)S(1)}, u32[]{:S(2)}, u32[]{:S(2)}) async-start(bf16[128,56,128]{2,1,0:T(8,128)(2,1)} %broadcast_in_dim.39), calls=%async_computation.7 | async-start | bytes 3670016 | tf_op jit(solution)/shard_map/all_to_all | solution.py:483
  275.7 2.7 slice-start
  275.7 2.7 slice-start.1
  303.4 1.3 copy-start.1
